TPU v7x, 32 devices: a whole 2x2x4 slice. The times are simulated.
32 devices in a mesh: dp: 8 (over z, y), tensor: 4 (over x, core).
Axes of the slice: x: 2, y: 2, z: 4, core: 2. Of those that a mesh axis runs over, the one named last changes fastest.
Arguments:
- inputs: bfloat16 [25600, 768], P(('dp', 'tensor')), may hold values from -6 to 6
- res_ids: int32 [32], P(('dp', 'tensor')), may hold values from 0 to 1
- memory: bfloat16 [2, 6400, 768], P(None, ('dp', 'tensor')), may hold values from -6 to 6
- gain_one: float32 [768], replicated, may hold values from 0.5 to 1.5
- bias_one: float32 [768], replicated, may hold values from -1.8 to 1.8
- w_qkv: bfloat16 [768, 2304], replicated, may hold values from -0.21875 to 0.21875
- b_qkv: float32 [2304], replicated, may hold values from -1.8 to 1.8
- pool_weight: float32 [3, 27, 96], replicated, may hold values from -1.25 to 1.25
- pool_gain: float32 [3, 96], replicated, may hold values from 0.5 to 1.5
- pool_bias: float32 [3, 96], replicated, may hold values from -1.8 to 1.8
- rel_table: float32 [53, 96], replicated, may hold values from -0.6 to 0.6
- w_proj: bfloat16 [768, 768], replicated, may hold values from -0.21875 to 0.21875
- b_proj: float32 [768], replicated, may hold values from -1.8 to 1.8
- gain_two: float32 [768], replicated, may hold values from 0.5 to 1.5
- bias_two: float32 [768], replicated, may hold values from -1.8 to 1.8
- w_up: bfloat16 [768, 3072], P(None, 'tensor'), may hold values from -0.21875 to 0.21875
- b_up: bfloat16 [3072], P('tensor'), may hold values from -1.796875 to 1.796875
- w_down: bfloat16 [3072, 768], P('tensor'), may hold values from -0.109375 to 0.109375
- b_down: float32 [768], replicated, may hold values from -1.8 to 1.8
- cotangent: bfloat16 [25600, 768], P(('dp', 'tensor')), may hold values from -6 to 6
Outputs:
- output: bfloat16 [25600, 768], P(('dp', 'tensor'))
- input_grad: float32 [25600, 768], P(('dp', 'tensor'))
- grad_gain_one: float32 [768], replicated
- grad_bias_one: float32 [768], replicated
- grad_w_qkv: float32 [768, 2304], replicated
- grad_b_qkv: float32 [2304], replicated
- grad_pool_weight: float32 [3, 27, 96], replicated
- grad_pool_gain: float32 [3, 96], replicated
- grad_pool_bias: float32 [3, 96], replicated
- grad_rel_table: float32 [53, 96], replicated
- grad_w_proj: float32 [768, 768], replicated
- grad_b_proj: float32 [768], replicated
- grad_gain_two: float32 [768], replicated
- grad_bias_two: float32 [768], replicated
- grad_w_up: float32 [768, 3072], P(None, 'tensor')
- grad_b_up: float32 [3072], P('tensor')
- grad_w_down: float32 [3072, 768], P('tensor')
- grad_b_down: float32 [768], replicated
Inputs may be any that keep to these rules, and one draw needn't show every extreme that they name: `res_ids`: 0 marks a clip whose frames hold 7 x 7 tokens in the corner of the 10 x 10 grid, 1 a clip that fills it.
All inputs are finite; a program needn't handle non-finite values.
Results may differ from a plain program's by a relative error of at most 0.012.
Values may be sent and summed in bfloat16 or wider, within the bound.
A program may use at most 384 MiB of HBM per device.

v0:
```python
import jax
import jax.numpy as jnp
from jax import lax
from jax.sharding import PartitionSpec as P

D = 768
HEADS = 8
HEAD_DIM = 96
FRAMES = 8
SIDE = 10
SMALL_SIDE = 7
LENGTH = 800
MEM = 200
OFFSETS = 28
REL_ROWS = 53


HIGHEST = lax.Precision.HIGHEST
NORM_EPS = 1e-06
INV_ROOT_TWO = 0.7071067811865476


def layer_norm(values, gain_vec, shift_vec):
    average = jnp.mean(values, axis=-1, keepdims=True)
    centered = values - average
    variance = jnp.mean(centered * centered, axis=-1, keepdims=True)
    return centered * lax.rsqrt(variance + NORM_EPS) * gain_vec + shift_vec


def gelu_exact(values):
    return 0.5 * values * (1.0 + lax.erf(values * INV_ROOT_TWO))


def grid_tables(res_ids):
    position = jnp.arange(LENGTH, dtype=jnp.int32)
    frame_of = position // (SIDE * SIDE)
    row_of = position // SIDE % SIDE
    column_of = position % SIDE
    large_clip = res_ids[:, None] == 1
    inside = (row_of < SMALL_SIDE) & (column_of < SMALL_SIDE)
    token_valid = large_clip | inside[None, :]
    memory_side = (SIDE + 1) // 2
    memory_small = (SMALL_SIDE + 1) // 2
    memory_index = jnp.arange(MEM, dtype=jnp.int32) % (MEM // 2)
    memory_row = memory_index // memory_side % memory_side
    memory_column = memory_index % memory_side
    memory_inside = (memory_row < memory_small) & (memory_column < memory_small)
    memory_valid = large_clip | memory_inside[None, :]
    frame_range = jnp.arange(FRAMES, dtype=jnp.int32)
    side_range = jnp.arange(SIDE, dtype=jnp.int32)
    row_base = 2 * FRAMES - 1
    column_base = row_base + 2 * SIDE - 1
    target = jnp.concatenate(
        [
            frame_of[:, None] - frame_range[None, :] + FRAMES - 1,
            row_base + row_of[:, None] - side_range[None, :] + SIDE - 1,
            column_base + column_of[:, None] - side_range[None, :] + SIDE - 1,
        ],
        axis=1,
    )
    select_table = (
        target[:, :, None] == jnp.arange(REL_ROWS, dtype=jnp.int32)[None, None, :]
    ).astype(jnp.float32)
    key_onehot = jnp.concatenate(
        [
            frame_of[:, None] == frame_range[None, :],
            row_of[:, None] == side_range[None, :],
            column_of[:, None] == side_range[None, :],
        ],
        axis=1,
    ).astype(jnp.float32)
    return (token_valid, memory_valid, select_table, key_onehot)


def pool_field(field, kernel):
    kernel_wide = jnp.tile(kernel, (1, HEADS))
    padded = jnp.pad(field, ((0, 0), (1, 1), (1, 1), (1, 1), (0, 0)))
    accumulated = jnp.zeros_like(field)
    for kernel_tap in range(27):
        frame_shift = kernel_tap // 9
        row_shift = kernel_tap // 3 % 3
        column_shift = kernel_tap % 3
        window = padded[
            :,
            frame_shift : frame_shift + FRAMES,
            row_shift : row_shift + SIDE,
            column_shift : column_shift + SIDE,
            :,
        ]
        accumulated = accumulated + window * kernel_wide[kernel_tap]
    return accumulated


def pool_norm(stacked, pool_weight, pool_gain, pool_bias):
    clip_count = stacked.shape[1]
    results = []
    for branch_index in range(3):
        pooled = pool_field(stacked[branch_index], pool_weight[branch_index])
        per_head = pooled.reshape(clip_count, LENGTH, HEADS, HEAD_DIM)
        results.append(layer_norm(per_head, pool_gain[branch_index], pool_bias[branch_index]))
    return jnp.stack(results)


def build_offsets(queries, rel_table, select_table):
    rel_scores = jnp.einsum("...lhe,re->...lhr", queries, rel_table, precision=HIGHEST)
    return jnp.einsum("...lhr,lpr->...lhp", rel_scores, select_table, precision=HIGHEST)


def extend_last(array_in, width_to):
    extra_cols = width_to - array_in.shape[-1]
    widths = [(0, 0)] * (array_in.ndim - 1) + [(0, extra_cols)]
    return jnp.pad(array_in, widths)


def per_device(
    inputs,
    res_ids,
    memory,
    gain_one,
    bias_one,
    w_qkv,
    b_qkv,
    pool_weight,
    pool_gain,
    pool_bias,
    rel_table,
    w_proj,
    b_proj,
    gain_two,
    bias_two,
    w_up,
    b_up,
    w_down,
    b_down,
    cotangent,
):
    clip_count = res_ids.shape[0]
    row_total = inputs.shape[0]
    scale_factor = HEAD_DIM ** (-0.5)
    ext_width = (HEAD_DIM + OFFSETS + 127) // 128 * 128
    token_valid, memory_valid, select_table, key_onehot = grid_tables(res_ids)
    token_weight = token_valid.reshape(-1).astype(jnp.float32)[:, None]
    wide_inputs = inputs.astype(jnp.float32)
    normed_one, norm_one_back = jax.vjp(layer_norm, wide_inputs, gain_one, bias_one)
    normed_low = normed_one.astype(jnp.bfloat16)
    qkv = jnp.dot(normed_low, w_qkv, preferred_element_type=jnp.float32) + b_qkv
    masked = qkv * token_weight
    stacked = jnp.moveaxis(masked.reshape(clip_count, FRAMES, SIDE, SIDE, 3, D), 4, 0)
    pooled, pool_back = jax.vjp(pool_norm, stacked, pool_weight, pool_gain, pool_bias)
    queries = pooled[0]
    offsets, offset_back = jax.vjp(
        lambda query_in, table_in: build_offsets(query_in, table_in, select_table),
        queries,
        rel_table,
    )
    query_ext = extend_last(
        jnp.concatenate([queries * scale_factor, offsets], axis=-1), ext_width
    ).astype(jnp.bfloat16)
    onehot_heads = jnp.broadcast_to(
        key_onehot[None, :, None, :], (clip_count, LENGTH, HEADS, OFFSETS)
    )
    keys_current = extend_last(
        jnp.concatenate(
            [pooled[1].astype(jnp.bfloat16), onehot_heads.astype(jnp.bfloat16)], axis=-1
        ),
        ext_width,
    )
    memory_heads = memory.reshape(2, clip_count, MEM, HEADS, HEAD_DIM)
    keys_memory = extend_last(memory_heads[0], ext_width)
    keys_ext = jnp.concatenate([keys_current, keys_memory], axis=1)
    values_all = jnp.concatenate([pooled[2].astype(jnp.bfloat16), memory_heads[1]], axis=1)
    valid_all = jnp.concatenate([token_valid, memory_valid], axis=1)[:, None, None, :]

    def masked_scores():
        raw_scores = jnp.einsum(
            "cqhx,ckhx->chqk", query_ext, keys_ext, preferred_element_type=jnp.float32
        )
        return jnp.where(valid_all, raw_scores, -1e30)

    scores = masked_scores()
    row_top = jnp.max(scores, axis=-1, keepdims=True)
    exponents = jnp.exp(scores - row_top)
    row_sum = jnp.sum(exponents, axis=-1, keepdims=True)
    probabilities = exponents / row_sum
    log_total = row_top + jnp.log(row_sum)
    weighted = jnp.einsum(
        "chqk,ckhe->cqhe",
        probabilities.astype(jnp.bfloat16),
        values_all,
        preferred_element_type=jnp.float32,
    )
    attended = (weighted + queries).reshape(row_total, D)
    attended_low = attended.astype(jnp.bfloat16)
    middle = (
        wide_inputs + jnp.dot(attended_low, w_proj, preferred_element_type=jnp.float32) + b_proj
    )
    normed_two, norm_two_back = jax.vjp(layer_norm, middle, gain_two, bias_two)
    rows_low = normed_two.astype(jnp.bfloat16)
    grad_out = cotangent.astype(jnp.float32) * token_weight
    grad_b_down = jnp.sum(grad_out, axis=0)
    grad_out_low = grad_out.astype(jnp.bfloat16)
    gathered = lax.all_gather(rows_low, "tensor", axis=0, tiled=True)
    hidden = jnp.dot(gathered, w_up, preferred_element_type=jnp.float32) + b_up.astype(jnp.float32)
    activated, gelu_back = jax.vjp(gelu_exact, hidden)
    act_low = activated.astype(jnp.bfloat16)
    row_piece = act_low
    mlp_sum = lax.psum_scatter(
        jnp.dot(row_piece, w_down, preferred_element_type=jnp.float32).astype(jnp.bfloat16),
        "tensor",
        scatter_dimension=0,
        tiled=True,
    ).astype(jnp.float32)
    grad_rows = lax.all_gather(grad_out_low, "tensor", axis=0, tiled=True)
    grad_w_down = jnp.einsum("rf,rd->fd", act_low, grad_rows, preferred_element_type=jnp.float32)
    grad_act = jnp.einsum("rd,fd->rf", grad_rows, w_down, preferred_element_type=jnp.float32)
    grad_hidden = gelu_back(grad_act)[0]
    grad_b_up = jnp.sum(grad_hidden, axis=0)
    hidden_low = grad_hidden.astype(jnp.bfloat16)
    grad_w_up = jnp.einsum("rd,rf->df", gathered, hidden_low, preferred_element_type=jnp.float32)
    row_piece = hidden_low
    grad_normed_two = lax.psum_scatter(
        jnp.einsum("rf,df->rd", row_piece, w_up, preferred_element_type=jnp.float32),
        "tensor",
        scatter_dimension=0,
        tiled=True,
    )
    output = ((middle + mlp_sum + b_down) * token_weight).astype(jnp.bfloat16)
    grad_from_two = norm_two_back(grad_normed_two)
    grad_middle = grad_out + grad_from_two[0]
    grad_b_proj = jnp.sum(grad_middle, axis=0)
    proj_low = grad_middle.astype(jnp.bfloat16)
    grad_w_proj = jnp.einsum(
        "rd,re->de", attended_low, proj_low, preferred_element_type=jnp.float32
    )
    grad_attended = jnp.einsum("re,de->rd", proj_low, w_proj, preferred_element_type=jnp.float32)
    grad_attended = grad_attended.reshape(clip_count, LENGTH, HEADS, HEAD_DIM)
    weighted_low = grad_attended.astype(jnp.bfloat16)
    probabilities = jnp.exp(masked_scores() - log_total)
    grad_probs = jnp.einsum(
        "cqhe,ckhe->chqk", weighted_low, values_all, preferred_element_type=jnp.float32
    )
    inner_sum = jnp.sum(probabilities * grad_probs, axis=-1, keepdims=True)
    grad_scores = (probabilities * (grad_probs - inner_sum)).astype(jnp.bfloat16)
    grad_query_ext = jnp.einsum(
        "chqk,ckhx->cqhx", grad_scores, keys_ext, preferred_element_type=jnp.float32
    )
    grad_key_ext = jnp.einsum(
        "chqk,cqhx->ckhx", grad_scores[..., :LENGTH], query_ext, preferred_element_type=jnp.float32
    )
    grad_values = jnp.einsum(
        "chqk,cqhe->ckhe",
        probabilities[..., :LENGTH].astype(jnp.bfloat16),
        weighted_low,
        preferred_element_type=jnp.float32,
    )
    offset_grads = offset_back(grad_query_ext[..., HEAD_DIM : HEAD_DIM + OFFSETS])
    grad_queries = grad_query_ext[..., :HEAD_DIM] * scale_factor + grad_attended + offset_grads[0]
    pool_grads = pool_back(jnp.stack([grad_queries, grad_key_ext[..., :HEAD_DIM], grad_values]))
    grad_qkv = jnp.moveaxis(pool_grads[0], 0, 4).reshape(row_total, 3 * D) * token_weight
    grad_b_qkv = jnp.sum(grad_qkv, axis=0)
    qkv_low = grad_qkv.astype(jnp.bfloat16)
    grad_w_qkv = jnp.einsum("rd,rq->dq", normed_low, qkv_low, preferred_element_type=jnp.float32)
    grad_normed_one = jnp.einsum("rq,dq->rd", qkv_low, w_qkv, preferred_element_type=jnp.float32)
    grad_from_one = norm_one_back(grad_normed_one)
    input_grad = grad_middle + grad_from_one[0]
    summed = lax.psum(
        (
            grad_from_one[1],
            grad_from_one[2],
            grad_w_qkv,
            grad_b_qkv,
            pool_grads[1],
            pool_grads[2],
            pool_grads[3],
            offset_grads[1],
            grad_w_proj,
            grad_b_proj,
            grad_from_two[1],
            grad_from_two[2],
            grad_b_down,
        ),
        ("dp", "tensor"),
    )
    mlp_summed = lax.psum((grad_w_up, grad_b_up, grad_w_down), "dp")
    return (
        output,
        input_grad,
        summed[0],
        summed[1],
        summed[2],
        summed[3],
        summed[4],
        summed[5],
        summed[6],
        summed[7],
        summed[8],
        summed[9],
        summed[10],
        summed[11],
        mlp_summed[0],
        mlp_summed[1],
        mlp_summed[2],
        summed[12],
    )


def solution(mesh):
    return jax.shard_map(
        per_device,
        mesh=mesh,
        in_specs=(
            P(("dp", "tensor"), None),
            P(("dp", "tensor")),
            P(None, ("dp", "tensor"), None),
            P(),
            P(),
            P(),
            P(),
            P(),
            P(),
            P(),
            P(),
            P(),
            P(),
            P(),
            P(),
            P(None, "tensor"),
            P("tensor"),
            P("tensor", None),
            P(),
            P(("dp", "tensor"), None),
        ),
        out_specs=(
            P(("dp", "tensor"), None),
            P(("dp", "tensor"), None),
            P(),
            P(),
            P(),
            P(),
            P(),
            P(),
            P(),
            P(),
            P(),
            P(),
            P(),
            P(),
            P(None, "tensor"),
            P("tensor"),
            P("tensor", None),
            P(),
        ),
        check_vma=False,
    )
```

profile of v0, /device:TPU:0, one launch (start us, length us, event | category | flops | bytes accessed | tf_op | source)
XLA Modules:
  0.0 2125.0 jit_solution(17922374645029894747)
XLA Ops:
  108.6 15.1 slice_bitcast_fusion.7
  125.3 69.1 %add_reduce_fusion.2 = f32[8,10,10,768]{3,2,1,0:T(8,128)} fusion(f32[768]{0:T(1024)S(1)} %copy-done.108, f32[768]{0:T(1024)S(1)} %copy-done.136, f32[768]{0:T(1024)S(1)} %copy-done.144, f32[768]{0:T(1024)S(1)} %copy-done.147, f32[768]{0:T(1024)S(1)} %copy-done.150, f32[768]{0:T(1024)S(1)} %copy-done.153, f32[768]{0:T(1024)S(1)} %copy-done.155, ...), kind=kLoop, calls=%fused_computation.210 | loop fusion | flops 32563200 | bytes 7455744 | tf_op jit(solution)/shard_map/jvp()/add | solution.py:90
  267.7 76.3 %add_reduce_fusion.1 = f32[8,10,10,768]{3,2,1,0:T(8,128)} fusion(f32[768]{0:T(1024)S(1)} %tile.497, f32[768]{0:T(1024)} %tile.495, f32[768]{0:T(1024)} %tile.493, f32[768]{0:T(1024)} %tile.491, f32[768]{0:T(1024)} %tile.489, f32[768]{0:T(1024)} %tile.487, f32[768]{0:T(1024)} %tile.485, f32[768]{0:T(1024)} %tile.483, f32[768]{0:T(1024)} %tile.481, ...), kind=kLoop, calls=%fused_computation.208 | loop fusion | flops 32563200 | bytes 7455744 | tf_op jit(solution)/shard_map/jvp()/add | solution.py:90
  419.8 76.1 %fusion.116 = (f32[8,10,10,768]{3,2,1,0:T(8,128)}, f32[1,8,10,10,768]{4,0,3,2,1:T(1,128)}) fusion(f32[768]{0:T(1024)} %tile.443, f32[768]{0:T(1024)} %tile.441, f32[768]{0:T(1024)} %tile.439, f32[768]{0:T(1024)} %tile.437, f32[768]{0:T(1024)} %tile.435, f32[768]{0:T(1024)} %tile.433, f32[768]{0:T(1024)} %tile.431, f32[768]{0:T(1024)} %tile.429, ...), kind=kLoop, calls=%fused_computation.511 | loop fusion | flops 32563200 | bytes 9913344 | tf_op jit(solution)/shard_map/jvp()/add | solution.py:90
  579.5 13.5 fusion.53
  602.8 14.4 select_reduce_fusion
  655.2 37.4 %all-gather.3.cloned.1.call-done = bf16[3200,768]{1,0:T(8,128)(2,1)} async-done(((bf16[800,768]{1,0:T(8,128)(2,1)}), bf16[3200,768]{1,0:T(8,128)(2,1)}) %all-gather.3.cloned.1.call-update) | async-done | bytes 4915216 | tf_op jit(solution)/shard_map/all_gather | solution.py:202
  703.8 29.5 %all-gather.5.cloned.1.call-done = bf16[3200,768]{1,0:T(8,128)(2,1)} async-done(((bf16[800,768]{1,0:T(8,128)(2,1)}), bf16[3200,768]{1,0:T(8,128)(2,1)}) %all-gather.5.cloned.1.call-update) | async-done | bytes 4915216 | tf_op jit(solution)/shard_map/all_gather | solution.py:213
  789.2 13.9 add_reduce_fusion
  841.1 47.1 %reduce-scatter.3.cloned.1.call-done = bf16[800,768]{1,0:T(8,128)(2,1)} async-done(((bf16[3200,768]{1,0:T(8,128)(2,1)}), bf16[800,768]{1,0:T(8,128)(2,1)}) %reduce-scatter.3.cloned.1.call-update) | async-done | bytes 1228816 | tf_op jit(solution)/shard_map/reduce_scatter | solution.py:207
  899.3 14.3 fusion.57
  913.6 24.3 %fusion.2 = (bf16[1,8,800,1000]{3,2,1,0:T(8,128)(2,1)}, f32[8,800]{1,0:T(8,128)S(1)}) fusion(f32[8,800,1000]{2,1,0:T(8,128)} %get-tuple-element.317, f32[8,800]{1,0:T(8,128)S(1)} %copy-done.77, pred[1000]{0:T(1024)(128)(4,1)S(1)} %copy-done.212, f32[8,800,1000]{2,1,0:T(8,128)} %fusion.57), kind=kLoop, calls=%fused_computation.8 | loop fusion | flops 31993600 | bytes 64052200 | tf_op jit(solution)/shard_map/exp | solution.py:238
  942.4 16.9 multiply_convert_fusion
  992.7 35.6 %multiply_reduce_fusion.62 = (f32[768]{0:T(1024)}, f32[768]{0:T(1024)}, f32[768]{0:T(1024)}, f32[768]{0:T(1024)}, f32[768]{0:T(1024)}, /*index=5*/f32[768]{0:T(1024)}, f32[768]{0:T(1024)}, f32[768]{0:T(1024)}, f32[768]{0:T(1024)}) fusion(f32[1,8,10,10,768]{4,0,3,2,1:T(1,128)} %reshape.3234, f32[1,8,10,10,768]{4,0,3,2,1:T(1,128)} %get-tuple-element.142), kind=kLoop, calls=%fused_computation.166 | loop fusion | flops 11052288 | bytes 4942848 | tf_op jit(solution)/shard_map/transpose(jvp())/reduce_sum | solution.py:90
  1028.4 26.9 %multiply_reduce_fusion.63 = (f32[768]{0:T(1024)}, f32[768]{0:T(1024)}, f32[768]{0:T(1024)}, f32[768]{0:T(1024)}, f32[768]{0:T(1024)}, /*index=5*/f32[768]{0:T(1024)}, f32[768]{0:T(1024)}, f32[768]{0:T(1024)}, f32[768]{0:T(1024)}) fusion(f32[1,8,10,10,768]{4,0,3,2,1:T(1,128)S(1)} %copy-done.2, f32[1,8,10,10,768]{4,0,3,2,1:T(1,128)S(1)} %copy-done.15), kind=kLoop, calls=%fused_computation.167 | loop fusion | flops 11052288 | bytes 4942848 | tf_op jit(solution)/shard_map/transpose(jvp())/reduce_sum | solution.py:90
  1075.7 35.6 %multiply_reduce_fusion.89 = (f32[768]{0:T(1024)}, f32[768]{0:T(1024)}, f32[768]{0:T(1024)}, f32[768]{0:T(1024)}, f32[768]{0:T(1024)}, /*index=5*/f32[768]{0:T(1024)}, f32[768]{0:T(1024)}, f32[768]{0:T(1024)}, f32[768]{0:T(1024)}) fusion(f32[1,8,10,10,768]{4,0,3,2,1:T(1,128)} %reshape.3232, f32[1,8,10,10,768]{4,0,3,2,1:T(1,128)} %copy-done.17), kind=kLoop, calls=%fused_computation.193 | loop fusion | flops 11052288 | bytes 4942848 | tf_op jit(solution)/shard_map/transpose(jvp())/reduce_sum | solution.py:90
  1111.3 26.9 %multiply_reduce_fusion.90 = (f32[768]{0:T(1024)}, f32[768]{0:T(1024)}, f32[768]{0:T(1024)}, f32[768]{0:T(1024)}, f32[768]{0:T(1024)}, /*index=5*/f32[768]{0:T(1024)}, f32[768]{0:T(1024)}, f32[768]{0:T(1024)}, f32[768]{0:T(1024)}) fusion(f32[1,8,10,10,768]{4,0,3,2,1:T(1,128)S(1)} %copy-done.5, f32[1,8,10,10,768]{4,0,3,2,1:T(1,128)S(1)} %copy-done.18), kind=kLoop, calls=%fused_computation.194 | loop fusion | flops 11052288 | bytes 4942848 | tf_op jit(solution)/shard_map/transpose(jvp())/reduce_sum | solution.py:90
  1148.9 26.9 %multiply_reduce_fusion.88 = (f32[768]{0:T(1024)}, f32[768]{0:T(1024)}, f32[768]{0:T(1024)}, f32[768]{0:T(1024)}, f32[768]{0:T(1024)}, /*index=5*/f32[768]{0:T(1...) fusion(f32[1,8,10,10,768]{4,0,3,2,1:T(1,128)} %reshape.3232, ...), kind=kLoop, calls=%fused_computation.192 | loop fusion | flops 11053056 | bytes 9861120 | tf_op jit(solution)/shard_map/transpose(jvp())/reduce_sum | solution.py:90
  1175.8 23.8 %multiply_reduce_fusion.61 = (f32[768]{0:T(1024)}, f32[768]{0:T(1024)}, f32[768]{0:T(1024)}, f32[768]{0:T(1024)}, f32[768]{0:T(1024)}, /*index=5*/f32[768]{0:T(1...) fusion(f32[1,8,10,10,768]{4,0,3,2,1:T(1,128)S(1)} %copy-done.3, ...), kind=kLoop, calls=%fused_computation.165 | loop fusion | flops 11053056 | bytes 9861120 | tf_op jit(solution)/shard_map/transpose(jvp())/reduce_sum | solution.py:90
  1256.2 35.1 %multiply_reduce_fusion.35 = (f32[768]{0:T(1024)S(1)}, f32[768]{0:T(1024)S(1)}, f32[768]{0:T(1024)S(1)}, f32[768]{0:T(1024)S(1)}, f32[768]{0:T(1024)S(1)}, /*ind...) fusion(f32[1,8,10,10,768]{4,0,3,2,1:T(1,128)} %reshape.3237, ...), kind=kLoop, calls=%fused_computation.139 | loop fusion | flops 11052288 | bytes 4942848 | tf_op jit(solution)/shard_map/transpose(jvp())/reduce_sum | solution.py:90
  1291.3 26.3 %multiply_reduce_fusion.36 = (f32[768]{0:T(1024)S(1)}, f32[768]{0:T(1024)S(1)}, f32[768]{0:T(1024)S(1)}, f32[768]{0:T(1024)S(1)}, f32[768]{0:T(1024)S(1)}, /*ind...) fusion(f32[1,8,10,10,768]{4,0,3,2,1:T(1,128)S(1)} %copy-done.11, ...), kind=kLoop, calls=%fused_computation.140 | loop fusion | flops 11052288 | bytes 4942848 | tf_op jit(solution)/shard_map/transpose(jvp())/reduce_sum | solution.py:90
  1317.8 22.0 %multiply_reduce_fusion.34 = (f32[768]{0:T(1024)S(1)}, f32[768]{0:T(1024)S(1)}, f32[768]{0:T(1024)S(1)}, f32[768]{0:T(1024)S(1)}, f32[768]{0:T(1024)S(1)}, /*ind...) fusion(f32[1,8,10,10,768]{4,0,3,2,1:T(1,128)S(1)} %copy-done.11, ...), kind=kLoop, calls=%fused_computation.138 | loop fusion | flops 11053056 | bytes 9861120 | tf_op jit(solution)/shard_map/transpose(jvp())/reduce_sum | solution.py:90
  1362.1 23.0 %multiply_reduce_fusion.77 = (f32[768]{0:T(1024)}, f32[768]{0:T(1024)S(1)}, f32[768]{0:T(1024)S(1)}, f32[1,8,10,10,768]{4,0,3,2,1:T(1,128)S(1)}, f32[1,8,10,10,7...) fusion(f32[1,8,10,10,768]{4,0,3,2,1:T(1,128)S(1)} %copy-done.6,, ...), kind=kLoop, calls=%fused_computation.181 | loop fusion | flops 11671296 | bytes 46743552 | tf_op jit(solution)/shard_map/transpose(jvp())/reduce_sum | solution.py:90
  1385.2 20.6 broadcast_multiply_fusion.27
  1406.2 31.8 %broadcast_multiply_fusion = (f32[1,8,10,10,768]{4,0,3,2,1:T(1,128)}, f32[1,8,10,10,768]{4,0,3,2,1:T(1,128)}, f32[1,8,10,10,768]{4,0,3,2,1:T(1,128)}, f32[1,8,10...) fusion(f32[1,8,10,10,768]{4,0,3,2,1:T(1,128)S(1)} %copy-done.4,, ...), kind=kLoop, calls=%fused_computation.224 | loop fusion | flops 11059200 | bytes 46749696 | tf_op jit(solution)/shard_map/transpose(jvp())/mul | solution.py:90
  1438.2 30.9 %broadcast_multiply_fusion.54 = (f32[1,8,10,10,768]{4,0,3,2,1:T(1,128)}, f32[1,8,10,10,768]{4,0,3,2,1:T(1,128)}, f32[1,8,10,10,768]{4,0,3,2,1:T(1,128)}, f32[1,8...) fusion(f32[1,8,10,10,768]{4,0,3,2,1:T(1,128)S(1)} %copy-done.6,, ...), kind=kLoop, calls=%fused_computation.278 | loop fusion | flops 11059200 | bytes 46749696 | tf_op jit(solution)/shard_map/transpose(jvp())/mul | solution.py:90
  1482.4 60.1 %pad_add_fusion.1 = f32[1,10,12,12,768]{4,0,3,2,1:T(1,128)S(1)} fusion(f32[1,8,10,10,768]{4,0,3,2,1:T(1,128)S(1)} %get-tuple-element.155, f32[1,8,10,10,768]{4,0,3,2,1:T(1,128)S(1)} %get-tuple-element.156, f32[1,8,10,10,768]{4,0,3,2,1:T(1,128)S(1)} %get-tuple-element.157, f32[1,8,10,10,768]{4,0,3,2,1:T(1,128)S(1)} %copy-done.37, ...), kind=kLoop, calls=%fused_computation.30 | loop fusion | flops 22118400 | bytes 56033280 | tf_op jit(solution)/shard_map/transpose(jvp())/add_any | solution.py:83
  1548.9 62.1 %pad_add_fusion.2 = f32[1,10,12,12,768]{4,0,3,2,1:T(1,128)S(1)} fusion(f32[1,8,10,10,768]{4,0,3,2,1:T(1,128)} %get-tuple-element.194, f32[1,8,10,10,768]{4,0,3,2,1:T(1,128)} %get-tuple-element.195, f32[1,8,10,10,768]{4,0,3,2,1:T(1,128)} %get-tuple-element.196, f32[1,8,10,10,768]{4,0,3,2,1:T(1,128)} %get-tuple-element.197, ...), kind=kLoop, calls=%fused_computation.31 | loop fusion | flops 22118400 | bytes 56033280 | tf_op jit(solution)/shard_map/transpose(jvp())/add_any | solution.py:83
  1617.6 61.5 %pad_add_fusion.3 = f32[1,10,12,12,768]{4,0,3,2,1:T(1,128)S(1)} fusion(f32[1,8,10,10,768]{4,0,3,2,1:T(1,128)} %get-tuple-element.169, f32[1,8,10,10,768]{4,0,3,2,1:T(1,128)} %get-tuple-element.170, f32[1,8,10,10,768]{4,0,3,2,1:T(1,128)} %get-tuple-element.171, f32[1,8,10,10,768]{4,0,3,2,1:T(1,128)} %get-tuple-element.172, ...), kind=kLoop, calls=%fused_computation.32 | loop fusion | flops 22118400 | bytes 56033280 | tf_op jit(solution)/shard_map/transpose(jvp())/add_any | solution.py:83
  1778.3 22.2 %psum.125 = f32[768]{0:T(1024)} all-reduce(f32[768]{0:T(1024)S(1)} %copy-done.227), channel_id=1, replica_groups=mesh['dp'=8,'tensor'=4] {'dp'}, use_global_device_ids=true, to_apply=%region_135.136 | all-reduce | flops 768 | bytes 6144 | tf_op jit(solution)/shard_map/psum | solution.py:284
  1800.5 100.8 %all-reduce.187.cloned.1.call-done = (f32[768]{0:T(1024)}, f32[768]{0:T(1024)}, f32[2304]{0:T(1024)}, f32[3,27,96]{2,1,0:T(8,128)}, f32[3,96]{1,0:T(4,128)}, /*i...) async-done(((f32[768]{0:T(1024)}, f32[768]{0:T(1024)}, f32[2304]{0:T(1024)}, ...) | async-done | bytes 81424 | tf_op jit(solution)/shard_map/psum | solution.py:266
  1901.3 197.9 %all-reduce.189.cloned.1.call-done = (f32[768,2304]{1,0:T(8,128)}, f32[768,768]{1,0:T(8,128)}) async-done(((f32[768,2304]{1,0:T(8,128)}, f32[768,768]{1,0:T(8,128)}), (f32[768,2304]{1,0:T(8,128)}, f32[768,768]{1,0:T(8,128)})) %all-reduce.189.cloned.1.call-update) | async-done | bytes 9437200 | tf_op jit(solution)/shard_map/psum | solution.py:266
  (940 shorter events, 788.6 us)
Async XLA Ops:
  7.2 81.0 %copy-start = (bf16[768,2304]{1,0:T(8,128)(2,1)S(1)}, bf16[768,2304]{1,0:T(8,128)(2,1)}, u32[]{:S(2)}) copy-start(bf16[768,2304]{1,0:T(8,128)(2,1)} %param.25) | copy-start | bytes 10616836
  7.2 685.4 %all-gather.3.cloned.1.call-start = ((), (), s32[]{:S(2)}) async-start(), calls=%async_computation.2 | async-start | bytes 6144000 | tf_op jit(solution)/shard_map/all_gather | solution.py:202
  9.3 883.9 %copy-start.87 = (f32[800]{0:T(1024)}, f32[800]{0:T(1024)S(1)}, u32[]{:S(2)}) copy-start(f32[800]{0:T(1024)S(1)} %or_convert_fusion.1) | copy-start | bytes 9604
  21.0 102.6 %copy-start.100 = (f32[768]{0:T(1024)}, f32[768]{0:T(1024)S(1)}, u32[]{:S(2)}) copy-start(f32[768]{0:T(1024)S(1)} %tile.345) | copy-start | bytes 9220
  24.6 71.2 %copy-start.89 = (f32[800]{0:T(1024)}, f32[800]{0:T(1024)S(1)}, u32[]{:S(2)}) copy-start(f32[800]{0:T(1024)S(1)} %broadcast_multiply_fusion.85) | copy-start | bytes 9604
  27.0 68.8 %copy-start.98 = (f32[800]{0:T(1024)}, f32[800]{0:T(1024)S(1)}, u32[]{:S(2)}) copy-start(f32[800]{0:T(1024)S(1)} %fusion.91) | copy-start | bytes 9604
  205.1 139.0 %copy-start.138 = (f32[768]{0:T(1024)}, f32[768]{0:T(1024)S(1)}, u32[]{:S(2)}) copy-start(f32[768]{0:T(1024)S(1)} %tile.497) | copy-start | bytes 9220
  206.5 137.6 %copy-start.140 = (f32[768]{0:T(1024)}, f32[768]{0:T(1024)S(1)}, u32[]{:S(2)}) copy-start(f32[768]{0:T(1024)S(1)} %tile.457) | copy-start | bytes 9220
  208.5 135.5 %copy-start.142 = (f32[768]{0:T(1024)}, f32[768]{0:T(1024)S(1)}, u32[]{:S(2)}) copy-start(f32[768]{0:T(1024)S(1)} %tile.455) | copy-start | bytes 9220
  355.0 141.0 %copy-start.181 = (f32[768]{0:T(1024)}, f32[768]{0:T(1024)S(1)}, u32[]{:S(2)}) copy-start(f32[768]{0:T(1024)S(1)} %tile.421) | copy-start | bytes 9220
  355.6 140.3 %copy-start.183 = (f32[768]{0:T(1024)}, f32[768]{0:T(1024)S(1)}, u32[]{:S(2)}) copy-start(f32[768]{0:T(1024)S(1)} %tile.419) | copy-start | bytes 9220
  357.6 138.3 %copy-start.185 = (f32[768]{0:T(1024)}, f32[768]{0:T(1024)S(1)}, u32[]{:S(2)}) copy-start(f32[768]{0:T(1024)S(1)} %tile.417) | copy-start | bytes 9220
  507.9 120.5 %copy-start.208 = (f32[96]{0:T(128)}, f32[96]{0:T(128)S(1)}, u32[]{:S(2)}) copy-start(f32[96]{0:T(128)S(1)} %get-tuple-element.312) | copy-start | bytes 1156
  651.2 82.2 %all-gather.5.cloned.1.call-start = ((), (), s32[]{:S(2)}) async-start(), calls=%async_computation.4 | async-start | bytes 6144000 | tf_op jit(solution)/shard_map/all_gather | solution.py:213
  653.8 182.7 %reduce-scatter.5.cloned.1.call-start = ((), (), s32[]{:S(2)}) async-start(), calls=%async_computation.5 | async-start | bytes 12288000 | tf_op jit(solution)/shard_map/reduce_scatter | solution.py:221
  755.4 132.8 %reduce-scatter.3.cloned.1.call-start = ((), (), s32[]{:S(2)}) async-start(), calls=%async_computation.3 | async-start | bytes 6144000 | tf_op jit(solution)/shard_map/reduce_scatter | solution.py:207
  765.8 1034.7 %all-reduce.191.cloned.1.call-start = ((), (), s32[]{:S(2)}) async-start(), calls=%async_computation.8 | async-start | bytes 9437184 | tf_op jit(solution)/shard_map/psum | solution.py:284
  830.1 1071.2 %all-reduce.187.cloned.1.call-start = ((), (), s32[]{:S(2)}) async-start(), calls=%async_computation.6 | async-start | bytes 237568 | tf_op jit(solution)/shard_map/psum | solution.py:266
  1548.8 136.7 %copy-start.24 = (f32[1,1,8,10,10,768]{5,0,4,3,2,1:T(1,128)}, f32[1,1,8,10,10,768]{5,0,4,3,2,1:T(1,128)S(1)}, u32[]{:S(2)}) copy-start(f32[1,1,8,10,10,768]{5,0,4,3,2,1:T(1,128)S(1)} %fusion.37) | copy-start | bytes 7372804
  1548.9 62.1 %copy-start.35 = (f32[1,8,10,10,768]{4,0,3,2,1:T(1,128)S(1)}, f32[1,8,10,10,768]{4,0,3,2,1:T(1,128)}, u32[]{:S(2)}) copy-start(f32[1,8,10,10,768]{4,0,3,2,1:T(1,128)} %get-tuple-element.147) | copy-start | bytes 7372804
  1548.9 62.1 %copy-start.36 = (f32[1,8,10,10,768]{4,0,3,2,1:T(1,128)S(1)}, f32[1,8,10,10,768]{4,0,3,2,1:T(1,128)}, u32[]{:S(2)}) copy-start(f32[1,8,10,10,768]{4,0,3,2,1:T(1,128)} %get-tuple-element.148) | copy-start | bytes 7372804
  1548.9 62.1 %copy-start.38 = (f32[1,8,10,10,768]{4,0,3,2,1:T(1,128)S(1)}, f32[1,8,10,10,768]{4,0,3,2,1:T(1,128)}, u32[]{:S(2)}) copy-start(f32[1,8,10,10,768]{4,0,3,2,1:T(1,128)} %get-tuple-element.190) | copy-start | bytes 7372804
  1548.9 62.1 %copy-start.39 = (f32[1,8,10,10,768]{4,0,3,2,1:T(1,128)S(1)}, f32[1,8,10,10,768]{4,0,3,2,1:T(1,128)}, u32[]{:S(2)}) copy-start(f32[1,8,10,10,768]{4,0,3,2,1:T(1,128)} %get-tuple-element.191) | copy-start | bytes 7372804
  1548.9 62.1 %copy-start.40 = (f32[1,8,10,10,768]{4,0,3,2,1:T(1,128)S(1)}, f32[1,8,10,10,768]{4,0,3,2,1:T(1,128)}, u32[]{:S(2)}) copy-start(f32[1,8,10,10,768]{4,0,3,2,1:T(1,128)} %get-tuple-element.192) | copy-start | bytes 7372804
  1548.9 62.1 %copy-start.41 = (f32[1,8,10,10,768]{4,0,3,2,1:T(1,128)S(1)}, f32[1,8,10,10,768]{4,0,3,2,1:T(1,128)}, u32[]{:S(2)}) copy-start(f32[1,8,10,10,768]{4,0,3,2,1:T(1,128)} %get-tuple-element.193) | copy-start | bytes 7372804
  1617.5 68.0 %copy-start.25 = (f32[1,1,8,10,10,768]{5,0,4,3,2,1:T(1,128)}, f32[1,1,8,10,10,768]{5,0,4,3,2,1:T(1,128)S(1)}, u32[]{:S(2)}) copy-start(f32[1,1,8,10,10,768]{5,0,4,3,2,1:T(1,128)S(1)} %fusion.38) | copy-start | bytes 7372804
  1617.5 61.5 %copy-start.33 = (f32[1,8,10,10,768]{4,0,3,2,1:T(1,128)S(1)}, f32[1,8,10,10,768]{4,0,3,2,1:T(1,128)}, u32[]{:S(2)}) copy-start(f32[1,8,10,10,768]{4,0,3,2,1:T(1,128)} %get-tuple-element.145) | copy-start | bytes 7372804
  1617.5 61.5 %copy-start.34 = (f32[1,8,10,10,768]{4,0,3,2,1:T(1,128)S(1)}, f32[1,8,10,10,768]{4,0,3,2,1:T(1,128)}, u32[]{:S(2)}) copy-start(f32[1,8,10,10,768]{4,0,3,2,1:T(1,128)} %get-tuple-element.146) | copy-start | bytes 7372804
  1617.5 61.5 %copy-start.42 = (f32[1,8,10,10,768]{4,0,3,2,1:T(1,128)S(1)}, f32[1,8,10,10,768]{4,0,3,2,1:T(1,128)}, u32[]{:S(2)}) copy-start(f32[1,8,10,10,768]{4,0,3,2,1:T(1,128)} %get-tuple-element.165) | copy-start | bytes 7372804
  1617.5 61.5 %copy-start.43 = (f32[1,8,10,10,768]{4,0,3,2,1:T(1,128)S(1)}, f32[1,8,10,10,768]{4,0,3,2,1:T(1,128)}, u32[]{:S(2)}) copy-start(f32[1,8,10,10,768]{4,0,3,2,1:T(1,128)} %get-tuple-element.166) | copy-start | bytes 7372804
  1617.6 61.5 %copy-start.44 = (f32[1,8,10,10,768]{4,0,3,2,1:T(1,128)S(1)}, f32[1,8,10,10,768]{4,0,3,2,1:T(1,128)}, u32[]{:S(2)}) copy-start(f32[1,8,10,10,768]{4,0,3,2,1:T(1,128)} %get-tuple-element.167) | copy-start | bytes 7372804
  1772.2 327.0 %all-reduce.189.cloned.1.call-start = ((), (), s32[]{:S(2)}) async-start(), calls=%async_computation.7 | async-start | bytes 18874368 | tf_op jit(solution)/shard_map/psum | solution.py:266
  (229 other events, 3374.9 us)
Sparse Core Ops, SparseCore 0:
  651.3 41.2 all-gather.2
  694.7 38.5 all-gather.4
  755.5 80.9 reduce-scatter.4
  839.0 49.1 reduce-scatter.2
  892.7 169.9 all-reduce.190
  1772.3 128.9 all-reduce.186
  1908.4 190.7 all-reduce.188
where the time goes:
time: 2140 us; the launch traced here: 2130 us
  other arithmetic  1000 us (47%)
  local copies, waits for them, and re-layouts  457 us (21%)
  waiting for transfers between devices  419 us (20%)
  matrix products  205 us (10%)
  blocking collectives  22.2 us (1%)
    psum x2, waiting for transfers between devices, per_device(): lax.psum((grad_from_one[1], grad_from_one[2], grad_w_qkv, grad_b_qkv, poo...  299 us
    reduce_sum x10, other arithmetic, pool_field(): accumulated = accumulated + window * kernel_wide[kernel_tap]  282 us
    add x3, other arithmetic, pool_field(): accumulated = accumulated + window * kernel_wide[kernel_tap]  221 us
    another operation x162, local copies, waits for them, and re-layouts, pool_field(): kernel_wide = jnp.tile(kernel, (1, HEADS))  191 us
    add_any x3, other arithmetic, pool_field(): padded[:, frame_shift:frame_shift + FRAMES, row_shift:row_shift + SIDE, c...  184 us
    mul x5, other arithmetic, pool_field(): accumulated = accumulated + window * kernel_wide[kernel_tap]  105 us
    reshape x10, local copies, waits for them, and re-layouts, pool_norm(): per_head = pooled.reshape(clip_count, LENGTH, HEADS, HEAD_DIM)  54.6 us
    reduce_scatter x1, waiting for transfers between devices, per_device(): lax.psum_scatter(jnp.dot(row_piece, w_down, preferred_element_type=jnp.fl...  47.1 us
  transfers between devices with their start and end apart: 7, of which 6 were waited for; matrix products, arithmetic and copies ran while one was open for 46% of the time, Pallas kernels for 0%

commit v1 on v0

v1 whole, which is shorter than its diff:
```python
import functools

import jax
import jax.numpy as jnp
import numpy as np
from jax import lax
from jax.experimental import pallas as pl
from jax.experimental.pallas import tpu as pltpu
from jax.sharding import PartitionSpec as P

D = 768
HEADS = 8
HEAD_DIM = 96
FRAMES = 8
SIDE = 10
SMALL_SIDE = 7
SPOTS = SIDE * SIDE
LENGTH = FRAMES * SPOTS
MEM = 200
KEYS = 1024
OFFSETS = FRAMES + 2 * SIDE
REL_ROWS = 53
GROUPS = 2
PER = HEADS // GROUPS
WIDE = PER * HEAD_DIM
TAPS = 27
LANES = 128
BAND = SIDE * FRAMES
CHUNK = 160
PAIRS = 384
MASK_LANE = HEAD_DIM + OFFSETS
EPS = 1e-6
SCALE = HEAD_DIM**-0.5
F32 = jnp.float32
BF16 = jnp.bfloat16
NEG = -1e30
VMEM_LIMIT = 60 * 1024 * 1024


def nn(a, b):
    return jnp.dot(a, b, preferred_element_type=F32)


def nt(a, b):
    return lax.dot_general(a, b, (((1,), (1,)), ((), ())), preferred_element_type=F32)


def tn(a, b):
    return lax.dot_general(a, b, (((0,), (0,)), ((), ())), preferred_element_type=F32)


def lane_of(shape):
    return lax.broadcasted_iota(jnp.int32, shape, len(shape) - 1)


def to_heads(tiles):
    t0, t1, t2 = tiles
    lane = lane_of(t0.shape)
    own = lane < HEAD_DIM
    h1 = pltpu.roll(jnp.where(lane >= 96, t0, t1), 32, t0.ndim - 1)
    h2 = pltpu.roll(jnp.where(lane >= 64, t1, t2), 64, t0.ndim - 1)
    h3 = pltpu.roll(t2, 96, t0.ndim - 1)
    return [jnp.where(own, h, 0.0) for h in (t0, h1, h2, h3)]


def to_dense(heads):
    p0, p1, p2, p3 = heads
    lane = lane_of(p0.shape)
    r1 = pltpu.roll(p1, 96, p0.ndim - 1)
    r2 = pltpu.roll(p2, 64, p0.ndim - 1)
    r3 = pltpu.roll(p3, 32, p0.ndim - 1)
    return [jnp.where(lane < 96, p0, r1), jnp.where(lane < 64, r1, r2), jnp.where(lane < 32, r2, r3)]


def row_norm(x):
    mean = jnp.mean(x, axis=-1, keepdims=True)
    c = x - mean
    rstd = lax.rsqrt(jnp.mean(c * c, axis=-1, keepdims=True) + EPS)
    return c * rstd, rstd


def frame_shift(x, up):
    frame = lax.broadcasted_iota(jnp.int32, x.shape, 1)
    if up:
        return jnp.where(frame == 0, 0.0, pltpu.roll(x, 1, 1))
    return jnp.where(frame == FRAMES - 1, 0.0, pltpu.roll(x, FRAMES - 1, 1))


def fold8(x):
    return jnp.sum(x.reshape(x.shape[0] // 8, 8, x.shape[1]), axis=0)


def tile_at(j):
    return pl.ds(pl.multiple_of(j * LANES, LANES), LANES)


def rows_at(r, size):
    return pl.ds(pl.multiple_of(r * size, size), size)


def fwd_kernel(
    x_ref, vec_ref, valid_ref, wq_ref, wk_ref, wv_ref, bq_ref, bk_ref, bv_ref, pw_ref, ln_ref,
    tall_ref, cmp_ref, sel_ref, kc_ref, memk_ref, memv_ref, wp_ref,
    mid_ref, field_ref, xh_ref, q_ref, k_ref, v_ref, p_ref, o_ref, att_ref,
    n_s, fld_s, pool_s, q_s, acc_s,
):
    g, h = pl.program_id(0), pl.program_id(1)

    @pl.when((g == 0) & (h == 0))
    def _():
        def body(i, _):
            rows = rows_at(i, BAND)
            xh, _ = row_norm(x_ref[rows, :].astype(F32))
            n_s[rows, :] = (xh * vec_ref[0:1, :] + vec_ref[1:2, :]).astype(BF16)
            return 0

        lax.fori_loop(0, SIDE, body, 0)
        for a in range(3):
            fld_s[a, 0:SIDE] = jnp.zeros((SIDE, 8, 3 * WIDE), F32)
            fld_s[a, SPOTS + SIDE : SPOTS + 2 * SIDE] = jnp.zeros((SIDE, 8, 3 * WIDE), F32)

    @pl.when(h == 0)
    def _():
        for p, (w, b) in enumerate(((wq_ref, bq_ref), (wk_ref, bk_ref), (wv_ref, bv_ref))):
            y = nn(n_s[...], w[...]) + b[...]
            field_ref[:, :, p * WIDE : (p + 1) * WIDE] = y.reshape(SPOTS, 8, WIDE)

        def spread(r, _):
            spots = rows_at(r, SIDE)
            ok = valid_ref[spots]
            for j in range(9):
                lanes = slice(j * LANES, (j + 1) * LANES)
                y = field_ref[spots, :, lanes] * ok
                field_ref[spots, :, lanes] = y
                there = rows_at(r + 1, SIDE)
                fld_s[0, there, :, lanes] = frame_shift(y, True)
                fld_s[1, there, :, lanes] = y
                fld_s[2, there, :, lanes] = frame_shift(y, False)
            return 0

        lax.fori_loop(0, SIDE, spread, 0)

        def pool(pj, _):
            p, j = pj // 3, pj % 3
            lanes, own = tile_at(pj), tile_at(j)
            w = [jnp.broadcast_to(pw_ref[p, t : t + 1, own], (8, LANES)) for t in range(TAPS)]

            def row(r, _):
                acc = [None] * SIDE
                for c_in in range(SIDE):
                    for b in range(3):
                        for a in range(3):
                            x = fld_s[a, (r + b) * SIDE + c_in, :, lanes]
                            for e in range(3):
                                c = c_in - e + 1
                                if 0 <= c < SIDE:
                                    term = w[9 * a + 3 * b + e] * x
                                    acc[c] = term if acc[c] is None else acc[c] + term
                for c in range(SIDE):
                    pool_s[r * SIDE + c, :, lanes] = acc[c]
                return 0

            lax.fori_loop(0, SIDE, row, 0)
            return 0

        lax.fori_loop(0, 9, pool, 0)
        lane = lane_of((BAND, LANES))

        def norm(r, _):
            spots, rows = rows_at(r, SIDE), rows_at(r, BAND)
            for p in range(3):
                tiles = [
                    pool_s[spots, :, (3 * p + j) * LANES : (3 * p + j + 1) * LANES].reshape(BAND, LANES)
                    for j in range(3)
                ]
                for i, x in enumerate(to_heads(tiles)):
                    mean = jnp.sum(x, axis=-1, keepdims=True) * (1 / HEAD_DIM)
                    c = jnp.where(lane < HEAD_DIM, x - mean, 0.0)
                    var = jnp.sum(c * c, axis=-1, keepdims=True) * (1 / HEAD_DIM)
                    rstd = lax.rsqrt(var + EPS)
                    xh = c * rstd
                    xh_ref[i, p, rows, :] = jnp.where(lane == HEAD_DIM, rstd, xh)
                    y = xh * ln_ref[p : p + 1, :] + ln_ref[3 + p : 4 + p, :]
                    if p == 0:
                        q_s[i, rows, :] = y
                    elif p == 1:
                        k_ref[i, rows, :] = (y + kc_ref[rows, :]).astype(BF16)
                    else:
                        one = (lane == HEAD_DIM) | (lane == HEAD_DIM + 1)
                        v_ref[i, rows, :] = jnp.where(one, 1.0, y).astype(BF16)
            return 0

        lax.fori_loop(0, SIDE, norm, 0)
        for i in range(PER):
            k_ref[i, LENGTH:KEYS, :] = memk_ref[i]
            v_ref[i, LENGTH:KEYS, :] = memv_ref[i]

    def prepare(r, _):
        rows = rows_at(r, CHUNK)
        q = q_s[h, rows, :]
        near = (nt(q.astype(BF16), tall_ref[...]) * sel_ref[rows, :]).astype(BF16)
        lane = lane_of((CHUNK, LANES))
        ext = q * SCALE + nn(near, cmp_ref[...])
        q_ref[h, rows, :] = jnp.where(lane == MASK_LANE, 1.0, ext).astype(BF16)
        return 0

    lax.fori_loop(0, LENGTH // CHUNK, prepare, 0)

    def attend(r, _):
        rows = rows_at(r, CHUNK)
        lane = lane_of((CHUNK, LANES))
        s = nt(q_ref[h, rows, :], k_ref[h])
        e = jnp.exp(s - jnp.max(s, axis=-1, keepdims=True)).astype(BF16)
        p_ref[0, rows, :] = e
        o = nn(e, v_ref[h])
        total = o[:, HEAD_DIM : HEAD_DIM + 1]
        o = jnp.where(lane < HEAD_DIM, o * (1.0 / total), 0.0)
        o_ref[0, rows, :] = jnp.where(lane == HEAD_DIM, total, o)
        q_s[h, rows, :] += o
        return 0

    lax.fori_loop(0, LENGTH // CHUNK, attend, 0)

    @pl.when(h == PER - 1)
    def _():
        def join(r, _):
            rows = rows_at(r, BAND)
            for j, t in enumerate(to_dense([q_s[i, rows, :] for i in range(PER)])):
                att_ref[rows, j * LANES : (j + 1) * LANES] = t.astype(BF16)
            return 0

        lax.fori_loop(0, SIDE, join, 0)

    @pl.when((h == PER - 1) & (g == 0))
    def _():
        acc_s[...] = nn(att_ref[...], wp_ref[...])

    @pl.when((h == PER - 1) & (g == GROUPS - 1))
    def _():
        mid_ref[...] = x_ref[...].astype(F32) + acc_s[...] + nn(att_ref[...], wp_ref[...]) + vec_ref[4:5, :]


def mlp_kernel(
    mid_ref, cot_ref, vec_ref, valid_ref, up_ref, bu_ref, down_ref,
    out_ref, gm_ref, gml_ref, small_ref, gup_ref, gbu_ref, gdown_ref,
    n_s, nt_s, go_s, y_s, gn_s,
):
    step = pl.program_id(0)

    @pl.when(step == 0)
    def _():
        def body(i, sums):
            rows = rows_at(i, BAND)
            xh, _ = row_norm(mid_ref[rows, :])
            n_s[rows, :] = (xh * vec_ref[2:3, :] + vec_ref[3:4, :]).astype(BF16)
            go = cot_ref[rows, :].astype(F32) * valid_ref[rows, 0:1]
            go_s[rows, :] = go.astype(BF16)
            return sums + fold8(go)

        sums = lax.fori_loop(0, SIDE, body, jnp.zeros((8, D), F32))
        small_ref[2] = sums
        nt_s[...] = n_s[...].T

    pre = nn(n_s[...], up_ref[0]) + bu_ref[0, 0:1, :].astype(F32)
    cdf = 0.5 * (1.0 + lax.erf(pre * 0.7071067811865476))
    act = (pre * cdf).astype(BF16)
    slope = cdf + pre * jnp.exp(pre * pre * -0.5) * 0.3989422804014327
    ga = nt(go_s[...], down_ref[0])
    gh = ga * slope
    gbu_ref[0] = fold8(gh)
    ghl = gh.astype(BF16)
    gdown_ref[0] = tn(act, go_s[...]).astype(gdown_ref.dtype)
    gup_ref[0] = nn(nt_s[...], ghl).astype(gup_ref.dtype)
    y = nn(act, down_ref[0])
    gn = nt(ghl, up_ref[0])

    @pl.when(step == 0)
    def _():
        y_s[...] = y
        gn_s[...] = gn

    @pl.when(step > 0)
    def _():
        y_s[...] += y
        gn_s[...] += gn

    @pl.when(step == pl.num_programs(0) - 1)
    def _():
        def body(i, sums):
            rows = rows_at(i, BAND)
            mid = mid_ref[rows, :]
            ok = valid_ref[rows, 0:1]
            out_ref[rows, :] = ((mid + y_s[rows, :] + vec_ref[5:6, :]) * ok).astype(BF16)
            xh, rstd = row_norm(mid)
            gy = gn_s[rows, :]
            gx = gy * vec_ref[2:3, :]
            m1 = jnp.mean(gx, axis=-1, keepdims=True)
            m2 = jnp.mean(gx * xh, axis=-1, keepdims=True)
            gm = cot_ref[rows, :].astype(F32) * ok + (gx - m1 - xh * m2) * rstd
            gm_ref[rows, :] = gm
            gml_ref[rows, :] = gm.astype(BF16)
            return sums[0] + fold8(gy * xh), sums[1] + fold8(gy), sums[2] + fold8(gm)

        zero = jnp.zeros((8, D), F32)
        sums = lax.fori_loop(0, SIDE, body, (zero, zero, zero))
        small_ref[0] = sums[0]
        small_ref[1] = sums[1]
        small_ref[3] = sums[2]


def bwd_kernel(
    x_ref, vec_ref, valid_ref, gm_ref, gml_ref, wq_ref, wk_ref, wv_ref, pw_ref, ln_ref,
    tall_ref, cmp_ref, sel_ref, wp_ref, field_ref, xh_ref, q_ref, k_ref, v_ref, p_ref, o_ref, att_ref,
    gx_ref, small_ref, gwq_ref, gwk_ref, gwv_ref, gb_ref, gpw_ref, gln_ref, gtall_ref, gwp_ref,
    n_s, do_s, ds_s, dpp_s, g_s, gq_s, gin_s, gn_s,
):
    g, h = pl.program_id(0), pl.program_id(1)

    @pl.when((g == 0) & (h == 0))
    def _():
        def body(i, _):
            rows = rows_at(i, BAND)
            xh, _ = row_norm(x_ref[rows, :].astype(F32))
            n_s[rows, :] = (xh * vec_ref[0:1, :] + vec_ref[1:2, :]).astype(BF16)
            return 0

        lax.fori_loop(0, SIDE, body, 0)
        for a in range(3):
            g_s[a, 0:SIDE] = jnp.zeros((SIDE, 8, WIDE), F32)
            g_s[a, SPOTS + SIDE : SPOTS + 2 * SIDE] = jnp.zeros((SIDE, 8, WIDE), F32)
        gtall_ref[...] = jnp.zeros(gtall_ref.shape, F32)
        gln_ref[...] = jnp.zeros(gln_ref.shape, F32)

    @pl.when(h == 0)
    def _():
        gin_s[:, 0:WIDE] = nt(gml_ref[...], wp_ref[...])

        def split(r, _):
            rows = rows_at(r, BAND)
            tiles = [gin_s[rows, j * LANES : (j + 1) * LANES] for j in range(3)]
            for i, t in enumerate(to_heads(tiles)):
                do_s[i, rows, :] = t
            return 0

        lax.fori_loop(0, SIDE, split, 0)
        gwp_ref[...] = tn(att_ref[...], gml_ref[...]).astype(gwp_ref.dtype)

    lane = lane_of((LENGTH, LANES))
    do = do_s[h]
    o = o_ref[0]
    inv = 1.0 / o[:, HEAD_DIM : HEAD_DIM + 1]
    delta = jnp.sum(do * o, axis=-1, keepdims=True) * inv
    high = delta.astype(BF16).astype(F32)
    doe = jnp.where(lane == HEAD_DIM, -high, jnp.where(lane == HEAD_DIM + 1, high - delta, do * inv)).astype(BF16)
    gq_s[:, 0:LANES] = doe

    def scores(r, _):
        rows = rows_at(r, CHUNK)
        dp = nt(gq_s[rows, 0:LANES], v_ref[0])
        ds_s[rows, :] = (p_ref[0, rows, :].astype(F32) * dp).astype(BF16)
        return 0

    lax.fori_loop(0, LENGTH // CHUNK, scores, 0)
    dqe = nn(ds_s[...], k_ref[0])
    dk = tn(q_ref[0], ds_s[...]).T[:LENGTH]
    dv = tn(doe, p_ref[0]).T[:LENGTH]
    far = (nt(dqe.astype(BF16), cmp_ref[...]) * sel_ref[...]).astype(BF16)
    xq = xh_ref[0, 0]
    query = (jnp.where(lane < HEAD_DIM, xq, 0.0) * ln_ref[0:1, :] + ln_ref[3:4, :]).astype(BF16)
    gtall_ref[...] += tn(far, query)
    dq = dqe * SCALE + do + nn(far, tall_ref[...])
    for p, gy in enumerate((dq, dk, dv)):
        raw = xh_ref[0, p]
        rstd = raw[:, HEAD_DIM : HEAD_DIM + 1]
        gx = gy * ln_ref[p : p + 1, :]
        m1 = jnp.sum(gx, axis=-1, keepdims=True) * (1 / HEAD_DIM)
        m2 = jnp.sum(gx * raw, axis=-1, keepdims=True) * (1 / HEAD_DIM)
        dpp_s[h, p] = (gx - m1 - raw * m2) * rstd
        gln_ref[p] += fold8(gy * raw)
        gln_ref[3 + p] += fold8(gy)

    @pl.when(h == PER - 1)
    def _():
        def branch(p, _):
            def spread(r, _):
                there, rows = rows_at(r + 1, SIDE), rows_at(r, BAND)
                for j, t in enumerate(to_dense([dpp_s[i, p, rows, :] for i in range(PER)])):
                    lanes = slice(j * LANES, (j + 1) * LANES)
                    t = t.reshape(SIDE, 8, LANES)
                    g_s[0, there, :, lanes] = frame_shift(t, False)
                    g_s[1, there, :, lanes] = t
                    g_s[2, there, :, lanes] = frame_shift(t, True)
                return 0

            lax.fori_loop(0, SIDE, spread, 0)

            def pool(j, _):
                lanes, own = tile_at(3 * p + j), tile_at(j)
                for a in range(3):
                    w = [
                        jnp.broadcast_to(pw_ref[p, t : t + 1, own], (8, LANES))
                        for t in range(9 * a, 9 * a + 9)
                    ]

                    def row(r, sums):
                        sums = list(sums)
                        x = [field_ref[r * SIDE + c, :, lanes] for c in range(SIDE)]
                        acc = [None] * SIDE
                        for c_in in range(SIDE):
                            for b in range(3):
                                t = g_s[a, (r + 2 - b) * SIDE + c_in, :, own]
                                for e in range(3):
                                    c = c_in + e - 1
                                    if 0 <= c < SIDE:
                                        term = w[3 * b + e] * t
                                        acc[c] = term if acc[c] is None else acc[c] + term
                                        sums[3 * b + e] = sums[3 * b + e] + x[c] * t
                        for c in range(SIDE):
                            at = pl.ds(pl.multiple_of(r * BAND + c * 8, 8), 8)
                            if a == 0:
                                gin_s[at, lanes] = acc[c]
                            else:
                                gin_s[at, lanes] += acc[c]
                        return tuple(sums)

                    sums = lax.fori_loop(0, SIDE, row, tuple(jnp.zeros((8, LANES), F32) for _ in range(9)))
                    for t in range(9):
                        gpw_ref[p, 9 * a + t, :, own] = sums[t]
                return 0

            lax.fori_loop(0, 3, pool, 0)
            return 0

        lax.fori_loop(0, 3, branch, 0)

        def finish(r, sums):
            rows = rows_at(r, BAND)
            t = gin_s[rows, :] * valid_ref[rows, 0:1]
            gq_s[rows, :] = t.astype(BF16)
            return sums + fold8(t)

        gb_ref[...] = lax.fori_loop(0, SIDE, finish, jnp.zeros((8, 3 * WIDE), F32))
        gn = None
        for p, (w, gw) in enumerate(((wq_ref, gwq_ref), (wk_ref, gwk_ref), (wv_ref, gwv_ref))):
            piece = gq_s[:, p * WIDE : (p + 1) * WIDE]
            gw[...] = tn(n_s[...], piece).astype(gw.dtype)
            term = nt(piece, w[...])
            gn = term if gn is None else gn + term

        @pl.when(g == 0)
        def _():
            gn_s[...] = gn

        @pl.when(g > 0)
        def _():
            gn_s[...] += gn

    @pl.when((h == PER - 1) & (g == GROUPS - 1))
    def _():
        def body(i, sums):
            rows = rows_at(i, BAND)
            xh, rstd = row_norm(x_ref[rows, :].astype(F32))
            gy = gn_s[rows, :]
            gx = gy * vec_ref[0:1, :]
            m1 = jnp.mean(gx, axis=-1, keepdims=True)
            m2 = jnp.mean(gx * xh, axis=-1, keepdims=True)
            gx_ref[rows, :] = gm_ref[rows, :] + (gx - m1 - xh * m2) * rstd
            return sums[0] + fold8(gy * xh), sums[1] + fold8(gy)

        zero = jnp.zeros((8, D), F32)
        sums = lax.fori_loop(0, SIDE, body, (zero, zero))
        small_ref[0] = sums[0]
        small_ref[1] = sums[1]


def position_tables():
    spot = np.arange(LENGTH) // FRAMES
    frame, row, column = np.arange(LENGTH) % FRAMES, spot // SIDE, spot % SIDE
    kinds = ((frame, FRAMES, 0), (row, SIDE, FRAMES), (column, SIDE, FRAMES + SIDE))
    bases = (FRAMES - 1, 2 * FRAMES - 1 + SIDE - 1, 2 * FRAMES - 1 + 2 * SIDE - 1 + SIDE - 1)
    pick = np.zeros((PAIRS, REL_ROWS), np.float32)
    squeeze = np.zeros((PAIRS, LANES), np.float32)
    select = np.zeros((LENGTH, PAIRS), np.float32)
    marks = np.zeros((LENGTH, LANES), np.float32)
    for tile, ((where, size, first), base) in enumerate(zip(kinds, bases)):
        for at in range(size):
            for m in range(size):
                col = tile * LANES + at * size + m
                pick[col, base + at - m] = 1.0
                squeeze[col, HEAD_DIM + first + m] = 1.0
                select[:, col] = where == at
        marks[np.arange(LENGTH), HEAD_DIM + first + where] = 1.0
    inside = (row < SMALL_SIDE) & (column < SMALL_SIDE)
    memory_at = np.arange(KEYS - LENGTH) % (MEM // 2)
    half, small = (SIDE + 1) // 2, (SMALL_SIDE + 1) // 2
    memory_inside = (memory_at // half % half < small) & (memory_at % half < small)
    exists = np.arange(KEYS - LENGTH) < MEM
    return pick, squeeze, select, marks, inside, memory_inside & exists, exists


def blocked(shape, index, single=False):
    if single:
        return pl.BlockSpec(shape, index, pipeline_mode=pl.Buffered(1))
    return pl.BlockSpec(shape, index)


def const(shape):
    return blocked(shape, lambda *_: (0,) * len(shape), True)


def to_spots(x):
    return x.reshape(FRAMES, SPOTS, -1).transpose(1, 0, 2).reshape(LENGTH, -1)


def to_frames(x):
    return x.reshape(SPOTS, FRAMES, -1).transpose(1, 0, 2).reshape(LENGTH, -1)


def sds(shape, dtype):
    return jax.ShapeDtypeStruct(shape, dtype)


def per_device(
    inputs, res_ids, memory, gain_one, bias_one, w_qkv, b_qkv, pool_weight, pool_gain, pool_bias, rel_table,
    w_proj, b_proj, gain_two, bias_two, w_up, b_up, w_down, b_down, cotangent,
):
    split = lax.axis_size("tensor")
    pick, squeeze, select, marks, inside, memory_inside, exists = position_tables()
    up_all = lax.all_gather(w_up, "tensor")
    down_all = lax.all_gather(w_down, "tensor")
    bu_all = lax.all_gather(b_up.reshape(1, -1), "tensor")

    large = res_ids[0] == 1
    valid = (large | inside).astype(F32)
    valid_rows = jnp.broadcast_to(valid[:, None], (LENGTH, LANES))
    x = to_spots(inputs)
    cot = to_spots(cotangent)
    vec = jnp.stack([gain_one, bias_one, gain_two, bias_two, b_proj, b_down, b_down, b_down])
    pw = jnp.pad(jnp.tile(pool_weight, (1, 1, PER)), ((0, 0), (0, 5), (0, 0)))
    ln = jnp.pad(jnp.concatenate([pool_gain, pool_bias]), ((0, 2), (0, LANES - HEAD_DIM)))
    tall = jnp.dot(pick, rel_table, precision=lax.Precision.HIGHEST)
    tall = jnp.pad(tall, ((0, 0), (0, LANES - HEAD_DIM))).astype(BF16)
    cmp = jnp.asarray(squeeze, BF16)
    lanes = np.arange(LANES)
    bar = np.where(lanes == MASK_LANE, np.float32(NEG), np.float32(0))
    kc = marks + (1.0 - valid)[:, None] * bar
    memory_ok = ((large & exists) | memory_inside).astype(F32)
    heads = memory.reshape(2, MEM, HEADS, HEAD_DIM).transpose(0, 2, 1, 3)
    heads = jnp.pad(heads, ((0, 0), (0, 0), (0, KEYS - LENGTH - MEM), (0, LANES - HEAD_DIM)))
    memk = heads[0] + ((1.0 - memory_ok)[:, None] * bar).astype(BF16)
    memv = heads[1] + ((lanes == HEAD_DIM) | (lanes == HEAD_DIM + 1)).astype(BF16)
    bq = b_qkv.reshape(1, -1)

    params = pltpu.CompilerParams(vmem_limit_bytes=VMEM_LIMIT)
    w_spec = [blocked((D, WIDE), lambda g, h, p=p: (0, GROUPS * p + g)) for p in range(3)]
    b_spec = [blocked((1, WIDE), lambda g, h, p=p: (0, GROUPS * p + g)) for p in range(3)]

    def per_group(*shape):
        return blocked(shape, lambda g, h: (g,) + (0,) * (len(shape) - 1))

    def per_head(*shape):
        return blocked(shape, lambda g, h: (PER * g + h,) + (0,) * (len(shape) - 1))

    field_spec = blocked((SPOTS, 8, 3 * WIDE), lambda g, h: (0, 0, g))
    att_spec = blocked((LENGTH, WIDE), lambda g, h: (0, g))
    mid, field, xh, qx, kx, vx, probs, outs, att = pl.pallas_call(
        fwd_kernel,
        grid=(GROUPS, PER),
        in_specs=[
            const((LENGTH, D)), const((8, D)), const((SPOTS, 8, LANES)), *w_spec, *b_spec,
            const((3, 32, WIDE)), const((8, LANES)), const((PAIRS, LANES)), const((PAIRS, LANES)),
            const((LENGTH, PAIRS)), const((LENGTH, LANES)),
            per_group(PER, KEYS - LENGTH, LANES), per_group(PER, KEYS - LENGTH, LANES),
            blocked((WIDE, D), lambda g, h: (g, 0)),
        ],
        out_specs=[
            const((LENGTH, D)), field_spec, per_group(PER, 3, LENGTH, LANES), per_group(PER, LENGTH, LANES),
            per_group(PER, KEYS, LANES), per_group(PER, KEYS, LANES), per_head(1, LENGTH, KEYS),
            per_head(1, LENGTH, LANES), att_spec,
        ],
        out_shape=[
            sds((LENGTH, D), F32), sds((SPOTS, 8, 3 * D), F32), sds((HEADS, 3, LENGTH, LANES), F32),
            sds((HEADS, LENGTH, LANES), BF16), sds((HEADS, KEYS, LANES), BF16), sds((HEADS, KEYS, LANES), BF16),
            sds((HEADS, LENGTH, KEYS), BF16), sds((HEADS, LENGTH, LANES), F32), sds((LENGTH, D), BF16),
        ],
        scratch_shapes=[
            pltpu.VMEM((LENGTH, D), BF16),
            pltpu.VMEM((3, SPOTS + 2 * SIDE, 8, 3 * WIDE), F32),
            pltpu.VMEM((SPOTS, 8, 3 * WIDE), F32),
            pltpu.VMEM((PER, LENGTH, LANES), F32),
            pltpu.VMEM((LENGTH, D), F32),
        ],
        compiler_params=params,
        name="attend",
        cost_estimate=pl.CostEstimate(flops=2 * 3_500_000_000, bytes_accessed=60_000_000, transcendentals=6_500_000),
    )(
        x, vec, valid_rows.reshape(SPOTS, 8, LANES), w_qkv, w_qkv, w_qkv, bq, bq, bq, pw, ln,
        tall, cmp, jnp.asarray(select), kc, memk, memv, w_proj,
    )

    hidden = w_up.shape[1]
    piece = 384
    parts = hidden // piece
    out, gm, gml, small, gup, gbu, gdown = pl.pallas_call(
        mlp_kernel,
        grid=(split * parts,),
        in_specs=[
            const((LENGTH, D)), const((LENGTH, D)), const((8, D)), const((LENGTH, LANES)),
            blocked((1, D, piece), lambda i: (i // parts, 0, i % parts)),
            blocked((1, 1, piece), lambda i: (i // parts, 0, i % parts)),
            blocked((1, piece, D), lambda i: (i // parts, i % parts, 0)),
        ],
        out_specs=[
            const((LENGTH, D)), const((LENGTH, D)), const((LENGTH, D)), const((4, 8, D)),
            blocked((1, D, piece), lambda i: (i // parts, 0, i % parts)),
            blocked((1, 8, piece), lambda i: (i // parts, 0, i % parts)),
            blocked((1, piece, D), lambda i: (i // parts, i % parts, 0)),
        ],
        out_shape=[
            sds((LENGTH, D), BF16), sds((LENGTH, D), F32), sds((LENGTH, D), BF16), sds((4, 8, D), F32),
            sds((split, D, hidden), BF16), sds((split, 8, hidden), F32), sds((split, hidden, D), BF16),
        ],
        scratch_shapes=[
            pltpu.VMEM((LENGTH, D), BF16),
            pltpu.VMEM((D, LENGTH), BF16),
            pltpu.VMEM((LENGTH, D), BF16),
            pltpu.VMEM((LENGTH, D), F32),
            pltpu.VMEM((LENGTH, D), F32),
        ],
        compiler_params=params,
        name="mlp",
        cost_estimate=pl.CostEstimate(flops=2 * 11_300_000_000, bytes_accessed=40_000_000, transcendentals=5_000_000),
    )(mid, cot, vec, valid_rows, up_all, bu_all, down_all)

    gup = lax.psum_scatter(gup, "tensor", scatter_dimension=0, tiled=False)
    gdown = lax.psum_scatter(gdown, "tensor", scatter_dimension=0, tiled=False)
    gup, gdown = lax.psum((gup, gdown), "dp")

    gx, small_one, gwq, gwk, gwv, gb, gpw, gln, gtall, gwp = pl.pallas_call(
        bwd_kernel,
        grid=(GROUPS, PER),
        in_specs=[
            const((LENGTH, D)), const((8, D)), const((LENGTH, LANES)), const((LENGTH, D)), const((LENGTH, D)), *w_spec,
            const((3, 32, WIDE)), const((8, LANES)), const((PAIRS, LANES)), const((PAIRS, LANES)),
            const((LENGTH, PAIRS)), blocked((WIDE, D), lambda g, h: (g, 0)), blocked((SPOTS, 8, 3 * WIDE), lambda g, h: (0, 0, g), True),
            per_head(1, 3, LENGTH, LANES), per_head(1, LENGTH, LANES), per_head(1, KEYS, LANES),
            per_head(1, KEYS, LANES), per_head(1, LENGTH, KEYS), per_head(1, LENGTH, LANES), att_spec,
        ],
        out_specs=[
            const((LENGTH, D)), const((2, 8, D)),
            *[blocked((D, WIDE), lambda g, h: (0, g)) for _ in range(3)],
            blocked((8, 3 * WIDE), lambda g, h: (0, g)),
            blocked((3, TAPS, 8, WIDE), lambda g, h: (0, 0, 0, g)),
            const((6, 8, LANES)), const((PAIRS, LANES)), blocked((WIDE, D), lambda g, h: (g, 0)),
        ],
        out_shape=[
            sds((LENGTH, D), F32), sds((2, 8, D), F32), sds((D, D), BF16), sds((D, D), BF16), sds((D, D), BF16),
            sds((8, 3 * D), F32), sds((3, TAPS, 8, D), F32), sds((6, 8, LANES), F32), sds((PAIRS, LANES), F32),
            sds((D, D), BF16),
        ],
        scratch_shapes=[
            pltpu.VMEM((LENGTH, D), BF16),
            pltpu.VMEM((PER, LENGTH, LANES), F32),
            pltpu.VMEM((LENGTH, KEYS), BF16),
            pltpu.VMEM((PER, 3, LENGTH, LANES), F32),
            pltpu.VMEM((3, SPOTS + 2 * SIDE, 8, WIDE), F32),
            pltpu.VMEM((LENGTH, 3 * WIDE), BF16),
            pltpu.VMEM((LENGTH, 3 * WIDE), F32),
            pltpu.VMEM((LENGTH, D), F32),
        ],
        compiler_params=params,
        name="attend_back",
        cost_estimate=pl.CostEstimate(flops=2 * 7_000_000_000, bytes_accessed=60_000_000, transcendentals=0),
    )(
        x, vec, valid_rows, gm, gml, w_qkv, w_qkv, w_qkv, pw, ln, tall, cmp, jnp.asarray(select), w_proj,
        field, xh, qx, kx, vx, probs, outs, att,
    )

    gb = jnp.sum(gb, axis=0).reshape(GROUPS, 3, WIDE).transpose(1, 0, 2).reshape(-1)
    gpw = jnp.sum(gpw.reshape(3, TAPS, 8, HEADS, HEAD_DIM), axis=(2, 3))
    gln = jnp.sum(gln, axis=1)[:, :HEAD_DIM]
    grel = jnp.dot(pick.T, gtall[:, :HEAD_DIM], precision=lax.Precision.HIGHEST)
    small = jnp.sum(small, axis=1)
    small_one = jnp.sum(small_one, axis=1)
    gbu = lax.psum(jnp.sum(gbu, axis=1), ("dp", "tensor"))
    gbu = lax.dynamic_index_in_dim(gbu, lax.axis_index("tensor"), 0, False)
    gw = lax.psum((gwq, gwk, gwv, gwp), ("dp", "tensor"))
    gb, gpw, gln, grel, small, small_one = lax.psum((gb, gpw, gln, grel, small, small_one), ("dp", "tensor"))
    return (
        to_frames(out),
        to_frames(gx),
        small_one[0],
        small_one[1],
        jnp.concatenate(gw[:3], axis=1).astype(F32),
        gb,
        gpw,
        gln[:3],
        gln[3:],
        grel,
        gw[3].astype(F32),
        small[3],
        small[0],
        small[1],
        gup.astype(F32),
        gbu,
        gdown.astype(F32),
        small[2],
    )


def solution(mesh):
    rows = P(("dp", "tensor"), None)
    return jax.shard_map(
        per_device,
        mesh=mesh,
        in_specs=(
            rows, P(("dp", "tensor")), P(None, ("dp", "tensor"), None), *[P()] * 12,
            P(None, "tensor"), P("tensor"), P("tensor", None), P(), rows,
        ),
        out_specs=(rows, rows, *[P()] * 12, P(None, "tensor"), P("tensor"), P("tensor", None), P()),
        check_vma=False,
    )
```

time: 2140 us -> 700 us (0.33)
  other arithmetic: 1000 us -> 18.9 us
  local copies, waits for them, and re-layouts: 457 us -> 27.4 us
  Pallas kernels: 0 us -> 253 us
  matrix products: 205 us -> 2.21 us
  waiting for transfers between devices: 419 us -> 376 us
    reduce_sum x33 -> x7, other arithmetic: 361 us -> 5.4 us  [the longest x2 2.88 us: per_device(): gpw = jnp.sum(gpw.reshape(3, TAPS, 8, HEADS, HEAD_DIM), axis=(2, 3))]
    pallas_call x0 -> x3, Pallas kernels: none -> 253 us  [the longest x1 111 us: per_device(): pl.pallas_call(bwd_kernel, grid=(GROUPS, PER), in_specs=[const((LENGTH, D...]
    add x8 -> x2, other arithmetic: 243 us -> 2.07 us  [the longest x1 1.15 us: per_device(): heads[1] + ((lanes == HEAD_DIM) | (lanes == HEAD_DIM + 1)).astype(BF16)]
    add_any x13 -> x0, other arithmetic: 206 us -> none  [the longest x3 184 us: pool_field(): padded[:, frame_shift:frame_shift + FRAMES, row_shift:row_shift + SIDE, c...]
    dot_general x23 -> x2, matrix products: 205 us -> 2.21 us  [the longest x1 1.34 us: per_device(): tall = jnp.dot(pick, rel_table, precision=lax.Precision.HIGHEST)]
    another operation x163 -> x10, local copies, waits for them, and re-layouts: 194 us -> 5.06 us  [the longest x7 4.14 us: per_device(): jnp.stack([gain_one, bias_one, gain_two, bias_two, b_proj, b_down, b_down...]
    mul x5 -> x0, other arithmetic: 105 us -> none  [pool_field(): accumulated = accumulated + window * kernel_wide[kernel_tap]]
    psum x3, waiting for transfers between devices: 299 us -> 373 us  [the longest x1 148 us: per_device(): gw = lax.psum((gwq, gwk, gwv, gwp), ('dp', 'tensor'))]
  transfers between devices with their start and end apart: 7 -> 7, of which waited for: 6 -> 3; matrix products, arithmetic and copies ran while one was open for 46% -> 6% of each run, Pallas kernels for 0% -> 29%
where the time goes in v1:
time: 700 us
  waiting for transfers between devices  376 us (54%)
  Pallas kernels  253 us (36%)
  local copies, waits for them, and re-layouts  27.4 us (4%)
  other arithmetic  18.9 us (3%)
  between operations  15.5 us (2%)
    psum x1, waiting for transfers between devices, per_device(): gw = lax.psum((gwq, gwk, gwv, gwp), ('dp', 'tensor'))  148 us
    psum x1, waiting for transfers between devices, per_device(): lax.psum((gb, gpw, gln, grel, small, small_one), ('dp', 'tensor'))  119 us
    pallas_call x1, Pallas kernels, per_device(): pl.pallas_call(bwd_kernel, grid=(GROUPS, PER), in_specs=[const((LENGTH, D...  111 us
    psum x1, waiting for transfers between devices, per_device(): gup, gdown = lax.psum((gup, gdown), 'dp')  106 us
    pallas_call x1, Pallas kernels, per_device(): pl.pallas_call(fwd_kernel, grid=(GROUPS, PER), in_specs=[const((LENGTH, D...  92.6 us
    pallas_call x1, Pallas kernels, per_device(): pl.pallas_call(mlp_kernel, grid=(split * parts,), in_specs=[const((LENGTH...  49.3 us
  transfers between devices with their start and end apart: 7, of which 3 were waited for; matrix products, arithmetic and copies ran while one was open for 6% of the time, Pallas kernels for 29%

profile of v1, /device:TPU:0, one launch (start us, length us, event | category | flops | bytes accessed | tf_op | source)
XLA Modules:
  0.0 699.8 jit_solution(8773007176007735548)
XLA Ops:
  8.0 0.7 all-gather.9.cloned.1.call-update
  9.6 0.9 reshape.119
  14.5 1.2 copy.89
  15.9 1.3 convolution_convert_fusion
  17.3 0.8 copy.75
  18.0 1.3 reshape.118.bq_ref.bk_ref.bv_ref
  19.8 1.2 copy.88
  23.1 6.6 all-gather.3.bu_ref
  30.4 0.9 multiply_add_fusion.kc_ref
  31.4 1.1 fusion.3
  32.5 0.9 broadcast_in_dim.7.valid_ref
  33.4 92.6 %attend.1 = (f32[800,768]{1,0:T(8,128)}, f32[100,8,2304]{2,1,0:T(8,128)}, f32[8,3,800,128]{3,2,1,0:T(8,128)}, bf16[8,800,128]{2,1,0:T(8,128)(2,1)}, bf16[8,1024,...) custom-call(bf16[800,768]{1,0:T(8,128)(2,1)} %bitcast.41, ...), custom_call_target="tpu_custom_call" | custom-call | flops 7000000000 | bytes 60000000 | tf_op jit(solution)/shard_map/attend/pallas_call | solution.py:566
  126.1 0.9 broadcast_in_dim.8.valid_ref
  127.0 49.3 %mlp.1 = (bf16[800,768]{1,0:T(8,128)(2,1)}, f32[800,768]{1,0:T(8,128)}, bf16[800,768]{1,0:T(8,128)(2,1)}, f32[4,8,768]{2,1,0:T(8,128)}, bf16[4,768,768]{2,1,0:T(...) custom-call(f32[800,768]{1,0:T(8,128)} %get-tuple-element.44.mid_ref, bf16[800,768]{1,0:T(8,128)(2,1)} %bitcast.46, ...), custom_call_target="tpu_custom_call" | custom-call | flops 22599999488 | bytes 40000000 | tf_op jit(solution)/shard_map/mlp/pallas_call | solution.py:604
  177.2 110.7 %attend_back.1 = (f32[800,768]{1,0:T(8,128)}, f32[2,8,768]{2,1,0:T(8,128)}, bf16[768,768]{1,0:T(8,128)(2,1)}, bf16[768,768]{1,0:T(8,128)(2,1)}, bf16[768,768]{1,...) custom-call(bf16[800,768]{1,0:T(8,128)(2,1)} %bitcast.42, ...), custom_call_target="tpu_custom_call" | custom-call | flops 14000000000 | bytes 60000000 | tf_op jit(solution)/shard_map/attend_back/pallas_call | solution.py:639
  288.0 2.2 reduce_sum.63
  290.3 0.7 reduce_sum.65
  294.2 0.9 fusion.4
  296.4 2.5 copy.86
  298.9 1.6 reshape.125
  300.5 1.5 copy.87
  302.0 1.2 reshape.123
  303.2 119.5 %all-reduce.11.cloned.1.call-done = (f32[2,768]{1,0:T(2,128)}, f32[2304]{0:T(1024)}, f32[3,27,96]{2,1,0:T(8,128)}, f32[6,96]{1,0:T(8,128)}, f32[53,96]{1,0:T(8,128)}, /*index=5*/f32[4,768]{1,0:T(4,128)}, f32[4,768]{1,0:T(4,128)}) async-done(((f32[2,768]{1,0:T(2,128)}, f32[2304]{0:T(1024)}, f32[3,27,96]{2,1,0:T(8,128)}, f32[6,96]{1,0:T(8,128)}, f32[53,96]{1,0:T(8,128)}, /*index=5*/f32[4,768]{1,0:T(4,128)}, ...) | async-done | bytes 93712 | tf_op jit(solution)/shard_map/psum | solution.py:688
  422.6 1.3 dynamic-slice_reduce_fusion
  424.0 1.5 slice_reduce_fusion
  425.5 1.3 fusion.7
  426.8 148.0 %all-reduce.13.cloned.1.call-done = (bf16[768,768]{1,0:T(8,128)(2,1)}, bf16[768,768]{1,0:T(8,128)(2,1)}, bf16[768,768]{1,0:T(8,128)(2,1)}, bf16[768,768]{1,0:T(8,128)(2,1)}) async-done(((bf16[768,768]{1,0:T(8,128)(2,1)}, bf16[768,768]{1,0:T(8,128)(2,1)}, bf16[768,768]{1,0:T(8,128)(2,1)}, bf16[768,768]{1,0:T(8,128)(2,1)}), (bf16[768,768]{1,0:T(8,128)(2,1)}, bf16[768,768]{1,0:T(8,128)(2,1)}, ...) | async-done | bytes 4718608 | tf_op jit(solution)/shard_map/psum | solution.py:687
  574.8 3.0 convert_element_type.38
  577.8 3.2 maximum_convert_fusion
  581.0 105.5 %all-reduce.15.cloned.1.call-done = (bf16[768,768]{1,0:T(8,128)(2,1)}, bf16[768,768]{1,0:T(8,128)(2,1)}) async-done(((bf16[768,768]{1,0:T(8,128)(2,1)}, bf16[768,768]{1,0:T(8,128)(2,1)}), (bf16[768,768]{1,0:T(8,128)(2,1)}, bf16[768,768]{1,0:T(8,128)(2,1)})) %all-reduce.15.cloned.1.call-update) | async-done | bytes 2359312 | tf_op jit(solution)/shard_map/psum | solution.py:637
  686.6 2.9 convert_element_type.39
  689.5 1.6 convert_element_type.40
  (140 shorter events, 15.4 us)
Async XLA Ops:
  7.2 8.7 %copy-start = (f32[53,96]{1,0:T(8,128)S(1)}, f32[53,96]{1,0:T(8,128)}, u32[]{:S(2)}) copy-start(f32[53,96]{1,0:T(8,128)} %param.40) | copy-start | bytes 61060
  7.2 118.8 %all-gather.7.cloned.1.call-start = ((), (), s32[]{:S(2)}) async-start(), calls=%async_computation.4 | async-start | bytes 5898240 | tf_op jit(solution)/shard_map/all_gather | solution.py:529
  8.0 118.1 %all-gather.9.cloned.1.call-start = ((), (), s32[]{:S(2)}) async-start(), calls=%async_computation.5 | async-start | bytes 5898240 | tf_op jit(solution)/shard_map/all_gather | solution.py:530
  8.7 3.1 copy-start.32
  8.7 3.7 copy-start.33
  8.8 4.3 copy-start.34
  8.8 4.9 copy-start.35
  8.8 5.4 copy-start.2
  8.8 287.2 %reduce-scatter.3.cloned.1.call-start = ((), (), s32[]{:S(2)}) async-start(), calls=%async_computation.2 | async-start | bytes 5898240 | tf_op jit(solution)/shard_map/reduce_scatter | solution.py:635
  10.6 3.0 copy-start.20
  14.5 4.9 copy-start.3
  19.7 9.9 %copy-start.39 = (f32[3,96]{1,0:T(4,128)S(1)}, f32[3,96]{1,0:T(4,128)}, u32[]{:S(2)}) copy-start(f32[3,96]{1,0:T(4,128)} %param.39) | copy-start | bytes 3460
  19.7 9.9 %copy-start.40 = (f32[3,96]{1,0:T(4,128)S(1)}, f32[3,96]{1,0:T(4,128)}, u32[]{:S(2)}) copy-start(f32[3,96]{1,0:T(4,128)} %param.38) | copy-start | bytes 3460
  19.7 10.5 %copy-start.42 = (pred[224]{0:T(512)(128)(4,1)S(1)}, pred[224]{0:T(512)(128)(4,1)}, u32[]{:S(2)}) copy-start(pred[224]{0:T(512)(128)(4,1)} %constant.48.clone) | copy-start | bytes 676
  19.8 10.5 %copy-start.43 = (pred[224]{0:T(512)(128)(4,1)S(1)}, pred[224]{0:T(512)(128)(4,1)}, u32[]{:S(2)}) copy-start(pred[224]{0:T(512)(128)(4,1)} %constant.49.clone) | copy-start | bytes 676
  19.8 10.5 %copy-start.37 = (pred[800]{0:T(1024)(128)(4,1)S(1)}, pred[800]{0:T(1024)(128)(4,1)}, u32[]{:S(2)}) copy-start(pred[800]{0:T(1024)(128)(4,1)} %constant.43.clone) | copy-start | bytes 2404
  19.8 10.5 %copy-start.41 = (f32[128]{0:T(128)S(1)}, f32[128]{0:T(128)}, u32[]{:S(2)}) copy-start(f32[128]{0:T(128)} %constant.46.clone) | copy-start | bytes 1540
  19.8 10.6 %copy-start.9 = (f32[800,128]{1,0:T(8,128)S(1)}, f32[800,128]{1,0:T(8,128)}, u32[]{:S(2)}) copy-start(f32[800,128]{1,0:T(8,128)} %constant.47.clone) | copy-start | bytes 1228804
  19.8 11.5 %copy-start.44 = (bf16[128]{0:T(256)(128)(2,1)S(1)}, bf16[128]{0:T(256)(128)(2,1)}, u32[]{:S(2)}) copy-start(bf16[128]{0:T(256)(128)(2,1)} %constant.50.clone) | copy-start | bytes 772
  33.4 92.6 %copy-start.21 = (f32[800]{0:T(1024)S(1)}, f32[800]{0:T(1024)}, u32[]{:S(2)}) copy-start(f32[800]{0:T(1024)} %copy-done.20) | copy-start | bytes 9604
  176.3 119.7 %reduce-scatter.5.cloned.1.call-start = ((), (), s32[]{:S(2)}) async-start(), calls=%async_computation.3 | async-start | bytes 5898240 | tf_op jit(solution)/shard_map/reduce_scatter | solution.py:636
  176.9 245.7 %all-reduce.11.cloned.1.call-start = ((), (), s32[]{:S(2)}) async-start(), calls=%async_computation.6 | async-start | bytes 249856 | tf_op jit(solution)/shard_map/psum | solution.py:688
  287.9 3.1 copy-start.15
  287.9 3.8 copy-start.18
  287.9 4.4 copy-start.23
  287.9 5.0 copy-start.13
  288.0 5.6 copy-start.12
  288.0 6.2 copy-start.11
  288.0 6.2 copy-start.14
  295.1 279.7 %all-reduce.13.cloned.1.call-start = ((), (), s32[]{:S(2)}) async-start(), calls=%async_computation.7 | async-start | bytes 9437184 | tf_op jit(solution)/shard_map/psum | solution.py:687
  295.7 390.9 %all-reduce.15.cloned.1.call-start = ((), (), s32[]{:S(2)}) async-start(), calls=%async_computation.8 | async-start | bytes 4718592 | tf_op jit(solution)/shard_map/psum | solution.py:637
  689.5 3.4 copy-start.1
  (20 other events, 48.6 us)
Sparse Core Ops, SparseCore 0:
  9.6 40.2 all-gather.6
  51.5 37.5 all-gather.8
  176.4 49.8 reduce-scatter.2
  228.9 47.8 reduce-scatter.4
  295.2 127.3 all-reduce.10
  429.7 145.0 all-reduce.12
  578.4 108.1 all-reduce.14

commit v2 on v1

v2 whole, which is shorter than its diff:
```python
import functools

import jax
import jax.numpy as jnp
import numpy as np
from jax import lax
from jax.experimental import pallas as pl
from jax.experimental.pallas import tpu as pltpu
from jax.sharding import PartitionSpec as P

D = 768
HEADS = 8
HEAD_DIM = 96
FRAMES = 8
SIDE = 10
SMALL_SIDE = 7
SPOTS = SIDE * SIDE
LENGTH = FRAMES * SPOTS
MEM = 200
KEYS = 1024
OFFSETS = FRAMES + 2 * SIDE
REL_ROWS = 53
GROUPS = 2
PER = HEADS // GROUPS
WIDE = PER * HEAD_DIM
TAPS = 27
LANES = 128
BAND = SIDE * FRAMES
CHUNK = 160
PAIRS = 384
MASK_LANE = HEAD_DIM + OFFSETS
EPS = 1e-6
SCALE = HEAD_DIM**-0.5
F32 = jnp.float32
BF16 = jnp.bfloat16
NEG = -1e30
VMEM_LIMIT = 60 * 1024 * 1024


def nn(a, b):
    return jnp.dot(a, b, preferred_element_type=F32)


def nt(a, b):
    return lax.dot_general(a, b, (((1,), (1,)), ((), ())), preferred_element_type=F32)


def tn(a, b):
    return lax.dot_general(a, b, (((0,), (0,)), ((), ())), preferred_element_type=F32)


def lane_of(shape):
    return lax.broadcasted_iota(jnp.int32, shape, len(shape) - 1)


def to_heads(tiles):
    t0, t1, t2 = tiles
    lane = lane_of(t0.shape)
    own = lane < HEAD_DIM
    h1 = pltpu.roll(jnp.where(lane >= 96, t0, t1), 32, t0.ndim - 1)
    h2 = pltpu.roll(jnp.where(lane >= 64, t1, t2), 64, t0.ndim - 1)
    h3 = pltpu.roll(t2, 96, t0.ndim - 1)
    return [jnp.where(own, h, 0.0) for h in (t0, h1, h2, h3)]


def to_dense(heads):
    p0, p1, p2, p3 = heads
    lane = lane_of(p0.shape)
    r1 = pltpu.roll(p1, 96, p0.ndim - 1)
    r2 = pltpu.roll(p2, 64, p0.ndim - 1)
    r3 = pltpu.roll(p3, 32, p0.ndim - 1)
    return [jnp.where(lane < 96, p0, r1), jnp.where(lane < 64, r1, r2), jnp.where(lane < 32, r2, r3)]


def row_norm(x):
    mean = jnp.mean(x, axis=-1, keepdims=True)
    c = x - mean
    rstd = lax.rsqrt(jnp.mean(c * c, axis=-1, keepdims=True) + EPS)
    return c * rstd, rstd


def frame_shift(x, up):
    frame = lax.broadcasted_iota(jnp.int32, x.shape, 1)
    if up:
        return jnp.where(frame == 0, 0.0, pltpu.roll(x, 1, 1))
    return jnp.where(frame == FRAMES - 1, 0.0, pltpu.roll(x, FRAMES - 1, 1))


def fold8(x):
    return jnp.sum(x.reshape(x.shape[0] // 8, 8, x.shape[1]), axis=0)


def put_rows(ref, at, v):
    for j in range(v.shape[1] // LANES):
        ref[pl.ds(at + j, 1), :] = v[:, j * LANES : (j + 1) * LANES]


def put_tiles(ref, v):
    for j in range(v.shape[1] // LANES):
        ref[0, j] = v[:, j * LANES : (j + 1) * LANES].astype(BF16)


def total(x):
    return jnp.sum(x, axis=0, keepdims=True)


def alive(r, large, shape):
    inside = jnp.where(r < SMALL_SIDE, SMALL_SIDE * FRAMES, 0)
    return jnp.where(lax.broadcasted_iota(jnp.int32, shape, 0) < inside, 1.0, large)


def is_large(res_ref):
    return jnp.where(res_ref[0] == 1, 1.0, 0.0).astype(F32)


def put_spots(tiles, r, x):
    for c in range(SIDE):
        for j, (ref, at) in enumerate(tiles):
            to = pl.ds(r * SIDE + c, FRAMES, stride=SPOTS)
            ref[(*at, to, slice(None))] = x[c * FRAMES : (c + 1) * FRAMES, j * LANES : (j + 1) * LANES]


def get_spots(tiles, r):
    rows = [
        jnp.concatenate([ref[(*at, pl.ds(r * SIDE + c, FRAMES, stride=SPOTS), slice(None))] for ref, at in tiles], axis=1)
        for c in range(SIDE)
    ]
    return jnp.concatenate(rows)


def six(ref):
    return [(ref, (j,)) for j in range(D // LANES)]


def line(ref):
    return ref[...].reshape(1, ref.shape[0])


def tile_at(j):
    return pl.ds(pl.multiple_of(j * LANES, LANES), LANES)


def rows_at(r, size):
    return pl.ds(pl.multiple_of(r * size, size), size)


def fwd_kernel(
    res_ref, x_ref, gain_ref, bias_ref, bp_ref, wq_ref, wk_ref, wv_ref, bq_ref, bk_ref, bv_ref, pw_ref, ln_ref,
    tall_ref, cmp_ref, sel_ref, marks_ref, code_ref, mem_ref, wp_ref,
    mid_ref, xs_ref, field_ref, xh_ref, q_ref, k_ref, v_ref, p_ref, o_ref, att_ref,
    n_s, fld_s, pool_s, q_s, acc_s,
):
    g, h = pl.program_id(0), pl.program_id(1)
    large = is_large(res_ref)

    @pl.when((g == 0) & (h == 0))
    def _():
        for j in range(D // LANES):
            acc_s[j] = x_ref[:, j * LANES : (j + 1) * LANES].astype(F32)

        def body(i, _):
            rows = rows_at(i, BAND)
            x = get_spots(six(acc_s), i)
            mid_ref[rows, :] = x + line(bp_ref)
            xs_ref[rows, :] = x.astype(BF16)
            xh, _ = row_norm(x)
            n_s[rows, :] = (xh * line(gain_ref) + line(bias_ref)).astype(BF16)
            return 0

        lax.fori_loop(0, SIDE, body, 0)
        for a in range(3):
            fld_s[a, 0:SIDE] = jnp.zeros((SIDE, 8, WIDE), F32)
            fld_s[a, SPOTS + SIDE : SPOTS + 2 * SIDE] = jnp.zeros((SIDE, 8, WIDE), F32)

    @pl.when(h == 0)
    def _():
        for p, (w, b) in enumerate(((wq_ref, bq_ref), (wk_ref, bk_ref), (wv_ref, bv_ref))):
            y = nn(n_s[...], w[...]) + b[...]
            field_ref[:, :, p * WIDE : (p + 1) * WIDE] = y.reshape(SPOTS, 8, WIDE)

        def branch(p, _):
            def spread(r, _):
                spots = rows_at(r, SIDE)
                ok = alive(r, large, (BAND, LANES)).reshape(SIDE, 8, LANES)
                there = rows_at(r + 1, SIDE)
                for j in range(3):
                    lanes, own = tile_at(3 * p + j), slice(j * LANES, (j + 1) * LANES)
                    y = field_ref[spots, :, lanes] * ok
                    field_ref[spots, :, lanes] = y
                    fld_s[0, there, :, own] = frame_shift(y, True)
                    fld_s[1, there, :, own] = y
                    fld_s[2, there, :, own] = frame_shift(y, False)
                return 0

            lax.fori_loop(0, SIDE, spread, 0)

            def pool(j, _):
                lanes, own = tile_at(3 * p + j), tile_at(j)
                w = [jnp.broadcast_to(pw_ref[p, t : t + 1, own], (8, LANES)) for t in range(TAPS)]

                def row(r, _):
                    acc = [None] * SIDE
                    for c_in in range(SIDE):
                        for b in range(3):
                            for a in range(3):
                                x = fld_s[a, (r + b) * SIDE + c_in, :, own]
                                for e in range(3):
                                    c = c_in - e + 1
                                    if 0 <= c < SIDE:
                                        term = w[9 * a + 3 * b + e] * x
                                        acc[c] = term if acc[c] is None else acc[c] + term
                    for c in range(SIDE):
                        pool_s[r * SIDE + c, :, lanes] = acc[c]
                    return 0

                lax.fori_loop(0, SIDE, row, 0)
                return 0

            lax.fori_loop(0, 3, pool, 0)
            return 0

        lax.fori_loop(0, 3, branch, 0)
        lane = lane_of((BAND, LANES))

        def norm(r, _):
            spots, rows = rows_at(r, SIDE), rows_at(r, BAND)
            bar = jnp.where(lane == MASK_LANE, NEG, 0.0) * (1.0 - alive(r, large, (BAND, LANES)))
            for p in range(3):
                tiles = [
                    pool_s[spots, :, (3 * p + j) * LANES : (3 * p + j + 1) * LANES].reshape(BAND, LANES)
                    for j in range(3)
                ]
                for i, x in enumerate(to_heads(tiles)):
                    mean = jnp.sum(x, axis=-1, keepdims=True) * (1 / HEAD_DIM)
                    c = jnp.where(lane < HEAD_DIM, x - mean, 0.0)
                    var = jnp.sum(c * c, axis=-1, keepdims=True) * (1 / HEAD_DIM)
                    rstd = lax.rsqrt(var + EPS)
                    xh = c * rstd
                    xh_ref[i, p, rows, :] = jnp.where(lane == HEAD_DIM, rstd, xh)
                    y = xh * ln_ref[p : p + 1, :] + ln_ref[3 + p : 4 + p, :]
                    if p == 0:
                        q_s[i, rows, :] = y
                    elif p == 1:
                        k_ref[i, rows, :] = (y + marks_ref[rows, :] + bar).astype(BF16)
                    else:
                        one = (lane == HEAD_DIM) | (lane == HEAD_DIM + 1)
                        v_ref[i, rows, :] = jnp.where(one, 1.0, y).astype(BF16)
            return 0

        lax.fori_loop(0, SIDE, norm, 0)
        code = code_ref[...]
        out = 1.0 - jnp.where(code == 2.0, 1.0, code * large)
        lane_m = lane_of(code.shape)
        for a, ref in enumerate((k_ref, v_ref)):
            tiles = [mem_ref[a, :, j * LANES : (j + 1) * LANES].astype(F32) for j in range(3)]
            for i, m in enumerate(to_heads(tiles)):
                if a == 0:
                    m = jnp.where(lane_m == MASK_LANE, out * NEG, m)
                else:
                    m = jnp.where((lane_m == HEAD_DIM) | (lane_m == HEAD_DIM + 1), 1.0, m)
                ref[i, LENGTH:KEYS, :] = m.astype(BF16)

    def prepare(r, _):
        rows = rows_at(r, CHUNK)
        q = q_s[h, rows, :]
        near = (nt(q.astype(BF16), tall_ref[...]) * sel_ref[rows, :]).astype(BF16)
        lane = lane_of((CHUNK, LANES))
        ext = q * SCALE + nn(near, cmp_ref[...])
        q_ref[h, rows, :] = jnp.where(lane == MASK_LANE, 1.0, ext).astype(BF16)
        return 0

    lax.fori_loop(0, LENGTH // CHUNK, prepare, 0)

    def attend(r, _):
        rows = rows_at(r, CHUNK)
        lane = lane_of((CHUNK, LANES))
        s = nt(q_ref[h, rows, :], k_ref[h])
        e = jnp.exp(s - jnp.max(s, axis=-1, keepdims=True)).astype(BF16)
        p_ref[0, rows, :] = e
        o = nn(e, v_ref[h])
        total = o[:, HEAD_DIM : HEAD_DIM + 1]
        o = jnp.where(lane < HEAD_DIM, o * (1.0 / total), 0.0)
        o_ref[0, rows, :] = jnp.where(lane == HEAD_DIM, total, o)
        q_s[h, rows, :] += o
        return 0

    lax.fori_loop(0, LENGTH // CHUNK, attend, 0)

    @pl.when(h == PER - 1)
    def _():
        def join(r, _):
            rows = rows_at(r, BAND)
            for j, t in enumerate(to_dense([q_s[i, rows, :] for i in range(PER)])):
                att_ref[rows, j * LANES : (j + 1) * LANES] = t.astype(BF16)
            return 0

        lax.fori_loop(0, SIDE, join, 0)
        mid_ref[...] += nn(att_ref[...], wp_ref[...])


def mlp_kernel(
    res_ref, mid_ref, cot_ref, gain_ref, bias_ref, bd_ref, up_ref, bu_ref, down_ref,
    out_ref, gm_ref, gml_ref, small_ref, gup_ref, gdown_ref,
    n_s, nt_s, go_s, y_s, gn_s, wide_s, stage_s,
):
    step = pl.program_id(0)
    large = is_large(res_ref)

    @pl.when(step == 0)
    def _():
        for j in range(D // LANES):
            stage_s[j] = cot_ref[:, j * LANES : (j + 1) * LANES].astype(F32)

        def body(i, sums):
            rows = rows_at(i, BAND)
            xh, _ = row_norm(mid_ref[rows, :])
            n_s[rows, :] = (xh * line(gain_ref) + line(bias_ref)).astype(BF16)
            go = get_spots(six(stage_s), i) * alive(i, large, (BAND, D))
            wide_s[rows, :] = go
            go_s[rows, :] = go.astype(BF16)
            return sums + fold8(go)

        sums = lax.fori_loop(0, SIDE, body, jnp.zeros((8, D), F32))
        put_rows(small_ref, 12, total(sums))
        nt_s[...] = n_s[...].T

    pre = nn(n_s[...], up_ref[0]) + bu_ref[0].astype(F32)[0:1, :]
    cdf = 0.5 * (1.0 + lax.erf(pre * 0.7071067811865476))
    act = (pre * cdf).astype(BF16)
    slope = cdf + pre * jnp.exp(pre * pre * -0.5) * 0.3989422804014327
    ga = nt(go_s[...], down_ref[0])
    gh = ga * slope
    put_rows(small_ref, 24 + step * (gh.shape[1] // LANES), total(fold8(gh)))
    ghl = gh.astype(BF16)
    put_tiles(gdown_ref, tn(act, go_s[...]))
    put_tiles(gup_ref, nn(nt_s[...], ghl))
    y = nn(act, down_ref[0])
    gn = nt(ghl, up_ref[0])

    @pl.when(step == 0)
    def _():
        y_s[...] = y
        gn_s[...] = gn

    @pl.when(step > 0)
    def _():
        y_s[...] += y
        gn_s[...] += gn

    @pl.when(step == pl.num_programs(0) - 1)
    def _():
        def body(i, sums):
            rows = rows_at(i, BAND)
            mid = mid_ref[rows, :]
            put_spots(six(stage_s), i, (mid + y_s[rows, :] + line(bd_ref)) * alive(i, large, (BAND, D)))
            xh, rstd = row_norm(mid)
            gy = gn_s[rows, :]
            gx = gy * line(gain_ref)
            m1 = jnp.mean(gx, axis=-1, keepdims=True)
            m2 = jnp.mean(gx * xh, axis=-1, keepdims=True)
            gm = wide_s[rows, :] + (gx - m1 - xh * m2) * rstd
            gm_ref[rows, :] = gm
            gml_ref[rows, :] = gm.astype(BF16)
            return sums[0] + fold8(gy * xh), sums[1] + fold8(gy), sums[2] + fold8(gm)

        zero = jnp.zeros((8, D), F32)
        sums = lax.fori_loop(0, SIDE, body, (zero, zero, zero))
        for j in range(D // LANES):
            out_ref[:, j * LANES : (j + 1) * LANES] = stage_s[j].astype(BF16)
        for at, v in zip((0, 6, 18), sums):
            put_rows(small_ref, at, total(v))


def bwd_kernel(
    res_ref, x_ref, gain_ref, bias_ref, gm_ref, gml_ref, wq_ref, wk_ref, wv_ref, pw_ref, ln_ref,
    tall_ref, cmp_ref, sel_ref, pick_ref, wp_ref, field_ref, xh_ref, q_ref, k_ref, v_ref, p_ref, o_ref, att_ref,
    gx_ref, small_ref, gwq_ref, gwk_ref, gwv_ref, gwp_ref,
    gpw_s, gtall_s, n_s, do_s, ds_s, dpp_s, g_s, gq_s, gin_s, gn_s,
):
    g, h = pl.program_id(0), pl.program_id(1)
    large = is_large(res_ref)

    @pl.when((g == 0) & (h == 0))
    def _():
        def body(i, _):
            rows = rows_at(i, BAND)
            xh, _ = row_norm(x_ref[rows, :].astype(F32))
            n_s[rows, :] = (xh * line(gain_ref) + line(bias_ref)).astype(BF16)
            return 0

        lax.fori_loop(0, SIDE, body, 0)
        for a in range(3):
            g_s[a, 0:SIDE] = jnp.zeros((SIDE, 8, WIDE), F32)
            g_s[a, SPOTS + SIDE : SPOTS + 2 * SIDE] = jnp.zeros((SIDE, 8, WIDE), F32)
        gtall_s[...] = jnp.zeros(gtall_s.shape, F32)
        small_ref[...] = jnp.zeros(small_ref.shape, F32)
        gpw_s[...] = jnp.zeros(gpw_s.shape, F32)

    @pl.when(h == 0)
    def _():
        gin_s[:, 0:WIDE] = nt(gml_ref[...], wp_ref[...])

        def split(r, _):
            rows = rows_at(r, BAND)
            tiles = [gin_s[rows, j * LANES : (j + 1) * LANES] for j in range(3)]
            for i, t in enumerate(to_heads(tiles)):
                do_s[i, rows, :] = t
            return 0

        lax.fori_loop(0, SIDE, split, 0)
        gw = tn(att_ref[...], gml_ref[...])
        for j in range(D // LANES):
            gwp_ref[j] = gw[:, j * LANES : (j + 1) * LANES].astype(BF16)

    lane = lane_of((LENGTH, LANES))
    do = do_s[h]
    o = o_ref[0]
    inv = 1.0 / o[:, HEAD_DIM : HEAD_DIM + 1]
    delta = jnp.sum(do * o, axis=-1, keepdims=True) * inv
    high = delta.astype(BF16).astype(F32)
    doe = jnp.where(lane == HEAD_DIM, -high, jnp.where(lane == HEAD_DIM + 1, high - delta, do * inv)).astype(BF16)
    gq_s[:, 0:LANES] = doe

    def scores(r, _):
        rows = rows_at(r, CHUNK)
        dp = nt(gq_s[rows, 0:LANES], v_ref[0])
        ds_s[rows, :] = (p_ref[0, rows, :].astype(F32) * dp).astype(BF16)
        return 0

    lax.fori_loop(0, LENGTH // CHUNK, scores, 0)
    dqe = nn(ds_s[...], k_ref[0])
    dk = tn(q_ref[0], ds_s[...]).T[:LENGTH]
    dv = tn(doe, p_ref[0]).T[:LENGTH]
    far = (nt(dqe.astype(BF16), cmp_ref[...]) * sel_ref[...]).astype(BF16)
    xq = xh_ref[0, 0]
    query = (jnp.where(lane < HEAD_DIM, xq, 0.0) * ln_ref[0:1, :] + ln_ref[3:4, :]).astype(BF16)
    gtall_s[...] += tn(far, query)
    dq = dqe * SCALE + do + nn(far, tall_ref[...])
    for p, gy in enumerate((dq, dk, dv)):
        raw = xh_ref[0, p]
        rstd = raw[:, HEAD_DIM : HEAD_DIM + 1]
        gx = gy * ln_ref[p : p + 1, :]
        m1 = jnp.sum(gx, axis=-1, keepdims=True) * (1 / HEAD_DIM)
        m2 = jnp.sum(gx * raw, axis=-1, keepdims=True) * (1 / HEAD_DIM)
        dpp_s[h, p] = (gx - m1 - raw * m2) * rstd
        small_ref[96 + p : 97 + p, :] += total(fold8(gy * raw))
        small_ref[99 + p : 100 + p, :] += total(fold8(gy))

    @pl.when(h == PER - 1)
    def _():
        def branch(p, _):
            def spread(r, _):
                there, rows = rows_at(r + 1, SIDE), rows_at(r, BAND)
                for j, t in enumerate(to_dense([dpp_s[i, p, rows, :] for i in range(PER)])):
                    lanes = slice(j * LANES, (j + 1) * LANES)
                    t = t.reshape(SIDE, 8, LANES)
                    g_s[0, there, :, lanes] = frame_shift(t, False)
                    g_s[1, there, :, lanes] = t
                    g_s[2, there, :, lanes] = frame_shift(t, True)
                return 0

            lax.fori_loop(0, SIDE, spread, 0)

            def pool(j, _):
                lanes, own = tile_at(3 * p + j), tile_at(j)
                for a in range(3):
                    w = [
                        jnp.broadcast_to(pw_ref[p, t : t + 1, own], (8, LANES))
                        for t in range(9 * a, 9 * a + 9)
                    ]

                    def row(r, sums):
                        sums = list(sums)
                        x = [field_ref[r * SIDE + c, :, lanes] for c in range(SIDE)]
                        acc = [None] * SIDE
                        for c_in in range(SIDE):
                            for b in range(3):
                                t = g_s[a, (r + 2 - b) * SIDE + c_in, :, own]
                                for e in range(3):
                                    c = c_in + e - 1
                                    if 0 <= c < SIDE:
                                        term = w[3 * b + e] * t
                                        acc[c] = term if acc[c] is None else acc[c] + term
                                        sums[3 * b + e] = sums[3 * b + e] + x[c] * t
                        for c in range(SIDE):
                            at = pl.ds(pl.multiple_of(r * BAND + c * 8, 8), 8)
                            if a == 0:
                                gin_s[at, lanes] = acc[c]
                            else:
                                gin_s[at, lanes] += acc[c]
                        return tuple(sums)

                    sums = lax.fori_loop(0, SIDE, row, tuple(jnp.zeros((8, LANES), F32) for _ in range(9)))
                    for t in range(9):
                        gpw_s[9 * a + t : 9 * a + t + 1, own] = total(sums[t])
                return 0

            lax.fori_loop(0, 3, pool, 0)
            heads = to_heads([gpw_s[:, j * LANES : (j + 1) * LANES] for j in range(3)])
            small_ref[rows_at(p, 32), :] += heads[0] + heads[1] + heads[2] + heads[3]
            return 0

        lax.fori_loop(0, 3, branch, 0)

        def finish(r, sums):
            rows = rows_at(r, BAND)
            t = gin_s[rows, :] * alive(r, large, (BAND, 3 * WIDE))
            gq_s[rows, :] = t.astype(BF16)
            return sums + fold8(t)

        put_rows(small_ref, 168 + 9 * g, total(lax.fori_loop(0, SIDE, finish, jnp.zeros((8, 3 * WIDE), F32))))
        gn = None
        for p, (w, gw) in enumerate(((wq_ref, gwq_ref), (wk_ref, gwk_ref), (wv_ref, gwv_ref))):
            piece = gq_s[:, p * WIDE : (p + 1) * WIDE]
            value = tn(n_s[...], piece)
            for j in range(WIDE // LANES):
                gw[j] = value[:, j * LANES : (j + 1) * LANES].astype(BF16)
            term = nt(piece, w[...])
            gn = term if gn is None else gn + term

        @pl.when(g == 0)
        def _():
            gn_s[...] = gn

        @pl.when(g > 0)
        def _():
            gn_s[...] += gn

    @pl.when((h == PER - 1) & (g == GROUPS - 1))
    def _():
        stage = [(dpp_s, (j // 3, j % 3)) for j in range(D // LANES)]

        def body(i, sums):
            rows = rows_at(i, BAND)
            xh, rstd = row_norm(x_ref[rows, :].astype(F32))
            gy = gn_s[rows, :]
            gx = gy * line(gain_ref)
            m1 = jnp.mean(gx, axis=-1, keepdims=True)
            m2 = jnp.mean(gx * xh, axis=-1, keepdims=True)
            put_spots(stage, i, gm_ref[rows, :] + (gx - m1 - xh * m2) * rstd)
            return sums[0] + fold8(gy * xh), sums[1] + fold8(gy)

        zero = jnp.zeros((8, D), F32)
        sums = lax.fori_loop(0, SIDE, body, (zero, zero))
        for j, (ref, at) in enumerate(stage):
            gx_ref[:, j * LANES : (j + 1) * LANES] = ref[at]
        put_rows(small_ref, 186, total(sums[0]))
        put_rows(small_ref, 192, total(sums[1]))
        rest, rel = gtall_s[...], None
        for _ in range(3):
            part = rest.astype(BF16)
            rest = rest - part.astype(F32)
            term = nn(pick_ref[...], part)
            rel = term if rel is None else rel + term
        small_ref[104:168, :] = rel


def bit_of(axis, bit):
    return lax.axis_index(axis) // bit % 2


def partner_of(axis, bit):
    me = lax.axis_index(axis)
    return {axis: me + (1 - 2 * (me // bit % 2)) * bit}


def halvings(rows):
    count = 0
    while rows % (32 << count) == 0:
        count += 1
    return count


def reduce_kernel(parts, pieces, links, *refs):
    n = len(pieces)
    ins, one, two, out, small = refs[:n], refs[n], refs[n + 1], refs[n + 2], refs[n + 3]
    big, land, small_land, load_sem, send_sem, recv_sem, back_sem, home_sem, ssend_sem, srecv_sem = refs[n + 4 :]
    loads = [
        pltpu.make_async_copy(ref, big.at[pl.ds(first, rows)], load_sem.at[i])
        for i, (ref, (first, rows)) in enumerate(zip(ins, pieces))
    ]
    for copy in loads:
        copy.start()
    barrier = pltpu.get_barrier_semaphore()
    for link in links:
        pl.semaphore_signal(barrier, inc=1, device_id=partner_of(*link), device_id_type=pl.DeviceIdType.MESH)
    pl.semaphore_wait(barrier, len(links))
    small[0 : one.shape[0]] = one[...]
    small[one.shape[0] :] = two[...]
    for copy in loads:
        copy.wait()

    def send(src, dst, one, two, link):
        return pltpu.make_async_remote_copy(
            src_ref=src, dst_ref=dst, send_sem=one, recv_sem=two,
            device_id=partner_of(*link), device_id_type=pl.DeviceIdType.MESH,
        )

    spans = [[(first, rows)] for first, rows, _ in parts]
    for s in range(max(len(order) for _, _, order in parts)):
        flying = []
        for i, (first, rows, order) in enumerate(parts):
            if s >= len(order):
                continue
            off, size = spans[i][-1]
            half = size // 2
            bit = bit_of(*order[s])
            keep, give, at = off + bit * half, off + (1 - bit) * half, first + rows - size
            if halvings(rows) <= s:
                keep, give, half = off, off, size
            copy = send(
                big.at[pl.ds(pl.multiple_of(give, 16), half)], land.at[pl.ds(at, half)], send_sem.at[i, s], recv_sem.at[i, s], order[s]
            )
            copy.start()
            flying.append((copy, keep, half, at))
            spans[i].append((keep, half))
        extra = None
        if s < len(links):
            extra = send(small, small_land.at[s], ssend_sem.at[s], srecv_sem.at[s], links[s])
            extra.start()
        for copy, keep, half, at in flying:
            copy.wait()
            block = next(b for b in (512, 256, 128, 64, 48, 32, 16) if half % b == 0)

            def add(k, _):
                a = pl.ds(pl.multiple_of(keep + k * block, 16), block)
                b = pl.ds(pl.multiple_of(at + k * block, 16), block)
                big[a, :] = (big[a, :].astype(F32) + land[b, :].astype(F32)).astype(BF16)
                return 0

            lax.fori_loop(0, half // block, add, 0)
        if extra is not None:
            extra.wait()
            small[...] += small_land[s]
    for span in spans:
        off, size = span[-1]
        own = pl.ds(pl.multiple_of(off, 16), size)
        out[own, :] = big[own, :]
    depth = max(len(order) for _, _, order in parts)
    for s in reversed(range(depth)):
        flying = []
        for i, (first, rows, order) in enumerate(parts):
            if s >= min(len(order), halvings(rows)):
                continue
            off, size = spans[i][s + 1]
            here = out.at[pl.ds(pl.multiple_of(off, 16), size)]
            copy = send(here, here, back_sem.at[i, s], home_sem.at[i, s], order[s])
            copy.start()
            flying.append(copy)
        for copy in flying:
            copy.wait()


def bits(axis, size):
    return [(axis, 1 << k) for k in range(size.bit_length() - 1)]


def all_reduce(whole, over_dp, one, two, sizes):
    dp, tensor = bits("dp", sizes["dp"]), bits("tensor", sizes["tensor"])
    links = tensor + dp
    small = sds((one.shape[0] + two.shape[0], LANES), F32)
    pieces, at = [], 0
    for a in whole + over_dp:
        pieces.append((at, a.shape[0]))
        at += a.shape[0]
    cut = sum(a.shape[0] for a in whole)
    core, rest = tensor[:1], tensor[1:]
    third = cut // 3
    orders = (core + rest + dp, core + dp[:1] + dp[1:] + rest, core + dp[1:] + rest + dp[:1])
    parts = [(k * third, third, order) for k, order in enumerate(orders)]
    if over_dp:
        half = (at - cut) // 2
        parts += [(cut, half, dp), (cut + half, half, dp[1:] + dp[:1])]
    assert all(len(order) <= halvings(rows) + 1 for _, rows, order in parts)
    depth = max(len(order) for _, _, order in parts)
    dma = pltpu.SemaphoreType.DMA
    return pl.pallas_call(
        functools.partial(reduce_kernel, parts, pieces, links),
        in_specs=[pl.BlockSpec(memory_space=pl.ANY)] * len(pieces) + [pl.BlockSpec(memory_space=pltpu.VMEM)] * 2,
        out_specs=[pl.BlockSpec(memory_space=pltpu.VMEM)] * 2,
        out_shape=[sds((at, LANES), BF16), sds(small.shape, F32)],
        scratch_shapes=[
            pltpu.VMEM((at, LANES), BF16),
            pltpu.VMEM((at, LANES), BF16),
            pltpu.VMEM((len(links), *small.shape), F32),
            dma((len(pieces),)),
            dma((len(parts), depth)), dma((len(parts), depth)), dma((len(parts), depth)), dma((len(parts), depth)),
            dma((len(links),)), dma((len(links),)),
        ],
        compiler_params=pltpu.CompilerParams(
            vmem_limit_bytes=VMEM_LIMIT, collective_id=1, has_side_effects=True
        ),
        name="sum_all",
        cost_estimate=pl.CostEstimate(flops=10_000_000, bytes_accessed=20_000_000, transcendentals=0),
    )(*whole, *over_dp, one, two)


def unpack_kernel(big_ref, small_ref, *outs):
    squares, vectors, gb_ref, gpw_ref, gain_ref, bias_ref, rel_ref = outs[:4], outs[4:11], *outs[11:]
    for k, first, n in ((0, 0, 18), (1, 18, 6), (2, 24, 6), (3, 30, 6)):
        for j in range(n):
            squares[k][:, j * LANES : (j + 1) * LANES] = big_ref[first + j].astype(F32)

    @pl.when(pl.program_id(0) == 0)
    def _():
        own = 232 + 6 * lax.axis_index("tensor")
        for ref, at in zip(vectors, (186, 192, 226, 208, 214, 220, own)):
            for j in range(6):
                ref[j * LANES : (j + 1) * LANES] = small_ref[at + j, :]
        for g in range(GROUPS):
            for j in range(9):
                to = (j // 3) * D + g * WIDE + j % 3 * LANES
                gb_ref[to : to + LANES] = small_ref[168 + 9 * g + j, :]
        for p in range(3):
            gpw_ref[p] = small_ref[32 * p : 32 * p + TAPS, :HEAD_DIM]
        gain_ref[...] = small_ref[96:99, :HEAD_DIM]
        bias_ref[...] = small_ref[99:102, :HEAD_DIM]
        rel_ref[...] = small_ref[104 : 104 + REL_ROWS, :HEAD_DIM]


def unpack(big, small):
    def whole(*shape):
        return pl.BlockSpec(shape, lambda i: (0,) * len(shape))

    def band(width):
        return pl.BlockSpec((LANES, width), lambda i: (i, 0))

    shapes = [(D,)] * 7 + [(3 * D,), (3, TAPS, HEAD_DIM), (3, HEAD_DIM), (3, HEAD_DIM), (REL_ROWS, HEAD_DIM)]
    return pl.pallas_call(
        unpack_kernel,
        grid=(D // LANES,),
        in_specs=[pl.BlockSpec((36, LANES, LANES), lambda i: (0, i, 0)), whole(*small.shape)],
        out_specs=[band(3 * D), band(D), band(D), band(D), *[whole(*shape) for shape in shapes]],
        out_shape=[sds((D, 3 * D), F32), *[sds((D, D), F32)] * 3, *[sds(shape, F32) for shape in shapes]],
        name="unpack",
        cost_estimate=pl.CostEstimate(flops=0, bytes_accessed=22_000_000, transcendentals=0),
    )(big, small)


def position_tables():
    spot = np.arange(LENGTH) // FRAMES
    frame, row, column = np.arange(LENGTH) % FRAMES, spot // SIDE, spot % SIDE
    kinds = ((frame, FRAMES, 0), (row, SIDE, FRAMES), (column, SIDE, FRAMES + SIDE))
    bases = (FRAMES - 1, 2 * FRAMES - 1 + SIDE - 1, 2 * FRAMES - 1 + 2 * SIDE - 1 + SIDE - 1)
    pick = np.zeros((PAIRS, REL_ROWS), np.float32)
    squeeze = np.zeros((PAIRS, LANES), np.float32)
    select = np.zeros((LENGTH, PAIRS), np.float32)
    marks = np.zeros((LENGTH, LANES), np.float32)
    for tile, ((where, size, first), base) in enumerate(zip(kinds, bases)):
        for at in range(size):
            for m in range(size):
                col = tile * LANES + at * size + m
                pick[col, base + at - m] = 1.0
                squeeze[col, HEAD_DIM + first + m] = 1.0
                select[:, col] = where == at
        marks[np.arange(LENGTH), HEAD_DIM + first + where] = 1.0
    memory_at = np.arange(KEYS - LENGTH) % (MEM // 2)
    half, small = (SIDE + 1) // 2, (SMALL_SIDE + 1) // 2
    memory_inside = (memory_at // half % half < small) & (memory_at % half < small)
    exists = np.arange(KEYS - LENGTH) < MEM
    code = np.where(exists, 1.0 + memory_inside, 0.0).astype(np.float32)
    return pick, squeeze, select, marks, np.repeat(code[:, None], LANES, 1)


def blocked(shape, index, single=False):
    if single:
        return pl.BlockSpec(shape, index, pipeline_mode=pl.Buffered(1))
    return pl.BlockSpec(shape, index)


def const(shape):
    return blocked(shape, lambda *_: (0,) * len(shape), True)


def sds(shape, dtype):
    return jax.ShapeDtypeStruct(shape, dtype)


def per_device(
    inputs, res_ids, memory, gain_one, bias_one, w_qkv, b_qkv, pool_weight, pool_gain, pool_bias, rel_table,
    w_proj, b_proj, gain_two, bias_two, w_up, b_up, w_down, b_down, cotangent,
):
    split = lax.axis_size("tensor")
    pick, squeeze, select, marks, code = position_tables()
    up_all = lax.all_gather(jnp.concatenate([w_up, jnp.broadcast_to(b_up, (16, b_up.shape[0]))]), "tensor")
    down_all = lax.all_gather(w_down, "tensor")
    pw = jnp.pad(jnp.tile(pool_weight, (1, 1, PER)), ((0, 0), (0, 5), (0, 0)))
    ln = jnp.pad(jnp.concatenate([pool_gain, pool_bias]), ((0, 2), (0, LANES - HEAD_DIM)))
    tall = jnp.dot(pick, rel_table, precision=lax.Precision.HIGHEST)
    tall = jnp.pad(tall, ((0, 0), (0, LANES - HEAD_DIM))).astype(BF16)
    cmp = jnp.asarray(squeeze, BF16)
    mem = jnp.pad(memory, ((0, 0), (0, KEYS - LENGTH - MEM), (0, 0)))
    bq = b_qkv.reshape(1, -1)

    params = pltpu.CompilerParams(vmem_limit_bytes=VMEM_LIMIT)
    w_spec = [blocked((D, WIDE), lambda g, h, p=p: (0, GROUPS * p + g)) for p in range(3)]
    b_spec = [blocked((1, WIDE), lambda g, h, p=p: (0, GROUPS * p + g)) for p in range(3)]

    scalar = pl.BlockSpec(memory_space=pltpu.SMEM)
    row = const((D,))

    def per_group(*shape):
        return blocked(shape, lambda g, h: (g,) + (0,) * (len(shape) - 1))

    def per_head(*shape):
        return blocked(shape, lambda g, h: (PER * g + h,) + (0,) * (len(shape) - 1))

    field_spec = blocked((SPOTS, 8, 3 * WIDE), lambda g, h: (0, 0, g))
    att_spec = blocked((LENGTH, WIDE), lambda g, h: (0, g))
    mid, xs, field, xh, qx, kx, vx, probs, outs, att = pl.pallas_call(
        fwd_kernel,
        grid=(GROUPS, PER),
        in_specs=[
            scalar, const((LENGTH, D)), row, row, row, *w_spec, *b_spec,
            const((3, 32, WIDE)), const((8, LANES)), const((PAIRS, LANES)), const((PAIRS, LANES)),
            const((LENGTH, PAIRS)), const((LENGTH, LANES)), const((KEYS - LENGTH, LANES)),
            blocked((2, KEYS - LENGTH, WIDE), lambda g, h: (0, 0, g)),
            blocked((WIDE, D), lambda g, h: (g, 0)),
        ],
        out_specs=[
            const((LENGTH, D)), const((LENGTH, D)), field_spec, per_group(PER, 3, LENGTH, LANES), per_group(PER, LENGTH, LANES),
            per_group(PER, KEYS, LANES), per_group(PER, KEYS, LANES), per_head(1, LENGTH, KEYS),
            per_head(1, LENGTH, LANES), att_spec,
        ],
        out_shape=[
            sds((LENGTH, D), F32), sds((LENGTH, D), BF16), sds((SPOTS, 8, 3 * D), F32), sds((HEADS, 3, LENGTH, LANES), F32),
            sds((HEADS, LENGTH, LANES), BF16), sds((HEADS, KEYS, LANES), BF16), sds((HEADS, KEYS, LANES), BF16),
            sds((HEADS, LENGTH, KEYS), BF16), sds((HEADS, LENGTH, LANES), F32), sds((LENGTH, D), BF16),
        ],
        scratch_shapes=[
            pltpu.VMEM((LENGTH, D), BF16),
            pltpu.VMEM((3, SPOTS + 2 * SIDE, 8, WIDE), F32),
            pltpu.VMEM((SPOTS, 8, 3 * WIDE), F32),
            pltpu.VMEM((PER, LENGTH, LANES), F32),
            pltpu.VMEM((D // LANES, LENGTH, LANES), F32),
        ],
        compiler_params=params,
        name="attend",
        cost_estimate=pl.CostEstimate(flops=2 * 3_500_000_000, bytes_accessed=60_000_000, transcendentals=6_500_000),
    )(
        res_ids, inputs, gain_one, bias_one, b_proj, w_qkv, w_qkv, w_qkv, bq, bq, bq, pw, ln,
        tall, cmp, jnp.asarray(select), jnp.asarray(marks), jnp.asarray(code), mem, w_proj,
    )

    hidden = w_up.shape[1]
    piece = 384
    parts = hidden // piece
    tiles = hidden // LANES
    out, gm, gml, small, gup, gdown = pl.pallas_call(
        mlp_kernel,
        grid=(split * parts,),
        in_specs=[
            scalar, const((LENGTH, D)), const((LENGTH, D)), row, row, row,
            blocked((1, D, piece), lambda i: (i // parts, 0, i % parts)),
            blocked((1, 16, piece), lambda i: (i // parts, D // 16, i % parts)),
            blocked((1, piece, D), lambda i: (i // parts, i % parts, 0)),
        ],
        out_specs=[
            const((LENGTH, D)), const((LENGTH, D)), const((LENGTH, D)), const((24 + split * tiles, LANES)),
            blocked((1, piece // LANES, D, LANES), lambda i: (i // parts, i % parts, 0, 0)),
            blocked((1, D // LANES, piece, LANES), lambda i: (i // parts, 0, i % parts, 0)),
        ],
        out_shape=[
            sds((LENGTH, D), BF16), sds((LENGTH, D), F32), sds((LENGTH, D), BF16), sds((24 + split * tiles, LANES), F32),
            sds((split, tiles, D, LANES), BF16), sds((split, D // LANES, hidden, LANES), BF16),
        ],
        scratch_shapes=[
            pltpu.VMEM((LENGTH, D), BF16),
            pltpu.VMEM((D, LENGTH), BF16),
            pltpu.VMEM((LENGTH, D), BF16),
            *[pltpu.VMEM((LENGTH, D), F32)] * 3,
            pltpu.VMEM((D // LANES, LENGTH, LANES), F32),
        ],
        compiler_params=params,
        name="mlp",
        cost_estimate=pl.CostEstimate(flops=2 * 11_300_000_000, bytes_accessed=40_000_000, transcendentals=5_000_000),
    )(res_ids, mid, cotangent, gain_two, bias_two, b_down, up_all, up_all, down_all)

    gup = lax.psum_scatter(gup, "tensor", scatter_dimension=0, tiled=False)
    gdown = lax.psum_scatter(gdown, "tensor", scatter_dimension=0, tiled=False)

    gx, small_one, gwq, gwk, gwv, gwp = pl.pallas_call(
        bwd_kernel,
        grid=(GROUPS, PER),
        in_specs=[
            scalar, const((LENGTH, D)), row, row, const((LENGTH, D)), const((LENGTH, D)), *w_spec,
            const((3, 32, WIDE)), const((8, LANES)), const((PAIRS, LANES)), const((PAIRS, LANES)),
            const((LENGTH, PAIRS)), const((64, PAIRS)), blocked((WIDE, D), lambda g, h: (g, 0)),
            blocked((SPOTS, 8, 3 * WIDE), lambda g, h: (0, 0, g), True),
            per_head(1, 3, LENGTH, LANES), per_head(1, LENGTH, LANES), per_head(1, KEYS, LANES),
            per_head(1, KEYS, LANES), per_head(1, LENGTH, KEYS), per_head(1, LENGTH, LANES), att_spec,
        ],
        out_specs=[
            const((LENGTH, D)), const((208, LANES)),
            *[blocked((3, D, LANES), lambda g, h: (g, 0, 0)) for _ in range(3)],
            blocked((6, WIDE, LANES), lambda g, h: (0, g, 0)),
        ],
        out_shape=[
            sds((LENGTH, D), F32), sds((208, LANES), F32), *[sds((6, D, LANES), BF16)] * 4,
        ],
        scratch_shapes=[
            pltpu.VMEM((32, WIDE), F32),
            pltpu.VMEM((PAIRS, LANES), F32),
            pltpu.VMEM((LENGTH, D), BF16),
            pltpu.VMEM((PER, LENGTH, LANES), F32),
            pltpu.VMEM((LENGTH, KEYS), BF16),
            pltpu.VMEM((PER, 3, LENGTH, LANES), F32),
            pltpu.VMEM((3, SPOTS + 2 * SIDE, 8, WIDE), F32),
            pltpu.VMEM((LENGTH, 3 * WIDE), BF16),
            pltpu.VMEM((LENGTH, 3 * WIDE), F32),
            pltpu.VMEM((LENGTH, D), F32),
        ],
        compiler_params=params,
        name="attend_back",
        cost_estimate=pl.CostEstimate(flops=2 * 7_000_000_000, bytes_accessed=60_000_000, transcendentals=0),
    )(
        res_ids, xs, gain_one, bias_one, gm, gml, w_qkv, w_qkv, w_qkv, pw, ln, tall, cmp, jnp.asarray(select), jnp.asarray(np.pad(pick.T, ((0, 11), (0, 0))), BF16), w_proj,
        field, xh, qx, kx, vx, probs, outs, att,
    )

    flat = [a.reshape(-1, LANES) for a in (gwq, gwk, gwv, gwp, gup, gdown)]
    sizes = {axis: lax.axis_size(axis) for axis in ("dp", "tensor")}
    big, small = all_reduce(flat[:4], flat[4:], small_one, small, sizes)
    outs = unpack(big.reshape(-1, D, LANES), small)
    squares, (gain1, bias1, bp, gain2, bias2, bd, bu), (gb, gpw, pg, pb, rel) = outs[:4], outs[4:11], outs[11:]

    return (
        out, gx, gain1, bias1, squares[0], gb, gpw, pg, pb, rel, squares[1], bp, gain2, bias2, squares[2], bu, squares[3], bd,
    )


def solution(mesh):
    rows = P(("dp", "tensor"), None)
    return jax.shard_map(
        per_device,
        mesh=mesh,
        in_specs=(
            rows, P(("dp", "tensor")), P(None, ("dp", "tensor"), None), *[P()] * 12,
            P(None, "tensor"), P("tensor"), P("tensor", None), P(), rows,
        ),
        out_specs=(rows, rows, *[P()] * 12, P(None, "tensor"), P("tensor"), P("tensor", None), P()),
        check_vma=False,
    )
```

time: 700 us -> 424 us (0.61)
  waiting for transfers between devices: 376 us -> 1.13 us
  Pallas kernels: 253 us -> 398 us
  local copies, waits for them, and re-layouts: 27.4 us -> 3.93 us
  other arithmetic: 18.9 us -> 3.03 us
    psum x3 -> x0, waiting for transfers between devices: 373 us -> none  [the longest x1 148 us: per_device(): gw = lax.psum((gwq, gwk, gwv, gwp), ('dp', 'tensor'))]
    pallas_call x3 -> x5, Pallas kernels: 253 us -> 398 us  [the longest x1 135 us: all_reduce(): pl.pallas_call(functools.partial(reduce_kernel, parts, pieces, links), in...]
    convert_element_type x6 -> x0, other arithmetic: 10.8 us -> none  [the longest x1 3.21 us: per_device(): jnp.concatenate(gw[:3], axis=1).astype(F32)]
    reshape x10 -> x0, local copies, waits for them, and re-layouts: 8.84 us -> none  [the longest x4 6.74 us: to_frames(): return x.reshape(SPOTS, FRAMES, -1).transpose(1, 0, 2).reshape(LENGTH, -1)]
  transfers between devices with their start and end apart: 7 -> 4, of which waited for: 3 -> 0; matrix products, arithmetic and copies ran while one was open for 6% -> 2% of each run, Pallas kernels for 29% -> 49%
where the time goes in v2:
time: 424 us; the launch traced here: 422 us
  Pallas kernels  398 us (94%)
  between operations  14.6 us (3%)
    pallas_call x1, Pallas kernels, all_reduce(): pl.pallas_call(functools.partial(reduce_kernel, parts, pieces, links), in...  135 us
    pallas_call x1, Pallas kernels, per_device(): pl.pallas_call(bwd_kernel, grid=(GROUPS, PER), in_specs=[scalar, const((L...  112 us
    pallas_call x1, Pallas kernels, per_device(): pl.pallas_call(fwd_kernel, grid=(GROUPS, PER), in_specs=[scalar, const((L...  93.8 us
    pallas_call x1, Pallas kernels, per_device(): pl.pallas_call(mlp_kernel, grid=(split * parts,), in_specs=[scalar, const...  49.1 us
    pallas_call x1, Pallas kernels, unpack(): pl.pallas_call(unpack_kernel, grid=(D // LANES,), in_specs=[pl.BlockSpec(...  8.87 us
  transfers between devices with their start and end apart: 4, of which 0 were waited for; matrix products, arithmetic and copies ran while one was open for 2% of the time, Pallas kernels for 49%

profile of v2, /device:TPU:0, one launch (start us, length us, event | category | flops | bytes accessed | tf_op | source)
XLA Modules:
  0.0 421.6 jit_solution(11568682703097105242)
XLA Ops:
  7.2 0.0 copy-start
  7.2 0.0 all-gather.7.cloned.1.call-start
  7.3 0.7 all-gather.7.cloned.1.call-update
  8.0 0.0 copy-start.3
  8.0 0.0 copy-start.4
  8.0 0.0 all-gather.5.cloned.1.call-start
  8.0 0.7 broadcast_in_dim.3
  8.8 2.4 pad_maximum_fusion
  11.2 0.0 all-gather.5.cloned.1.call-update
  11.2 0.0 reduce-scatter.3.cloned.1.call-start
  11.9 0.0 copy-done.5
  11.9 0.6 reshape.58.bq_ref.bk_ref.bv_ref
  12.5 0.4 convolution_convert_fusion
  13.0 0.1 copy.45
  13.1 0.1 tile.10
  13.3 0.7 pad.19.tall_ref
  14.0 0.9 pad.20.mem_ref
  14.8 0.7 pad.17.pw_ref
  15.5 0.6 select_maximum_fusion.ln_ref
  16.1 93.8 %attend.1 = (f32[800,768]{1,0:T(8,128)}, bf16[800,768]{1,0:T(8,128)(2,1)}, f32[100,8,2304]{2,1,0:T(8,128)}, f32[8,3,800,128]{3,2,1,0:T(8,128)}, bf16[8,800,128]{...) custom-call(s32[1]{0:T(128)S(6)} %copy.46.res_ref, ...), custom_call_target="tpu_custom_call" | custom-call | flops 7000000000 | bytes 60000000 | tf_op jit(solution)/shard_map/attend/pallas_call | solution.py:810
  109.9 0.0 all-gather.7.cloned.1.call-done
  110.0 0.0 all-gather.5.cloned.1.call-done
  110.0 49.1 %mlp.1 = (bf16[800,768]{1,0:T(8,128)(2,1)}, f32[800,768]{1,0:T(8,128)}, bf16[800,768]{1,0:T(8,128)(2,1)}, f32[48,128]{1,0:T(8,128)}, bf16[4,6,768,128]{3,2,1,0:T(8,128)(2,1)}, /*index=5*/bf16[4,6,768,128]{3,2,1,0:T(8,128)(2,1)}) custom-call(s32[1]{0:T(128)S(6)} %copy.46.res_ref, f32[800,768]{1,0:T(8,128)} %get-tuple-element.58.mid_ref, ...), custom_call_target="tpu_custom_call" | custom-call | flops 22599999488 | bytes 40000000 | tf_op jit(solution)/shard_map/mlp/pallas_call | solution.py:849
  159.1 0.0 reduce-scatter.3.cloned.1.call-update
  159.1 0.2 reduce-scatter.5.cloned.1.call-start
  159.3 0.3 reduce-scatter.5.cloned.1.call-update
  159.7 111.6 %attend_back.1 = (f32[800,768]{1,0:T(8,128)}, f32[208,128]{1,0:T(8,128)}, bf16[6,768,128]{2,1,0:T(8,128)(2,1)}, bf16[6,768,128]{2,1,0:T(8,128)(2,1)}, bf16[6,768...) custom-call(s32[1]{0:T(128)S(6)} %copy.46.res_ref, bf16[800,768]{1,0:T(8,128)(2,1)} %get-tuple-element.60.x_ref, ...), custom_call_target="tpu_custom_call" | custom-call | flops 14000000000 | bytes 60000000 | tf_op jit(solution)/shard_map/attend_back/pallas_call | solution.py:882
  271.3 0.0 reduce-scatter.3.cloned.1.call-done
  271.4 0.0 reduce-scatter.5.cloned.1.call-done
  271.4 134.8 %sum_all.1 = (bf16[27648,128]{1,0:T(8,128)(2,1)}, f32[256,128]{1,0:T(8,128)}) custom-call(bf16[4608,128]{1,0:T(8,128)(2,1)} %bitcast.14, bf16[4608,128]{1,0:T(8,128)(2,1)} %bitcast.15, bf16[4608,128]{1,0:T(8,128)(2,1)} %bitcast.16, bf16[4608,128]{1,0:T(8,128)(2,1)} %bitcast.17, bf16[4608,128]{1,0:T(8,128)(2,1)} %bitcast.12, bf16[4608,128]{1,0:T(8,128)(2,1)} %bitcast.13, ...), custom_call_target="tpu_custom_call" | custom-call | flops 10000000 | bytes 20000000 | tf_op jit(solution)/shard_map/sum_all/pallas_call | solution.py:677
  406.1 0.0 copy-start.1
  406.2 8.9 %unpack.1 = (f32[768,2304]{1,0:T(8,128)}, f32[768,768]{1,0:T(8,128)}, f32[768,768]{1,0:T(8,128)}, f32[768,768]{1,0:T(8,128)}, f32[768]{0:T(1024)}, /*index=5*/f3...) custom-call(bf16[36,768,128]{2,1,0:T(8,128)(2,1)} %bitcast.11, ...), custom_call_target="tpu_custom_call" | custom-call | bytes 22000000 | tf_op jit(solution)/shard_map/unpack/pallas_call | solution.py:729
  (12 shorter events, 0.1 us)
Async XLA Ops:
  7.2 5.3 %copy-start = (f32[53,96]{1,0:T(8,128)S(1)}, f32[53,96]{1,0:T(8,128)}, u32[]{:S(2)}) copy-start(f32[53,96]{1,0:T(8,128)} %param.36) | copy-start | bytes 61060
  7.2 102.7 %all-gather.7.cloned.1.call-start = ((), (), s32[]{:S(2)}) async-start(), calls=%async_computation.5 | async-start | bytes 5898240 | tf_op jit(solution)/shard_map/all_gather | solution.py:786
  7.9 4.0 copy-start.5
  8.0 4.6 %copy-start.3 = (f32[384,53]{1,0:T(8,128)S(1)}, f32[384,53]{1,0:T(8,128)}, u32[]{:S(2)}) copy-start(f32[384,53]{1,0:T(8,128)} %constant.18.clone) | copy-start | bytes 244228
  8.0 5.1 %copy-start.4 = (f32[3,27,96]{2,1,0:T(8,128)S(1)}, f32[3,27,96]{2,1,0:T(8,128)}, u32[]{:S(2)}) copy-start(f32[3,27,96]{2,1,0:T(8,128)} %param.33) | copy-start | bytes 93316
  8.0 102.0 %all-gather.5.cloned.1.call-start = ((), (), s32[]{:S(2)}) async-start(), calls=%async_computation.4 | async-start | bytes 6021120 | tf_op jit(solution)/shard_map/all_gather | solution.py:785
  8.8 5.2 %copy-start.2 = (bf16[2,200,768]{2,1,0:T(8,128)(2,1)S(1)}, bf16[2,200,768]{2,1,0:T(8,128)(2,1)}, u32[]{:S(2)}) copy-start(bf16[2,200,768]{2,1,0:T(8,128)(2,1)} %param.28) | copy-start | bytes 1843204
  11.2 4.3 %copy-start.6 = (f32[3,96]{1,0:T(4,128)S(1)}, f32[3,96]{1,0:T(4,128)}, u32[]{:S(2)}) copy-start(f32[3,96]{1,0:T(4,128)} %param.35) | copy-start | bytes 3460
  11.2 4.3 %copy-start.7 = (f32[3,96]{1,0:T(4,128)S(1)}, f32[3,96]{1,0:T(4,128)}, u32[]{:S(2)}) copy-start(f32[3,96]{1,0:T(4,128)} %param.34) | copy-start | bytes 3460
  11.2 260.1 %reduce-scatter.3.cloned.1.call-start = ((), (), s32[]{:S(2)}) async-start(), calls=%async_computation.2 | async-start | bytes 5898240 | tf_op jit(solution)/shard_map/reduce_scatter | solution.py:879
  159.1 112.3 %reduce-scatter.5.cloned.1.call-start = ((), (), s32[]{:S(2)}) async-start(), calls=%async_computation.3 | async-start | bytes 5898240 | tf_op jit(solution)/shard_map/reduce_scatter | solution.py:880
  406.1 8.9 %copy-start.1 = (f32[53,96]{1,0:T(8,128)S(1)}, f32[53,96]{1,0:T(8,128)}, u32[]{:S(2)}) copy-start(f32[53,96]{1,0:T(8,128)} %param.36) | copy-start | bytes 61060
Sparse Core Ops, SparseCore 0:
  9.6 40.1 all-gather.6
  51.9 38.1 all-gather.4
  159.2 50.9 reduce-scatter.2
  212.8 47.8 reduce-scatter.4

commit v3 on v2

--- a/solution.py
+++ b/solution.py
@@ -34,6 +34,8 @@
 F32 = jnp.float32
 BF16 = jnp.bfloat16
 NEG = -1e30
+UP_TICKS = (0, 2, 3, 4, 5, 7, 9)
+DOWN_TICKS = (2, 4, 7, 8, 9, 10, 11, 14)
 VMEM_LIMIT = 60 * 1024 * 1024
 
 
@@ -95,11 +97,6 @@
         ref[pl.ds(at + j, 1), :] = v[:, j * LANES : (j + 1) * LANES]
 
 
-def put_tiles(ref, v):
-    for j in range(v.shape[1] // LANES):
-        ref[0, j] = v[:, j * LANES : (j + 1) * LANES].astype(BF16)
-
-
 def total(x):
     return jnp.sum(x, axis=0, keepdims=True)
 
@@ -142,6 +139,125 @@
 
 def rows_at(r, size):
     return pl.ds(pl.multiple_of(r * size, size), size)
+
+
+def bit_of(axis, bit):
+    return lax.axis_index(axis) // bit % 2
+
+
+def partner_of(axis, bit):
+    me = lax.axis_index(axis)
+    return {axis: me + (1 - 2 * (me // bit % 2)) * bit}
+
+
+def halvings(rows):
+    count = 0
+    while rows % (32 << count) == 0:
+        count += 1
+    return count
+
+
+def bits(axis, size):
+    return [(axis, 1 << k) for k in range(size.bit_length() - 1)]
+
+
+def send(src, dst, one, two, link):
+    return pltpu.make_async_remote_copy(
+        src_ref=src, dst_ref=dst, send_sem=one, recv_sem=two,
+        device_id=partner_of(*link), device_id_type=pl.DeviceIdType.MESH,
+    )
+
+
+def greet(links):
+    barrier = pltpu.get_barrier_semaphore()
+    for link in links:
+        pl.semaphore_signal(barrier, inc=1, device_id=partner_of(*link), device_id_type=pl.DeviceIdType.MESH)
+    pl.semaphore_wait(barrier, len(links))
+
+
+def some(start, rows):
+    return pl.ds(pl.multiple_of(start, 16), rows)
+
+
+def add_rows(dst, at, src, start, rows):
+    block = next(b for b in (512, 256, 128, 64, 48, 32, 16) if rows % b == 0)
+
+    def add(k, _):
+        a, b = some(at + k * block, block), some(start + k * block, block)
+        dst[a, :] = (dst[a, :].astype(F32) + src[b, :].astype(F32)).astype(BF16)
+        return 0
+
+    lax.fori_loop(0, rows // block, add, 0)
+
+
+def chain(work, land, out, send_sem, recv_sem, own_sem, order, merge=None):
+    rows, count = work.shape[0], halvings(work.shape[0])
+
+    def span(s):
+        off, size = 0, rows
+        for k in range(min(s, count)):
+            size //= 2
+            off = off + bit_of(*order[k]) * size
+        return off, size
+
+    def halve(s, k):
+        off, size = span(s)
+        half, bit, at = size // 2, bit_of(*order[s]), rows - size
+        keep, give = off + bit * half, off + (1 - bit) * half
+        if s >= count:
+            keep, give, half = off, off, size
+        copy = send(work.at[some(give, half)], land.at[some(at, half)], send_sem.at[k], recv_sem.at[k], order[s])
+        return copy, (work, keep, land, at, half)
+
+    def join(k):
+        ref, landing, link = merge
+        return send(ref, landing, send_sem.at[k], recv_sem.at[k], link), (work, span(1)[0], landing, 0, ref.shape[0])
+
+    def double(s, k):
+        off, size = span(s + 1)
+        here = out.at[some(off, size)]
+        return send(here, here, send_sem.at[k], recv_sem.at[k], order[s]), None
+
+    def own():
+        off, size = span(len(order))
+        copy = pltpu.make_async_copy(work.at[some(off, size)], out.at[some(off, size)], own_sem)
+        copy.start()
+        copy.wait()
+
+    plans = [functools.partial(halve, s) for s in range(len(order))]
+    if merge is not None:
+        plans.insert(1, join)
+    gather = len(plans)
+    plans += [functools.partial(double, s) for s in reversed(range(min(len(order), count)))]
+
+    def start(k):
+        if k == gather:
+            own()
+        plans[k](k)[0].start()
+
+    def finish(k):
+        copy, todo = plans[k](k)
+        copy.wait()
+        if todo is not None:
+            add_rows(*todo)
+
+    def step(k):
+        if k > 0:
+            finish(k - 1)
+        if k < len(plans):
+            start(k)
+
+    return [functools.partial(step, k) for k in range(len(plans) + 1)]
+
+
+def at_ticks(tick, table, steps):
+    for n in sorted(set(table)):
+        due = [k for k in range(len(steps)) if table[min(k, len(table) - 1)] == n]
+
+        @pl.when(tick == n)
+        def _():
+            for k in due:
+                steps[k]()
 
 
 def fwd_kernel(
@@ -299,12 +415,58 @@
 
 
 def mlp_kernel(
-    res_ref, mid_ref, cot_ref, gain_ref, bias_ref, bd_ref, up_ref, bu_ref, down_ref,
-    out_ref, gm_ref, gml_ref, small_ref, gup_ref, gdown_ref,
-    n_s, nt_s, go_s, y_s, gn_s, wide_s, stage_s,
+    parts, res_ref, mid_ref, cot_ref, gain_ref, bias_ref, bd_ref, up_all, down_all,
+    out_ref, gm_ref, gml_ref, small_ref, gup_ref, gdown_ref, gfar_ref,
+    n_s, nt_s, go_s, y_s, gn_s, wide_s, stage_s, up_s, bu_s, down_s, grad_s, land_s, side_s, load_sem, send_sem, recv_sem,
 ):
     step = pl.program_id(0)
     large = is_large(res_ref)
+    tiles, width = D // LANES, up_s.shape[2]
+    cut, half = tiles * D, tiles * D // 2
+    core, other, near = ("tensor", 1), ("tensor", 2), ("dp", 1)
+
+    def slice_of(k):
+        k = k // parts
+        return (bit_of(*core) + 1 - k % 2) % 2 + 2 * ((bit_of(*other) + 1 - k // 2) % 2)
+
+    def loads(k):
+        t, c = slice_of(k), k % parts
+        lanes = pl.ds(pl.multiple_of(c * width, LANES), width)
+        return [
+            pltpu.make_async_copy(up_all.at[t, pl.ds(0, D), lanes], up_s.at[k], load_sem.at[0, k]),
+            pltpu.make_async_copy(up_all.at[t, pl.ds(D, 16), lanes], bu_s.at[k], load_sem.at[1, k]),
+            pltpu.make_async_copy(down_all.at[t, some(c * width, width)], down_s.at[k], load_sem.at[2, k]),
+        ]
+
+    def to_core(k):
+        return send(grad_s.at[2 * k], land_s.at[k], send_sem.at[k], recv_sem.at[k], core)
+
+    def to_side():
+        return send(grad_s.at[1, pl.ds(0, cut)], side_s.at[pl.ds(0, cut)], send_sem.at[2], recv_sem.at[2], other)
+
+    def to_near():
+        give = cut + (1 - bit_of(*near)) * half
+        return send(grad_s.at[1, some(give, half)], side_s.at[pl.ds(cut, half)], send_sem.at[3], recv_sem.at[3], near)
+
+    @pl.when(step == 0)
+    def _():
+        for k in range(parts * 4):
+            for copy in loads(k):
+                copy.start()
+        greet((core, other, near))
+
+    @pl.when(step == 2 * parts)
+    def _():
+        to_core(0).wait()
+        add_rows(grad_s.at[1], 0, land_s.at[0], 0, 2 * cut)
+        to_side().start()
+        to_near().start()
+
+    for k in range(2):
+
+        @pl.when(step == (2 * k + 1) * parts)
+        def _():
+            to_core(k).start()
 
     @pl.when(step == 0)
     def _():
@@ -324,18 +486,25 @@
         put_rows(small_ref, 12, total(sums))
         nt_s[...] = n_s[...].T
 
-    pre = nn(n_s[...], up_ref[0]) + bu_ref[0].astype(F32)[0:1, :]
+    for copy in loads(step):
+        copy.wait()
+    pre = nn(n_s[...], up_s[step]) + bu_s[step].astype(F32)[0:1, :]
     cdf = 0.5 * (1.0 + lax.erf(pre * 0.7071067811865476))
     act = (pre * cdf).astype(BF16)
     slope = cdf + pre * jnp.exp(pre * pre * -0.5) * 0.3989422804014327
-    ga = nt(go_s[...], down_ref[0])
+    ga = nt(go_s[...], down_s[step])
     gh = ga * slope
-    put_rows(small_ref, 24 + step * (gh.shape[1] // LANES), total(fold8(gh)))
+    own, part = step // parts, step % parts
+    put_rows(small_ref, 24 + slice_of(step) * tiles + part * (width // LANES), total(fold8(gh)))
     ghl = gh.astype(BF16)
-    put_tiles(gdown_ref, tn(act, go_s[...]))
-    put_tiles(gup_ref, nn(nt_s[...], ghl))
-    y = nn(act, down_ref[0])
-    gn = nt(ghl, up_ref[0])
+    value = tn(act, go_s[...]).astype(BF16)
+    for j in range(tiles):
+        grad_s[own, some(cut + j * D + part * width, width), :] = value[:, j * LANES : (j + 1) * LANES]
+    value = nn(nt_s[...], ghl).astype(BF16)
+    for j in range(width // LANES):
+        grad_s[own, some((part * (width // LANES) + j) * D, D), :] = value[:, j * LANES : (j + 1) * LANES]
+    y = nn(act, down_s[step])
+    gn = nt(ghl, up_s[step])
 
     @pl.when(step == 0)
     def _():
@@ -369,16 +538,49 @@
             out_ref[:, j * LANES : (j + 1) * LANES] = stage_s[j].astype(BF16)
         for at, v in zip((0, 6, 18), sums):
             put_rows(small_ref, at, total(v))
+        to_core(1).wait()
+        add_rows(grad_s.at[3], 0, land_s.at[1], 0, 2 * cut)
+        to_side().wait()
+        add_rows(grad_s.at[3], 0, side_s, 0, cut)
+        to_near().wait()
+        keep = cut + bit_of(*near) * half
+        add_rows(grad_s.at[1], keep, side_s, cut, half)
+        gup_ref[...] = grad_s[3, 0:cut, :]
+        gdown_ref[...] = grad_s[3, cut : 2 * cut, :]
+        gfar_ref[...] = grad_s[1, some(keep, half), :]
 
 
 def bwd_kernel(
-    res_ref, x_ref, gain_ref, bias_ref, gm_ref, gml_ref, wq_ref, wk_ref, wv_ref, pw_ref, ln_ref,
+    order, res_ref, x_ref, gain_ref, bias_ref, gm_any, gml_ref, wq_ref, wk_ref, wv_ref, pw_ref, ln_ref,
     tall_ref, cmp_ref, sel_ref, pick_ref, wp_ref, field_ref, xh_ref, q_ref, k_ref, v_ref, p_ref, o_ref, att_ref,
-    gx_ref, small_ref, gwq_ref, gwk_ref, gwv_ref, gwp_ref,
-    gpw_s, gtall_s, n_s, do_s, ds_s, dpp_s, g_s, gq_s, gin_s, gn_s,
+    gup_any, gdown_any, gfar_any,
+    gx_ref, small_ref, gwq_ref, gwk_ref, gwv_ref, gwp_ref, gup_out, gdown_out,
+    gpw_s, gtall_s, n_s, do_s, ds_s, dpp_s, g_s, gq_s, gin_s,
+    up_s, down_s, far_s, up_land, down_land, far_land, load_sem, own_sem, send_sem, recv_sem,
 ):
     g, h = pl.program_id(0), pl.program_id(1)
     large = is_large(res_ref)
+    up_steps = chain(up_s, up_land, gup_out, send_sem.at[0], recv_sem.at[0], own_sem.at[0], order)
+    side = (far_s, far_land, ("tensor", 2))
+    down_steps = chain(down_s, down_land, gdown_out, send_sem.at[1], recv_sem.at[1], own_sem.at[1], order, side)
+
+    def travel(tick):
+        at_ticks(tick, UP_TICKS, up_steps)
+        at_ticks(tick, DOWN_TICKS, down_steps)
+
+    @pl.when((g == 0) & (h == 0))
+    def _():
+        loads = [
+            pltpu.make_async_copy(src, dst, load_sem.at[k])
+            for k, (src, dst) in enumerate(((gup_any, up_s), (gdown_any, down_s), (gfar_any, far_s)))
+        ]
+        for copy in loads:
+            copy.start()
+        greet((("tensor", 2), *order))
+        for copy in loads:
+            copy.wait()
+
+    travel((PER + 3) * g + h)
 
     @pl.when((g == 0) & (h == 0))
     def _():
@@ -496,6 +698,7 @@
                 return 0
 
             lax.fori_loop(0, 3, pool, 0)
+            travel((PER + 3) * g + PER + p)
             heads = to_heads([gpw_s[:, j * LANES : (j + 1) * LANES] for j in range(3)])
             small_ref[rows_at(p, 32), :] += heads[0] + heads[1] + heads[2] + heads[3]
             return 0
@@ -509,6 +712,12 @@
             return sums + fold8(t)
 
         put_rows(small_ref, 168 + 9 * g, total(lax.fori_loop(0, SIDE, finish, jnp.zeros((8, 3 * WIDE), F32))))
+        gm_load = pltpu.make_async_copy(gm_any, gin_s.at[:, pl.ds(0, D)], load_sem.at[3])
+
+        @pl.when(g == GROUPS - 1)
+        def _():
+            gm_load.start()
+
         gn = None
         for p, (w, gw) in enumerate(((wq_ref, gwq_ref), (wk_ref, gwk_ref), (wv_ref, gwv_ref))):
             piece = gq_s[:, p * WIDE : (p + 1) * WIDE]
@@ -520,24 +729,25 @@
 
         @pl.when(g == 0)
         def _():
-            gn_s[...] = gn
+            gx_ref[...] = gn
 
         @pl.when(g > 0)
         def _():
-            gn_s[...] += gn
+            gx_ref[...] += gn
 
     @pl.when((h == PER - 1) & (g == GROUPS - 1))
     def _():
+        pltpu.make_async_copy(gm_any, gin_s.at[:, pl.ds(0, D)], load_sem.at[3]).wait()
         stage = [(dpp_s, (j // 3, j % 3)) for j in range(D // LANES)]
 
         def body(i, sums):
             rows = rows_at(i, BAND)
             xh, rstd = row_norm(x_ref[rows, :].astype(F32))
-            gy = gn_s[rows, :]
+            gy = gx_ref[rows, :]
             gx = gy * line(gain_ref)
             m1 = jnp.mean(gx, axis=-1, keepdims=True)
             m2 = jnp.mean(gx * xh, axis=-1, keepdims=True)
-            put_spots(stage, i, gm_ref[rows, :] + (gx - m1 - xh * m2) * rstd)
+            put_spots(stage, i, gin_s[rows, 0:D] + (gx - m1 - xh * m2) * rstd)
             return sums[0] + fold8(gy * xh), sums[1] + fold8(gy)
 
         zero = jnp.zeros((8, D), F32)
@@ -553,22 +763,7 @@
             term = nn(pick_ref[...], part)
             rel = term if rel is None else rel + term
         small_ref[104:168, :] = rel
-
-
-def bit_of(axis, bit):
-    return lax.axis_index(axis) // bit % 2
-
-
-def partner_of(axis, bit):
-    me = lax.axis_index(axis)
-    return {axis: me + (1 - 2 * (me // bit % 2)) * bit}
-
-
-def halvings(rows):
-    count = 0
-    while rows % (32 << count) == 0:
-        count += 1
-    return count
+        travel(2 * (PER + 3))
 
 
 def reduce_kernel(parts, pieces, links, *refs):
@@ -581,20 +776,11 @@
     ]
     for copy in loads:
         copy.start()
-    barrier = pltpu.get_barrier_semaphore()
-    for link in links:
-        pl.semaphore_signal(barrier, inc=1, device_id=partner_of(*link), device_id_type=pl.DeviceIdType.MESH)
-    pl.semaphore_wait(barrier, len(links))
+    greet(links)
     small[0 : one.shape[0]] = one[...]
     small[one.shape[0] :] = two[...]
     for copy in loads:
         copy.wait()
-
-    def send(src, dst, one, two, link):
-        return pltpu.make_async_remote_copy(
-            src_ref=src, dst_ref=dst, send_sem=one, recv_sem=two,
-            device_id=partner_of(*link), device_id_type=pl.DeviceIdType.MESH,
-        )
 
     spans = [[(first, rows)] for first, rows, _ in parts]
     for s in range(max(len(order) for _, _, order in parts)):
@@ -620,15 +806,7 @@
             extra.start()
         for copy, keep, half, at in flying:
             copy.wait()
-            block = next(b for b in (512, 256, 128, 64, 48, 32, 16) if half % b == 0)
-
-            def add(k, _):
-                a = pl.ds(pl.multiple_of(keep + k * block, 16), block)
-                b = pl.ds(pl.multiple_of(at + k * block, 16), block)
-                big[a, :] = (big[a, :].astype(F32) + land[b, :].astype(F32)).astype(BF16)
-                return 0
-
-            lax.fori_loop(0, half // block, add, 0)
+            add_rows(big, keep, land, at, half)
         if extra is not None:
             extra.wait()
             small[...] += small_land[s]
@@ -649,10 +827,6 @@
             flying.append(copy)
         for copy in flying:
             copy.wait()
-
-
-def bits(axis, size):
-    return [(axis, 1 << k) for k in range(size.bit_length() - 1)]
 
 
 def all_reduce(whole, over_dp, one, two, sizes):
@@ -695,11 +869,11 @@
     )(*whole, *over_dp, one, two)
 
 
-def unpack_kernel(big_ref, small_ref, *outs):
+def unpack_kernel(big_ref, up_ref, down_ref, small_ref, *outs):
     squares, vectors, gb_ref, gpw_ref, gain_ref, bias_ref, rel_ref = outs[:4], outs[4:11], *outs[11:]
-    for k, first, n in ((0, 0, 18), (1, 18, 6), (2, 24, 6), (3, 30, 6)):
+    for out, ref, first, n in zip(squares, (big_ref, big_ref, up_ref, down_ref), (0, 18, 0, 0), (18, 6, 6, 6)):
         for j in range(n):
-            squares[k][:, j * LANES : (j + 1) * LANES] = big_ref[first + j].astype(F32)
+            out[:, j * LANES : (j + 1) * LANES] = ref[first + j].astype(F32)
 
     @pl.when(pl.program_id(0) == 0)
     def _():
@@ -718,7 +892,7 @@
         rel_ref[...] = small_ref[104 : 104 + REL_ROWS, :HEAD_DIM]
 
 
-def unpack(big, small):
+def unpack(big, up, down, small):
     def whole(*shape):
         return pl.BlockSpec(shape, lambda i: (0,) * len(shape))
 
@@ -729,12 +903,14 @@
     return pl.pallas_call(
         unpack_kernel,
         grid=(D // LANES,),
-        in_specs=[pl.BlockSpec((36, LANES, LANES), lambda i: (0, i, 0)), whole(*small.shape)],
+        in_specs=[
+            *[pl.BlockSpec((n, LANES, LANES), lambda i: (0, i, 0)) for n in (24, 6, 6)], whole(*small.shape),
+        ],
         out_specs=[band(3 * D), band(D), band(D), band(D), *[whole(*shape) for shape in shapes]],
         out_shape=[sds((D, 3 * D), F32), *[sds((D, D), F32)] * 3, *[sds(shape, F32) for shape in shapes]],
         name="unpack",
         cost_estimate=pl.CostEstimate(flops=0, bytes_accessed=22_000_000, transcendentals=0),
-    )(big, small)
+    )(big, up, down, small)
 
 
 def position_tables():
@@ -846,23 +1022,20 @@
     piece = 384
     parts = hidden // piece
     tiles = hidden // LANES
-    out, gm, gml, small, gup, gdown = pl.pallas_call(
-        mlp_kernel,
-        grid=(split * parts,),
-        in_specs=[
-            scalar, const((LENGTH, D)), const((LENGTH, D)), row, row, row,
-            blocked((1, D, piece), lambda i: (i // parts, 0, i % parts)),
-            blocked((1, 16, piece), lambda i: (i // parts, D // 16, i % parts)),
-            blocked((1, piece, D), lambda i: (i // parts, i % parts, 0)),
-        ],
+    chunks, cut = split * parts, D // LANES * D
+    dma = pltpu.SemaphoreType.DMA
+    anywhere = pl.BlockSpec(memory_space=pl.ANY)
+    out, gm, gml, small, gup, gdown, gfar = pl.pallas_call(
+        functools.partial(mlp_kernel, parts),
+        grid=(chunks,),
+        in_specs=[scalar, const((LENGTH, D)), const((LENGTH, D)), row, row, row, anywhere, anywhere],
         out_specs=[
             const((LENGTH, D)), const((LENGTH, D)), const((LENGTH, D)), const((24 + split * tiles, LANES)),
-            blocked((1, piece // LANES, D, LANES), lambda i: (i // parts, i % parts, 0, 0)),
-            blocked((1, D // LANES, piece, LANES), lambda i: (i // parts, 0, i % parts, 0)),
+            const((cut, LANES)), const((cut, LANES)), const((cut // 2, LANES)),
         ],
         out_shape=[
             sds((LENGTH, D), BF16), sds((LENGTH, D), F32), sds((LENGTH, D), BF16), sds((24 + split * tiles, LANES), F32),
-            sds((split, tiles, D, LANES), BF16), sds((split, D // LANES, hidden, LANES), BF16),
+            sds((cut, LANES), BF16), sds((cut, LANES), BF16), sds((cut // 2, LANES), BF16),
         ],
         scratch_shapes=[
             pltpu.VMEM((LENGTH, D), BF16),
@@ -870,33 +1043,40 @@
             pltpu.VMEM((LENGTH, D), BF16),
             *[pltpu.VMEM((LENGTH, D), F32)] * 3,
             pltpu.VMEM((D // LANES, LENGTH, LANES), F32),
-        ],
-        compiler_params=params,
+            pltpu.VMEM((chunks, D, piece), BF16),
+            pltpu.VMEM((chunks, 16, piece), BF16),
+            pltpu.VMEM((chunks, piece, D), BF16),
+            pltpu.VMEM((split, 2 * cut, LANES), BF16),
+            pltpu.VMEM((2, 2 * cut, LANES), BF16),
+            pltpu.VMEM((cut + cut // 2, LANES), BF16),
+            dma((3, chunks)), dma((4,)), dma((4,)),
+        ],
+        compiler_params=pltpu.CompilerParams(vmem_limit_bytes=VMEM_LIMIT, collective_id=2, has_side_effects=True),
         name="mlp",
         cost_estimate=pl.CostEstimate(flops=2 * 11_300_000_000, bytes_accessed=40_000_000, transcendentals=5_000_000),
-    )(res_ids, mid, cotangent, gain_two, bias_two, b_down, up_all, up_all, down_all)
-
-    gup = lax.psum_scatter(gup, "tensor", scatter_dimension=0, tiled=False)
-    gdown = lax.psum_scatter(gdown, "tensor", scatter_dimension=0, tiled=False)
-
-    gx, small_one, gwq, gwk, gwv, gwp = pl.pallas_call(
-        bwd_kernel,
+    )(res_ids, mid, cotangent, gain_two, bias_two, b_down, up_all, down_all)
+
+    links = bits("dp", lax.axis_size("dp"))
+    gx, small_one, gwq, gwk, gwv, gwp, gup, gdown = pl.pallas_call(
+        functools.partial(bwd_kernel, links),
         grid=(GROUPS, PER),
         in_specs=[
-            scalar, const((LENGTH, D)), row, row, const((LENGTH, D)), const((LENGTH, D)), *w_spec,
+            scalar, const((LENGTH, D)), row, row, anywhere, const((LENGTH, D)), *w_spec,
             const((3, 32, WIDE)), const((8, LANES)), const((PAIRS, LANES)), const((PAIRS, LANES)),
             const((LENGTH, PAIRS)), const((64, PAIRS)), blocked((WIDE, D), lambda g, h: (g, 0)),
             blocked((SPOTS, 8, 3 * WIDE), lambda g, h: (0, 0, g), True),
             per_head(1, 3, LENGTH, LANES), per_head(1, LENGTH, LANES), per_head(1, KEYS, LANES),
             per_head(1, KEYS, LANES), per_head(1, LENGTH, KEYS), per_head(1, LENGTH, LANES), att_spec,
+            anywhere, anywhere, anywhere,
         ],
         out_specs=[
             const((LENGTH, D)), const((208, LANES)),
             *[blocked((3, D, LANES), lambda g, h: (g, 0, 0)) for _ in range(3)],
-            blocked((6, WIDE, LANES), lambda g, h: (0, g, 0)),
+            blocked((6, WIDE, LANES), lambda g, h: (0, g, 0)), anywhere, anywhere,
         ],
         out_shape=[
             sds((LENGTH, D), F32), sds((208, LANES), F32), *[sds((6, D, LANES), BF16)] * 4,
+            sds((cut, LANES), BF16), sds((cut, LANES), BF16),
         ],
         scratch_shapes=[
             pltpu.VMEM((32, WIDE), F32),
@@ -908,20 +1088,22 @@
             pltpu.VMEM((3, SPOTS + 2 * SIDE, 8, WIDE), F32),
             pltpu.VMEM((LENGTH, 3 * WIDE), BF16),
             pltpu.VMEM((LENGTH, 3 * WIDE), F32),
-            pltpu.VMEM((LENGTH, D), F32),
-        ],
-        compiler_params=params,
+            pltpu.VMEM((cut, LANES), BF16), pltpu.VMEM((cut, LANES), BF16), pltpu.VMEM((cut // 2, LANES), BF16),
+            pltpu.VMEM((cut, LANES), BF16), pltpu.VMEM((cut, LANES), BF16), pltpu.VMEM((cut // 2, LANES), BF16),
+            dma((4,)), dma((2,)), dma((2, 2 * len(links) + 1)), dma((2, 2 * len(links) + 1)),
+        ],
+        compiler_params=pltpu.CompilerParams(vmem_limit_bytes=VMEM_LIMIT, collective_id=3, has_side_effects=True),
         name="attend_back",
         cost_estimate=pl.CostEstimate(flops=2 * 7_000_000_000, bytes_accessed=60_000_000, transcendentals=0),
     )(
         res_ids, xs, gain_one, bias_one, gm, gml, w_qkv, w_qkv, w_qkv, pw, ln, tall, cmp, jnp.asarray(select), jnp.asarray(np.pad(pick.T, ((0, 11), (0, 0))), BF16), w_proj,
-        field, xh, qx, kx, vx, probs, outs, att,
+        field, xh, qx, kx, vx, probs, outs, att, gup, gdown, gfar,
     )
 
-    flat = [a.reshape(-1, LANES) for a in (gwq, gwk, gwv, gwp, gup, gdown)]
+    flat = [a.reshape(-1, LANES) for a in (gwq, gwk, gwv, gwp)]
     sizes = {axis: lax.axis_size(axis) for axis in ("dp", "tensor")}
-    big, small = all_reduce(flat[:4], flat[4:], small_one, small, sizes)
-    outs = unpack(big.reshape(-1, D, LANES), small)
+    big, small = all_reduce(flat, [], small_one, small, sizes)
+    outs = unpack(*[a.reshape(-1, D, LANES) for a in (big, gup, gdown)], small)
     squares, (gain1, bias1, bp, gain2, bias2, bd, bu), (gb, gpw, pg, pb, rel) = outs[:4], outs[4:11], outs[11:]
 
     return (

time: 424 us -> 399 us (0.941)
  Pallas kernels: 398 us -> 372 us
    pallas_call x1, Pallas kernels: 135 us -> 84.4 us  [all_reduce(): pl.pallas_call(functools.partial(reduce_kernel, parts, pieces, links), in...]
    pallas_call x3, Pallas kernels: 170 us -> 195 us  [the longest x1 127 us: per_device(): pl.pallas_call(functools.partial(bwd_kernel, links), grid=(GROUPS, PER),...]
  transfers between devices with their start and end apart: 4 -> 2, of which waited for: 0 -> 0; matrix products, arithmetic and copies ran while one was open for 2% -> 2% of each run, Pallas kernels for 49% -> 24%
where the time goes in v3:
time: 399 us; the launch traced here: 398 us
  Pallas kernels  372 us (93%)
  between operations  14.9 us (4%)
  local copies, waits for them, and re-layouts  7.49 us (2%)
    pallas_call x1, Pallas kernels, per_device(): pl.pallas_call(functools.partial(bwd_kernel, links), grid=(GROUPS, PER),...  127 us
    pallas_call x1, Pallas kernels, per_device(): pl.pallas_call(fwd_kernel, grid=(GROUPS, PER), in_specs=[scalar, const((L...  93.5 us
    pallas_call x1, Pallas kernels, all_reduce(): pl.pallas_call(functools.partial(reduce_kernel, parts, pieces, links), in...  84.4 us
    pallas_call x1, Pallas kernels, per_device(): pl.pallas_call(functools.partial(mlp_kernel, parts), grid=(chunks,), in_s...  58.9 us
    pallas_call x1, Pallas kernels, unpack(): pl.pallas_call(unpack_kernel, grid=(D // LANES,), in_specs=[*[pl.BlockSpe...  9 us
  transfers between devices with their start and end apart: 2, of which 0 were waited for; matrix products, arithmetic and copies ran while one was open for 2% of the time, Pallas kernels for 24%

profile of v3, /device:TPU:0, one launch (start us, length us, event | category | flops | bytes accessed | tf_op | source)
XLA Modules:
  0.0 397.7 jit_solution(16617285312741087339)
XLA Ops:
  7.2 0.0 copy-start
  7.2 0.0 copy-start.4
  7.2 0.0 all-gather.7.cloned.1.call-start
  7.3 0.7 all-gather.7.cloned.1.call-update
  8.0 0.0 all-gather.5.cloned.1.call-start
  8.0 0.7 broadcast_in_dim.3
  8.7 0.0 copy-start.6
  8.7 1.1 pad_maximum_fusion
  9.8 0.0 all-gather.5.cloned.1.call-update
  10.6 0.6 reshape.64.bq_ref.bk_ref.bv_ref
  11.2 0.0 copy-done.6
  11.2 0.4 convolution_convert_fusion
  11.6 0.0 copy-start.10
  11.6 0.1 copy.45
  11.8 0.1 tile.10
  11.9 0.7 pad.19.tall_ref
  12.6 0.9 pad.20.mem_ref
  13.5 0.7 pad.17.pw_ref
  14.2 0.0 copy-done.9
  14.2 0.6 select_maximum_fusion.ln_ref
  14.8 93.5 %attend.1 = (f32[800,768]{1,0:T(8,128)}, bf16[800,768]{1,0:T(8,128)(2,1)}, f32[100,8,2304]{2,1,0:T(8,128)}, f32[8,3,800,128]{3,2,1,0:T(8,128)}, bf16[8,800,128]{...) custom-call(s32[1]{0:T(128)S(6)} %copy.48.res_ref, ...), custom_call_target="tpu_custom_call" | custom-call | flops 7000000000 | bytes 60000000 | tf_op jit(solution)/shard_map/attend/pallas_call | solution.py:986
  108.3 0.0 all-gather.7.cloned.1.call-done
  108.3 0.0 all-gather.5.cloned.1.call-done
  108.4 58.9 %mlp.1 = (bf16[800,768]{1,0:T(8,128)(2,1)}, f32[800,768]{1,0:T(8,128)}, bf16[800,768]{1,0:T(8,128)(2,1)}, f32[48,128]{1,0:T(8,128)}, bf16[4608,128]{1,0:T(8,128)...) custom-call(s32[1]{0:T(128)S(6)} %copy.48.res_ref, f32[800,768]{1,0:T(8,128)} %get-tuple-element.61.mid_ref, ...), custom_call_target="tpu_custom_call" | custom-call | flops 22599999488 | bytes 40000000 | tf_op jit(solution)/shard_map/mlp/pallas_call | solution.py:1028
  167.3 126.6 %attend_back.1 = (f32[800,768]{1,0:T(8,128)}, f32[208,128]{1,0:T(8,128)}, bf16[6,768,128]{2,1,0:T(8,128)(2,1)}, bf16[6,768,128]{2,1,0:T(8,128)(2,1)}, bf16[6,768...) custom-call(s32[1]{0:T(128)S(6)} %copy.48.res_ref, ...), custom_call_target="tpu_custom_call" | custom-call | flops 14000000000 | bytes 60000000 | tf_op jit(solution)/shard_map/attend_back/pallas_call | solution.py:1060
  293.9 84.4 %sum_all.1 = (bf16[18432,128]{1,0:T(8,128)(2,1)}, f32[256,128]{1,0:T(8,128)}) custom-call(bf16[4608,128]{1,0:T(8,128)(2,1)} %bitcast.14, bf16[4608,128]{1,0:T(8,128)(2,1)} %bitcast.15, bf16[4608,128]{1,0:T(8,128)(2,1)} %bitcast.16, bf16[4608,128]{1,0:T(8,128)(2,1)} %bitcast.17, f32[208,128]{1,0:T(8,128)} %get-tuple-element.82.refs_4_, ...), custom_call_target="tpu_custom_call" | custom-call | flops 10000000 | bytes 20000000 | tf_op jit(solution)/shard_map/sum_all/pallas_call | solution.py:851
  378.3 9.0 %unpack.1 = (f32[768,2304]{1,0:T(8,128)}, f32[768,768]{1,0:T(8,128)}, f32[768,768]{1,0:T(8,128)}, f32[768,768]{1,0:T(8,128)}, f32[768]{0:T(1024)}, /*index=5*/f3...) custom-call(bf16[24,768,128]{2,1,0:T(8,128)(2,1)} %bitcast.11, ...), custom_call_target="tpu_custom_call" | custom-call | bytes 22000000 | tf_op jit(solution)/shard_map/unpack/pallas_call | solution.py:903
  387.3 0.0 copy-done.3
  387.3 0.0 copy-start.2
  387.3 1.0 copy.49
  388.4 1.1 copy-done.2
  389.5 1.4 copy.50
  (14 shorter events, 0.1 us)
Async XLA Ops:
  7.2 4.0 copy-start
  7.2 1.5 copy-start.4
  7.2 101.1 %all-gather.7.cloned.1.call-start = ((), (), s32[]{:S(2)}) async-start(), calls=%async_computation.1 | async-start | bytes 5898240 | tf_op jit(solution)/shard_map/all_gather | solution.py:962
  8.0 100.4 %all-gather.5.cloned.1.call-start = ((), (), s32[]{:S(2)}) async-start(), calls=%async_computation | async-start | bytes 6021120 | tf_op jit(solution)/shard_map/all_gather | solution.py:961
  8.7 1.9 copy-start.8
  8.7 2.5 copy-start.6
  9.8 1.9 copy-start.7
  9.8 2.8 copy-start.5
  11.6 2.6 copy-start.9
  11.6 2.6 copy-start.10
  378.3 9.0 %copy-start.3 = (bf16[800,768]{1,0:T(8,128)(2,1)S(1)}, bf16[800,768]{1,0:T(8,128)(2,1)}, u32[]{:S(2)}) copy-start(bf16[800,768]{1,0:T(8,128)(2,1)} %get-tuple-element.122) | copy-start | bytes 3686404
  387.3 2.1 copy-start.2
  389.5 1.4 copy-start.1
Sparse Core Ops, SparseCore 0:
  9.6 40.1 all-gather.6
  51.4 38.0 all-gather.4

commit v4 on v3

--- a/solution.py
+++ b/solution.py
@@ -26,7 +26,6 @@
 TAPS = 27
 LANES = 128
 BAND = SIDE * FRAMES
-CHUNK = 160
 PAIRS = 384
 MASK_LANE = HEAD_DIM + OFFSETS
 EPS = 1e-6
@@ -34,8 +33,8 @@
 F32 = jnp.float32
 BF16 = jnp.bfloat16
 NEG = -1e30
-UP_TICKS = (0, 2, 3, 4, 5, 7, 9)
-DOWN_TICKS = (2, 4, 7, 8, 9, 10, 11, 14)
+UP_TICKS = (0, 3, 4, 5, 6, 8, 11)
+DOWN_TICKS = (3, 5, 7, 9, 10, 11, 12, 14)
 VMEM_LIMIT = 60 * 1024 * 1024
 
 
@@ -81,6 +80,20 @@
     return c * rstd, rstd
 
 
+def ones_matrix():
+    return jnp.where(lax.broadcasted_iota(jnp.int32, (LANES, LANES), 0) < HEAD_DIM, 1.0, 0.0).astype(BF16)
+
+
+def lane_mean(x, ones):
+    return nn(x.astype(BF16), ones) * (1 / HEAD_DIM)
+
+
+def fine_mean(x, ones):
+    high = x.astype(BF16)
+    low = (x - high.astype(F32)).astype(BF16)
+    return nn(jnp.concatenate([high, low], axis=1), jnp.concatenate([ones, ones])) * (1 / HEAD_DIM)
+
+
 def frame_shift(x, up):
     frame = lax.broadcasted_iota(jnp.int32, x.shape, 1)
     if up:
@@ -138,6 +151,8 @@
 
 
 def rows_at(r, size):
+    if isinstance(r, int):
+        return pl.ds(r * size, size)
     return pl.ds(pl.multiple_of(r * size, size), size)
 
 
@@ -262,12 +277,32 @@
 
 def fwd_kernel(
     res_ref, x_ref, gain_ref, bias_ref, bp_ref, wq_ref, wk_ref, wv_ref, bq_ref, bk_ref, bv_ref, pw_ref, ln_ref,
-    tall_ref, cmp_ref, sel_ref, marks_ref, code_ref, mem_ref, wp_ref,
-    mid_ref, xs_ref, field_ref, xh_ref, q_ref, k_ref, v_ref, p_ref, o_ref, att_ref,
-    n_s, fld_s, pool_s, q_s, acc_s,
+    tall_ref, cmp_ref, sel_ref, marks_ref, code_ref, mem_ref, wp_ref, up_any, bu_any, down_any,
+    mid_ref, xs_ref, field_ref, xh_ref, q_ref, k_ref, v_ref, p_ref, o_ref, att_ref, up_all, bu_all, down_all,
+    send_sem, recv_sem, n_s, fld_s, pool_s, q_s, acc_s,
 ):
     g, h = pl.program_id(0), pl.program_id(1)
     large = is_large(res_ref)
+    core, other = ("tensor", 1), ("tensor", 2)
+    shards = ((up_any, up_all), (bu_any, bu_all), (down_any, down_all))
+
+    def share(k, link, to):
+        src = shards[k][0] if to < 2 else shards[k][1].at[1]
+        return send(src, shards[k][1].at[to], send_sem.at[k, to], recv_sem.at[k, to], link)
+
+    @pl.when((g == 0) & (h == 0))
+    def _():
+        greet((core, other))
+        for k in range(3):
+            share(k, other, 1).start()
+            share(k, core, 0).start()
+
+    @pl.when((h == PER - 1) & (g == GROUPS - 1))
+    def _():
+        for k in range(3):
+            share(k, other, 1).wait()
+            share(k, core, 2).start()
+
 
     @pl.when((g == 0) & (h == 0))
     def _():
@@ -338,29 +373,33 @@
         lax.fori_loop(0, 3, branch, 0)
         lane = lane_of((BAND, LANES))
 
+        ones = ones_matrix()
+
         def norm(r, _):
             spots, rows = rows_at(r, SIDE), rows_at(r, BAND)
             bar = jnp.where(lane == MASK_LANE, NEG, 0.0) * (1.0 - alive(r, large, (BAND, LANES)))
+            heads = []
             for p in range(3):
-                tiles = [
+                heads += to_heads([
                     pool_s[spots, :, (3 * p + j) * LANES : (3 * p + j + 1) * LANES].reshape(BAND, LANES)
                     for j in range(3)
-                ]
-                for i, x in enumerate(to_heads(tiles)):
-                    mean = jnp.sum(x, axis=-1, keepdims=True) * (1 / HEAD_DIM)
-                    c = jnp.where(lane < HEAD_DIM, x - mean, 0.0)
-                    var = jnp.sum(c * c, axis=-1, keepdims=True) * (1 / HEAD_DIM)
-                    rstd = lax.rsqrt(var + EPS)
-                    xh = c * rstd
-                    xh_ref[i, p, rows, :] = jnp.where(lane == HEAD_DIM, rstd, xh)
-                    y = xh * ln_ref[p : p + 1, :] + ln_ref[3 + p : 4 + p, :]
-                    if p == 0:
-                        q_s[i, rows, :] = y
-                    elif p == 1:
-                        k_ref[i, rows, :] = (y + marks_ref[rows, :] + bar).astype(BF16)
-                    else:
-                        one = (lane == HEAD_DIM) | (lane == HEAD_DIM + 1)
-                        v_ref[i, rows, :] = jnp.where(one, 1.0, y).astype(BF16)
+                ])
+            x = jnp.concatenate(heads)
+            c = jnp.where(lane_of(x.shape) < HEAD_DIM, x - fine_mean(x, ones), 0.0)
+            rstd_all = lax.rsqrt(lane_mean(c * c, ones) + EPS)
+            xh_all = c * rstd_all
+            for k in range(3 * PER):
+                p, i = k // PER, k % PER
+                xh, rstd = xh_all[k * BAND : (k + 1) * BAND], rstd_all[k * BAND : (k + 1) * BAND]
+                xh_ref[i, p, rows, :] = jnp.where(lane == HEAD_DIM, rstd, xh)
+                y = xh * ln_ref[p : p + 1, :] + ln_ref[3 + p : 4 + p, :]
+                if p == 0:
+                    q_s[i, rows, :] = y
+                elif p == 1:
+                    k_ref[i, rows, :] = (y + marks_ref[rows, :] + bar).astype(BF16)
+                else:
+                    one = (lane == HEAD_DIM) | (lane == HEAD_DIM + 1)
+                    v_ref[i, rows, :] = jnp.where(one, 1.0, y).astype(BF16)
             return 0
 
         lax.fori_loop(0, SIDE, norm, 0)
@@ -376,31 +415,20 @@
                     m = jnp.where((lane_m == HEAD_DIM) | (lane_m == HEAD_DIM + 1), 1.0, m)
                 ref[i, LENGTH:KEYS, :] = m.astype(BF16)
 
-    def prepare(r, _):
-        rows = rows_at(r, CHUNK)
-        q = q_s[h, rows, :]
-        near = (nt(q.astype(BF16), tall_ref[...]) * sel_ref[rows, :]).astype(BF16)
-        lane = lane_of((CHUNK, LANES))
-        ext = q * SCALE + nn(near, cmp_ref[...])
-        q_ref[h, rows, :] = jnp.where(lane == MASK_LANE, 1.0, ext).astype(BF16)
-        return 0
-
-    lax.fori_loop(0, LENGTH // CHUNK, prepare, 0)
-
-    def attend(r, _):
-        rows = rows_at(r, CHUNK)
-        lane = lane_of((CHUNK, LANES))
-        s = nt(q_ref[h, rows, :], k_ref[h])
-        e = jnp.exp(s - jnp.max(s, axis=-1, keepdims=True)).astype(BF16)
-        p_ref[0, rows, :] = e
-        o = nn(e, v_ref[h])
-        total = o[:, HEAD_DIM : HEAD_DIM + 1]
-        o = jnp.where(lane < HEAD_DIM, o * (1.0 / total), 0.0)
-        o_ref[0, rows, :] = jnp.where(lane == HEAD_DIM, total, o)
-        q_s[h, rows, :] += o
-        return 0
-
-    lax.fori_loop(0, LENGTH // CHUNK, attend, 0)
+    q = q_s[h]
+    near = (nt(q.astype(BF16), tall_ref[...]) * sel_ref[...]).astype(BF16)
+    ext = q * SCALE + nn(near, cmp_ref[...])
+    q_ref[h] = jnp.where(lane_of((LENGTH, LANES)) == MASK_LANE, 1.0, ext).astype(BF16)
+
+    lane = lane_of((LENGTH, LANES))
+    scores = nt(q_ref[h], k_ref[h])
+    e = jnp.exp(scores - jnp.max(scores, axis=-1, keepdims=True)).astype(BF16)
+    p_ref[0] = e
+    o = nn(e, v_ref[h])
+    whole = o[:, HEAD_DIM : HEAD_DIM + 1]
+    o = jnp.where(lane < HEAD_DIM, o * (1.0 / whole), 0.0)
+    o_ref[0] = jnp.where(lane == HEAD_DIM, whole, o)
+    q_s[h] += o
 
     @pl.when(h == PER - 1)
     def _():
@@ -413,9 +441,15 @@
         lax.fori_loop(0, SIDE, join, 0)
         mid_ref[...] += nn(att_ref[...], wp_ref[...])
 
+    @pl.when((h == PER - 1) & (g == GROUPS - 1))
+    def _():
+        for k in range(3):
+            share(k, core, 0).wait()
+            share(k, core, 2).wait()
+
 
 def mlp_kernel(
-    parts, res_ref, mid_ref, cot_ref, gain_ref, bias_ref, bd_ref, up_all, down_all,
+    parts, res_ref, mid_ref, cot_ref, gain_ref, bias_ref, bd_ref, up_all, bu_all, down_all, up_any, bu_any, down_any,
     out_ref, gm_ref, gml_ref, small_ref, gup_ref, gdown_ref, gfar_ref,
     n_s, nt_s, go_s, y_s, gn_s, wide_s, stage_s, up_s, bu_s, down_s, grad_s, land_s, side_s, load_sem, send_sem, recv_sem,
 ):
@@ -429,13 +463,14 @@
         k = k // parts
         return (bit_of(*core) + 1 - k % 2) % 2 + 2 * ((bit_of(*other) + 1 - k // 2) % 2)
 
-    def loads(k):
-        t, c = slice_of(k), k % parts
+    def loads(k, own=False):
+        up, bu, down = (up_any, bu_any, down_any) if own else [a.at[2 - k // parts] for a in (up_all, bu_all, down_all)]
+        c = k % parts
         lanes = pl.ds(pl.multiple_of(c * width, LANES), width)
         return [
-            pltpu.make_async_copy(up_all.at[t, pl.ds(0, D), lanes], up_s.at[k], load_sem.at[0, k]),
-            pltpu.make_async_copy(up_all.at[t, pl.ds(D, 16), lanes], bu_s.at[k], load_sem.at[1, k]),
-            pltpu.make_async_copy(down_all.at[t, some(c * width, width)], down_s.at[k], load_sem.at[2, k]),
+            pltpu.make_async_copy(up.at[:, lanes], up_s.at[k], load_sem.at[0, k]),
+            pltpu.make_async_copy(bu.at[:, lanes], bu_s.at[k], load_sem.at[1, k]),
+            pltpu.make_async_copy(down.at[some(c * width, width)], down_s.at[k], load_sem.at[2, k]),
         ]
 
     def to_core(k):
@@ -451,7 +486,7 @@
     @pl.when(step == 0)
     def _():
         for k in range(parts * 4):
-            for copy in loads(k):
+            for copy in loads(k, k >= 3 * parts):
                 copy.start()
         greet((core, other, near))
 
@@ -486,8 +521,16 @@
         put_rows(small_ref, 12, total(sums))
         nt_s[...] = n_s[...].T
 
-    for copy in loads(step):
-        copy.wait()
+    @pl.when(step < 3 * parts)
+    def _():
+        for copy in loads(step):
+            copy.wait()
+
+    @pl.when(step >= 3 * parts)
+    def _():
+        for copy in loads(step, True):
+            copy.wait()
+
     pre = nn(n_s[...], up_s[step]) + bu_s[step].astype(F32)[0:1, :]
     cdf = 0.5 * (1.0 + lax.erf(pre * 0.7071067811865476))
     act = (pre * cdf).astype(BF16)
@@ -618,18 +661,11 @@
     do = do_s[h]
     o = o_ref[0]
     inv = 1.0 / o[:, HEAD_DIM : HEAD_DIM + 1]
-    delta = jnp.sum(do * o, axis=-1, keepdims=True) * inv
+    ones = ones_matrix()
+    delta = nn((do * o).astype(BF16), ones) * inv
     high = delta.astype(BF16).astype(F32)
     doe = jnp.where(lane == HEAD_DIM, -high, jnp.where(lane == HEAD_DIM + 1, high - delta, do * inv)).astype(BF16)
-    gq_s[:, 0:LANES] = doe
-
-    def scores(r, _):
-        rows = rows_at(r, CHUNK)
-        dp = nt(gq_s[rows, 0:LANES], v_ref[0])
-        ds_s[rows, :] = (p_ref[0, rows, :].astype(F32) * dp).astype(BF16)
-        return 0
-
-    lax.fori_loop(0, LENGTH // CHUNK, scores, 0)
+    ds_s[...] = (p_ref[0].astype(F32) * nt(doe, v_ref[0])).astype(BF16)
     dqe = nn(ds_s[...], k_ref[0])
     dk = tn(q_ref[0], ds_s[...]).T[:LENGTH]
     dv = tn(doe, p_ref[0]).T[:LENGTH]
@@ -642,8 +678,8 @@
         raw = xh_ref[0, p]
         rstd = raw[:, HEAD_DIM : HEAD_DIM + 1]
         gx = gy * ln_ref[p : p + 1, :]
-        m1 = jnp.sum(gx, axis=-1, keepdims=True) * (1 / HEAD_DIM)
-        m2 = jnp.sum(gx * raw, axis=-1, keepdims=True) * (1 / HEAD_DIM)
+        m1 = lane_mean(gx, ones)
+        m2 = lane_mean(gx * raw, ones)
         dpp_s[h, p] = (gx - m1 - raw * m2) * rstd
         small_ref[96 + p : 97 + p, :] += total(fold8(gy * raw))
         small_ref[99 + p : 100 + p, :] += total(fold8(gy))
@@ -665,36 +701,29 @@
 
             def pool(j, _):
                 lanes, own = tile_at(3 * p + j), tile_at(j)
-                for a in range(3):
-                    w = [
-                        jnp.broadcast_to(pw_ref[p, t : t + 1, own], (8, LANES))
-                        for t in range(9 * a, 9 * a + 9)
-                    ]
-
-                    def row(r, sums):
-                        sums = list(sums)
-                        x = [field_ref[r * SIDE + c, :, lanes] for c in range(SIDE)]
-                        acc = [None] * SIDE
-                        for c_in in range(SIDE):
-                            for b in range(3):
+                w = [jnp.broadcast_to(pw_ref[p, t : t + 1, own], (8, LANES)) for t in range(TAPS)]
+
+                def row(r, sums):
+                    sums = list(sums)
+                    x = [field_ref[r * SIDE + c, :, lanes] for c in range(SIDE)]
+                    acc = [None] * SIDE
+                    for c_in in range(SIDE):
+                        for b in range(3):
+                            for a in range(3):
                                 t = g_s[a, (r + 2 - b) * SIDE + c_in, :, own]
                                 for e in range(3):
-                                    c = c_in + e - 1
+                                    c, k = c_in + e - 1, 9 * a + 3 * b + e
                                     if 0 <= c < SIDE:
-                                        term = w[3 * b + e] * t
+                                        term = w[k] * t
                                         acc[c] = term if acc[c] is None else acc[c] + term
-                                        sums[3 * b + e] = sums[3 * b + e] + x[c] * t
-                        for c in range(SIDE):
-                            at = pl.ds(pl.multiple_of(r * BAND + c * 8, 8), 8)
-                            if a == 0:
-                                gin_s[at, lanes] = acc[c]
-                            else:
-                                gin_s[at, lanes] += acc[c]
-                        return tuple(sums)
-
-                    sums = lax.fori_loop(0, SIDE, row, tuple(jnp.zeros((8, LANES), F32) for _ in range(9)))
-                    for t in range(9):
-                        gpw_s[9 * a + t : 9 * a + t + 1, own] = total(sums[t])
+                                        sums[k] = sums[k] + x[c] * t
+                    for c in range(SIDE):
+                        gin_s[pl.ds(pl.multiple_of(r * BAND + c * 8, 8), 8), lanes] = acc[c]
+                    return tuple(sums)
+
+                sums = lax.fori_loop(0, SIDE, row, tuple(jnp.zeros((8, LANES), F32) for _ in range(TAPS)))
+                for t in range(TAPS):
+                    gpw_s[t : t + 1, own] = total(sums[t])
                 return 0
 
             lax.fori_loop(0, 3, pool, 0)
@@ -769,7 +798,7 @@
 def reduce_kernel(parts, pieces, links, *refs):
     n = len(pieces)
     ins, one, two, out, small = refs[:n], refs[n], refs[n + 1], refs[n + 2], refs[n + 3]
-    big, land, small_land, load_sem, send_sem, recv_sem, back_sem, home_sem, ssend_sem, srecv_sem = refs[n + 4 :]
+    big, land, small_land, load_sem, send_sem, recv_sem, own_sem, ssend_sem, srecv_sem = refs[n + 4 :]
     loads = [
         pltpu.make_async_copy(ref, big.at[pl.ds(first, rows)], load_sem.at[i])
         for i, (ref, (first, rows)) in enumerate(zip(ins, pieces))
@@ -781,84 +810,57 @@
     small[one.shape[0] :] = two[...]
     for copy in loads:
         copy.wait()
-
-    spans = [[(first, rows)] for first, rows, _ in parts]
-    for s in range(max(len(order) for _, _, order in parts)):
-        flying = []
-        for i, (first, rows, order) in enumerate(parts):
-            if s >= len(order):
-                continue
-            off, size = spans[i][-1]
-            half = size // 2
-            bit = bit_of(*order[s])
-            keep, give, at = off + bit * half, off + (1 - bit) * half, first + rows - size
-            if halvings(rows) <= s:
-                keep, give, half = off, off, size
-            copy = send(
-                big.at[pl.ds(pl.multiple_of(give, 16), half)], land.at[pl.ds(at, half)], send_sem.at[i, s], recv_sem.at[i, s], order[s]
-            )
-            copy.start()
-            flying.append((copy, keep, half, at))
-            spans[i].append((keep, half))
-        extra = None
-        if s < len(links):
-            extra = send(small, small_land.at[s], ssend_sem.at[s], srecv_sem.at[s], links[s])
-            extra.start()
-        for copy, keep, half, at in flying:
-            copy.wait()
-            add_rows(big, keep, land, at, half)
-        if extra is not None:
-            extra.wait()
-            small[...] += small_land[s]
-    for span in spans:
-        off, size = span[-1]
-        own = pl.ds(pl.multiple_of(off, 16), size)
-        out[own, :] = big[own, :]
-    depth = max(len(order) for _, _, order in parts)
-    for s in reversed(range(depth)):
-        flying = []
-        for i, (first, rows, order) in enumerate(parts):
-            if s >= min(len(order), halvings(rows)):
-                continue
-            off, size = spans[i][s + 1]
-            here = out.at[pl.ds(pl.multiple_of(off, 16), size)]
-            copy = send(here, here, back_sem.at[i, s], home_sem.at[i, s], order[s])
-            copy.start()
-            flying.append(copy)
-        for copy in flying:
-            copy.wait()
-
-
-def all_reduce(whole, over_dp, one, two, sizes):
+    chains = []
+    for i, (first, rows, order) in enumerate(parts):
+        here = pl.ds(first, rows)
+        chains.append(
+            chain(big.at[here], land.at[here], out.at[here], send_sem.at[i], recv_sem.at[i], own_sem.at[i], order)
+        )
+
+    def extra(s):
+        return send(small, small_land.at[s], ssend_sem.at[s], srecv_sem.at[s], links[s])
+
+    for k in range(max(len(c) for c in chains)):
+        for c in chains:
+            if k < len(c):
+                c[k]()
+        if 0 < k <= len(links):
+            extra(k - 1).wait()
+            small[...] += small_land[k - 1]
+        if k < len(links):
+            extra(k).start()
+
+
+def all_reduce(whole, one, two, sizes):
     dp, tensor = bits("dp", sizes["dp"]), bits("tensor", sizes["tensor"])
     links = tensor + dp
     small = sds((one.shape[0] + two.shape[0], LANES), F32)
     pieces, at = [], 0
-    for a in whole + over_dp:
+    for a in whole:
         pieces.append((at, a.shape[0]))
         at += a.shape[0]
-    cut = sum(a.shape[0] for a in whole)
     core, rest = tensor[:1], tensor[1:]
-    third = cut // 3
-    orders = (core + rest + dp, core + dp[:1] + dp[1:] + rest, core + dp[1:] + rest + dp[:1])
-    parts = [(k * third, third, order) for k, order in enumerate(orders)]
-    if over_dp:
-        half = (at - cut) // 2
-        parts += [(cut, half, dp), (cut + half, half, dp[1:] + dp[:1])]
-    assert all(len(order) <= halvings(rows) + 1 for _, rows, order in parts)
-    depth = max(len(order) for _, _, order in parts)
+    one_way, other_way = core + rest + dp, core + dp[:1] + rest + dp[1:]
+    far_ways = [core + dp[1:2] + rest + dp[:1] + dp[2:], core + dp[1:2] + dp[:1] + rest + dp[2:]]
+    ways = [one_way, other_way, far_ways[0], one_way, other_way, far_ways[1]]
+    count = next(n for n in (12, 6, 3) if len(links) <= halvings(at // n) + 1)
+    orders = (ways + ways)[:count]
+    share = at // len(orders)
+    parts = [(k * share, share, order) for k, order in enumerate(orders)]
+    assert at % len(orders) == 0 and all(len(order) <= halvings(rows) + 1 for _, rows, order in parts)
     dma = pltpu.SemaphoreType.DMA
+    stages = 2 * len(links)
     return pl.pallas_call(
         functools.partial(reduce_kernel, parts, pieces, links),
         in_specs=[pl.BlockSpec(memory_space=pl.ANY)] * len(pieces) + [pl.BlockSpec(memory_space=pltpu.VMEM)] * 2,
         out_specs=[pl.BlockSpec(memory_space=pltpu.VMEM)] * 2,
-        out_shape=[sds((at, LANES), BF16), sds(small.shape, F32)],
+        out_shape=[sds((at, LANES), BF16), small],
         scratch_shapes=[
             pltpu.VMEM((at, LANES), BF16),
             pltpu.VMEM((at, LANES), BF16),
             pltpu.VMEM((len(links), *small.shape), F32),
             dma((len(pieces),)),
-            dma((len(parts), depth)), dma((len(parts), depth)), dma((len(parts), depth)), dma((len(parts), depth)),
+            dma((len(parts), stages)), dma((len(parts), stages)), dma((len(parts),)),
             dma((len(links),)), dma((len(links),)),
         ],
         compiler_params=pltpu.CompilerParams(
@@ -866,7 +868,7 @@
         ),
         name="sum_all",
         cost_estimate=pl.CostEstimate(flops=10_000_000, bytes_accessed=20_000_000, transcendentals=0),
-    )(*whole, *over_dp, one, two)
+    )(*whole, one, two)
 
 
 def unpack_kernel(big_ref, up_ref, down_ref, small_ref, *outs):
@@ -958,8 +960,8 @@
 ):
     split = lax.axis_size("tensor")
     pick, squeeze, select, marks, code = position_tables()
-    up_all = lax.all_gather(jnp.concatenate([w_up, jnp.broadcast_to(b_up, (16, b_up.shape[0]))]), "tensor")
-    down_all = lax.all_gather(w_down, "tensor")
+    assert split == 4
+    b_rows = jnp.broadcast_to(b_up, (16, b_up.shape[0]))
     pw = jnp.pad(jnp.tile(pool_weight, (1, 1, PER)), ((0, 0), (0, 5), (0, 0)))
     ln = jnp.pad(jnp.concatenate([pool_gain, pool_bias]), ((0, 2), (0, LANES - HEAD_DIM)))
     tall = jnp.dot(pick, rel_table, precision=lax.Precision.HIGHEST)
@@ -968,7 +970,8 @@
     mem = jnp.pad(memory, ((0, 0), (0, KEYS - LENGTH - MEM), (0, 0)))
     bq = b_qkv.reshape(1, -1)
 
-    params = pltpu.CompilerParams(vmem_limit_bytes=VMEM_LIMIT)
+    dma = pltpu.SemaphoreType.DMA
+    anywhere = pl.BlockSpec(memory_space=pl.ANY)
     w_spec = [blocked((D, WIDE), lambda g, h, p=p: (0, GROUPS * p + g)) for p in range(3)]
     b_spec = [blocked((1, WIDE), lambda g, h, p=p: (0, GROUPS * p + g)) for p in range(3)]
 
@@ -983,7 +986,7 @@
 
     field_spec = blocked((SPOTS, 8, 3 * WIDE), lambda g, h: (0, 0, g))
     att_spec = blocked((LENGTH, WIDE), lambda g, h: (0, g))
-    mid, xs, field, xh, qx, kx, vx, probs, outs, att = pl.pallas_call(
+    mid, xs, field, xh, qx, kx, vx, probs, outs, att, up_all, bu_all, down_all = pl.pallas_call(
         fwd_kernel,
         grid=(GROUPS, PER),
         in_specs=[
@@ -991,31 +994,33 @@
             const((3, 32, WIDE)), const((8, LANES)), const((PAIRS, LANES)), const((PAIRS, LANES)),
             const((LENGTH, PAIRS)), const((LENGTH, LANES)), const((KEYS - LENGTH, LANES)),
             blocked((2, KEYS - LENGTH, WIDE), lambda g, h: (0, 0, g)),
-            blocked((WIDE, D), lambda g, h: (g, 0)),
+            blocked((WIDE, D), lambda g, h: (g, 0)), anywhere, anywhere, anywhere,
         ],
         out_specs=[
             const((LENGTH, D)), const((LENGTH, D)), field_spec, per_group(PER, 3, LENGTH, LANES), per_group(PER, LENGTH, LANES),
             per_group(PER, KEYS, LANES), per_group(PER, KEYS, LANES), per_head(1, LENGTH, KEYS),
-            per_head(1, LENGTH, LANES), att_spec,
+            per_head(1, LENGTH, LANES), att_spec, anywhere, anywhere, anywhere,
         ],
         out_shape=[
             sds((LENGTH, D), F32), sds((LENGTH, D), BF16), sds((SPOTS, 8, 3 * D), F32), sds((HEADS, 3, LENGTH, LANES), F32),
             sds((HEADS, LENGTH, LANES), BF16), sds((HEADS, KEYS, LANES), BF16), sds((HEADS, KEYS, LANES), BF16),
             sds((HEADS, LENGTH, KEYS), BF16), sds((HEADS, LENGTH, LANES), F32), sds((LENGTH, D), BF16),
+            *[sds((split - 1, *a.shape), BF16) for a in (w_up, b_rows, w_down)],
         ],
         scratch_shapes=[
+            dma((3, 3)), dma((3, 3)),
             pltpu.VMEM((LENGTH, D), BF16),
             pltpu.VMEM((3, SPOTS + 2 * SIDE, 8, WIDE), F32),
             pltpu.VMEM((SPOTS, 8, 3 * WIDE), F32),
             pltpu.VMEM((PER, LENGTH, LANES), F32),
             pltpu.VMEM((D // LANES, LENGTH, LANES), F32),
         ],
-        compiler_params=params,
+        compiler_params=pltpu.CompilerParams(vmem_limit_bytes=VMEM_LIMIT, collective_id=4, has_side_effects=True),
         name="attend",
         cost_estimate=pl.CostEstimate(flops=2 * 3_500_000_000, bytes_accessed=60_000_000, transcendentals=6_500_000),
     )(
         res_ids, inputs, gain_one, bias_one, b_proj, w_qkv, w_qkv, w_qkv, bq, bq, bq, pw, ln,
-        tall, cmp, jnp.asarray(select), jnp.asarray(marks), jnp.asarray(code), mem, w_proj,
+        tall, cmp, jnp.asarray(select), jnp.asarray(marks), jnp.asarray(code), mem, w_proj, w_up, b_rows, w_down,
     )
 
     hidden = w_up.shape[1]
@@ -1023,12 +1028,10 @@
     parts = hidden // piece
     tiles = hidden // LANES
     chunks, cut = split * parts, D // LANES * D
-    dma = pltpu.SemaphoreType.DMA
-    anywhere = pl.BlockSpec(memory_space=pl.ANY)
     out, gm, gml, small, gup, gdown, gfar = pl.pallas_call(
         functools.partial(mlp_kernel, parts),
         grid=(chunks,),
-        in_specs=[scalar, const((LENGTH, D)), const((LENGTH, D)), row, row, row, anywhere, anywhere],
+        in_specs=[scalar, const((LENGTH, D)), const((LENGTH, D)), row, row, row, *[anywhere] * 6],
         out_specs=[
             const((LENGTH, D)), const((LENGTH, D)), const((LENGTH, D)), const((24 + split * tiles, LANES)),
             const((cut, LANES)), const((cut, LANES)), const((cut // 2, LANES)),
@@ -1054,7 +1057,7 @@
         compiler_params=pltpu.CompilerParams(vmem_limit_bytes=VMEM_LIMIT, collective_id=2, has_side_effects=True),
         name="mlp",
         cost_estimate=pl.CostEstimate(flops=2 * 11_300_000_000, bytes_accessed=40_000_000, transcendentals=5_000_000),
-    )(res_ids, mid, cotangent, gain_two, bias_two, b_down, up_all, down_all)
+    )(res_ids, mid, cotangent, gain_two, bias_two, b_down, up_all, bu_all, down_all, w_up, b_rows, w_down)
 
     links = bits("dp", lax.axis_size("dp"))
     gx, small_one, gwq, gwk, gwv, gwp, gup, gdown = pl.pallas_call(
@@ -1102,7 +1105,7 @@
 
     flat = [a.reshape(-1, LANES) for a in (gwq, gwk, gwv, gwp)]
     sizes = {axis: lax.axis_size(axis) for axis in ("dp", "tensor")}
-    big, small = all_reduce(flat, [], small_one, small, sizes)
+    big, small = all_reduce(flat, small_one, small, sizes)
     outs = unpack(*[a.reshape(-1, D, LANES) for a in (big, gup, gdown)], small)
     squares, (gain1, bias1, bp, gain2, bias2, bd, bu), (gb, gpw, pg, pb, rel) = outs[:4], outs[4:11], outs[11:]
 

time: 399 us -> 323 us (0.81)
  Pallas kernels: 372 us -> 309 us
  between operations: 14.9 us -> 1.47 us
    pallas_call x1, Pallas kernels: 93.5 us -> 68.6 us  [per_device(): pl.pallas_call(fwd_kernel, grid=(GROUPS, PER), in_specs=[scalar, const((L...]
    pallas_call x1, Pallas kernels: 127 us -> 106 us  [per_device(): pl.pallas_call(functools.partial(bwd_kernel, links), grid=(GROUPS, PER),...]
    pallas_call x1, Pallas kernels: 84.4 us -> 69.7 us  [all_reduce(): pl.pallas_call(functools.partial(reduce_kernel, parts, pieces, links), in...]
  transfers between devices with their start and end apart: 2 -> 0, of which waited for: 0 -> 0; matrix products, arithmetic and copies ran while one was open for 2% -> 0% of each run, Pallas kernels for 24% -> 0%
where the time goes in v4:
time: 323 us
  Pallas kernels  309 us (96%)
  local copies, waits for them, and re-layouts  9.5 us (3%)
    pallas_call x1, Pallas kernels, per_device(): pl.pallas_call(functools.partial(bwd_kernel, links), grid=(GROUPS, PER),...  106 us
    pallas_call x1, Pallas kernels, all_reduce(): pl.pallas_call(functools.partial(reduce_kernel, parts, pieces, links), in...  69.7 us
    pallas_call x1, Pallas kernels, per_device(): pl.pallas_call(fwd_kernel, grid=(GROUPS, PER), in_specs=[scalar, const((L...  68.6 us
    pallas_call x1, Pallas kernels, per_device(): pl.pallas_call(functools.partial(mlp_kernel, parts), grid=(chunks,), in_s...  56.4 us
    pallas_call x1, Pallas kernels, unpack(): pl.pallas_call(unpack_kernel, grid=(D // LANES,), in_specs=[*[pl.BlockSpe...  9 us

profile of v4, /device:TPU:0, one launch (start us, length us, event | category | flops | bytes accessed | tf_op | source)
XLA Modules:
  0.0 322.9 jit_solution(11431830084044976551)
XLA Ops:
  0.7 0.0 copy-start
  0.7 0.0 copy-start.4
  1.4 1.3 select_maximum_fusion.ln_ref
  2.7 1.3 reshape.64.bq_ref.bk_ref.bv_ref
  4.0 1.3 broadcast_in_dim.3.bu_any
  5.3 0.0 copy-done
  5.3 1.3 convolution_convert_fusion
  6.6 0.1 copy.45
  6.8 0.7 pad.19.tall_ref
  7.4 0.8 tile.4
  8.3 0.1 tile.10
  8.4 0.7 pad.17.pw_ref
  9.1 0.0 copy-done.4
  9.1 0.9 pad.20.mem_ref
  10.0 68.6 %attend.1 = (f32[800,768]{1,0:T(8,128)}, bf16[800,768]{1,0:T(8,128)(2,1)}, f32[100,8,2304]{2,1,0:T(8,128)}, f32[8,3,800,128]{3,2,1,0:T(8,128)}, bf16[8,800,128]{...) custom-call(s32[1]{0:T(128)S(6)} %copy.48.res_ref, ...), custom_call_target="tpu_custom_call" | custom-call | flops 7000000000 | bytes 60000000 | tf_op jit(solution)/shard_map/attend/pallas_call | solution.py:989
  78.6 56.4 %mlp.1 = (bf16[800,768]{1,0:T(8,128)(2,1)}, f32[800,768]{1,0:T(8,128)}, bf16[800,768]{1,0:T(8,128)(2,1)}, f32[48,128]{1,0:T(8,128)}, bf16[4608,128]{1,0:T(8,128)...) custom-call(s32[1]{0:T(128)S(6)} %copy.48.res_ref, f32[800,768]{1,0:T(8,128)} %get-tuple-element.64.mid_ref, ...), custom_call_target="tpu_custom_call" | custom-call | flops 22599999488 | bytes 40000000 | tf_op jit(solution)/shard_map/mlp/pallas_call | solution.py:1031
  135.0 105.7 %attend_back.1 = (f32[800,768]{1,0:T(8,128)}, f32[208,128]{1,0:T(8,128)}, bf16[6,768,128]{2,1,0:T(8,128)(2,1)}, bf16[6,768,128]{2,1,0:T(8,128)(2,1)}, bf16[6,768...) custom-call(s32[1]{0:T(128)S(6)} %copy.48.res_ref, ...), custom_call_target="tpu_custom_call" | custom-call | flops 14000000000 | bytes 60000000 | tf_op jit(solution)/shard_map/attend_back/pallas_call | solution.py:1063
  240.7 69.7 %sum_all.1 = (bf16[18432,128]{1,0:T(8,128)(2,1)}, f32[256,128]{1,0:T(8,128)}) custom-call(bf16[4608,128]{1,0:T(8,128)(2,1)} %bitcast.12, bf16[4608,128]{1,0:T(8,128)(2,1)} %bitcast.13, bf16[4608,128]{1,0:T(8,128)(2,1)} %bitcast.14, bf16[4608,128]{1,0:T(8,128)(2,1)} %bitcast.15, f32[208,128]{1,0:T(8,128)} %get-tuple-element.88.refs_4_, ...), custom_call_target="tpu_custom_call" | custom-call | flops 10000000 | bytes 20000000 | tf_op jit(solution)/shard_map/sum_all/pallas_call | solution.py:853
  310.3 0.0 copy-start.3
  310.4 9.0 %unpack.1 = (f32[768,2304]{1,0:T(8,128)}, f32[768,768]{1,0:T(8,128)}, f32[768,768]{1,0:T(8,128)}, f32[768,768]{1,0:T(8,128)}, f32[768]{0:T(1024)}, /*index=5*/f3...) custom-call(bf16[24,768,128]{2,1,0:T(8,128)(2,1)} %bitcast.9, ...), custom_call_target="tpu_custom_call" | custom-call | bytes 22000000 | tf_op jit(solution)/shard_map/unpack/pallas_call | solution.py:905
  319.4 0.0 copy-start.2
  319.4 0.0 copy-done.3
  319.4 0.0 copy-start.1
  319.4 1.0 copy.49
  320.4 1.1 copy-done.2
  321.5 1.4 copy.50
  322.9 0.0 copy-done.1
Async XLA Ops:
  0.7 4.6 %copy-start = (f32[53,96]{1,0:T(8,128)S(1)}, f32[53,96]{1,0:T(8,128)}, u32[]{:S(2)}) copy-start(f32[53,96]{1,0:T(8,128)} %param.36) | copy-start | bytes 61060
  0.7 8.4 %copy-start.4 = (bf16[2,200,768]{2,1,0:T(8,128)(2,1)S(1)}, bf16[2,200,768]{2,1,0:T(8,128)(2,1)}, u32[]{:S(2)}) copy-start(bf16[2,200,768]{2,1,0:T(8,128)(2,1)} %param.28) | copy-start | bytes 1843204
  310.3 9.0 %copy-start.3 = (bf16[800,768]{1,0:T(8,128)(2,1)S(1)}, bf16[800,768]{1,0:T(8,128)(2,1)}, u32[]{:S(2)}) copy-start(bf16[800,768]{1,0:T(8,128)(2,1)} %get-tuple-element.128) | copy-start | bytes 3686404
  319.4 2.1 copy-start.2
  319.4 3.6 %copy-start.1 = (f32[53,96]{1,0:T(8,128)S(1)}, f32[53,96]{1,0:T(8,128)}, u32[]{:S(2)}) copy-start(f32[53,96]{1,0:T(8,128)} %param.36) | copy-start | bytes 61060

commit v5 on v4

--- a/solution.py
+++ b/solution.py
@@ -35,6 +35,7 @@
 NEG = -1e30
 UP_TICKS = (0, 3, 4, 5, 6, 8, 11)
 DOWN_TICKS = (3, 5, 7, 9, 10, 11, 12, 14)
+FIRST_TICKS = (7, 8, 10, 11, 12, 14)
 VMEM_LIMIT = 60 * 1024 * 1024
 
 
@@ -205,49 +206,57 @@
     lax.fori_loop(0, rows // block, add, 0)
 
 
-def chain(work, land, out, send_sem, recv_sem, own_sem, order, merge=None):
-    rows, count = work.shape[0], halvings(work.shape[0])
-
-    def span(s):
-        off, size = 0, rows
-        for k in range(min(s, count)):
-            size //= 2
-            off = off + bit_of(*order[k]) * size
-        return off, size
+def span(rows, order, s):
+    off, size = 0, rows
+    for k in range(min(s, halvings(rows))):
+        size //= 2
+        off = off + bit_of(*order[k]) * size
+    return off, size
+
+
+def landing(rows, count):
+    return rows + max(0, count - halvings(rows) - 1) * (rows >> halvings(rows))
+
+
+def chain(work, land, out, send_sem, recv_sem, own_sem, order, merge=None, own=None):
+    rows = (work if own is None else out).shape[0]
+    count = halvings(rows)
 
     def halve(s, k):
-        off, size = span(s)
+        off, size = span(rows, order, s)
         half, bit, at = size // 2, bit_of(*order[s]), rows - size
         keep, give = off + bit * half, off + (1 - bit) * half
         if s >= count:
-            keep, give, half = off, off, size
+            keep, give, half, at = off, off, size, rows - size + (s - count) * size
         copy = send(work.at[some(give, half)], land.at[some(at, half)], send_sem.at[k], recv_sem.at[k], order[s])
         return copy, (work, keep, land, at, half)
 
     def join(k):
-        ref, landing, link = merge
-        return send(ref, landing, send_sem.at[k], recv_sem.at[k], link), (work, span(1)[0], landing, 0, ref.shape[0])
+        ref, there, link = merge
+        keep = span(rows, order, 1)[0]
+        return send(ref, there, send_sem.at[k], recv_sem.at[k], link), (work, keep, there, 0, ref.shape[0])
 
     def double(s, k):
-        off, size = span(s + 1)
+        off, size = span(rows, order, s + 1)
         here = out.at[some(off, size)]
         return send(here, here, send_sem.at[k], recv_sem.at[k], order[s]), None
 
-    def own():
-        off, size = span(len(order))
-        copy = pltpu.make_async_copy(work.at[some(off, size)], out.at[some(off, size)], own_sem)
-        copy.start()
-        copy.wait()
-
-    plans = [functools.partial(halve, s) for s in range(len(order))]
+    plans = []
+    if own is None:
+        plans = [functools.partial(halve, s) for s in range(len(order))]
     if merge is not None:
         plans.insert(1, join)
     gather = len(plans)
-    plans += [functools.partial(double, s) for s in reversed(range(min(len(order), count)))]
+    if out is not None:
+        plans += [functools.partial(double, s) for s in reversed(range(min(len(order), count)))]
 
     def start(k):
         if k == gather:
-            own()
+            off, size = span(rows, order, len(order))
+            mine = work.at[some(off, size)] if own is None else own
+            copy = pltpu.make_async_copy(mine, out.at[some(off, size)], own_sem)
+            copy.start()
+            copy.wait()
         plans[k](k)[0].start()
 
     def finish(k):
@@ -449,29 +458,23 @@
 
 
 def mlp_kernel(
-    parts, res_ref, mid_ref, cot_ref, gain_ref, bias_ref, bd_ref, up_all, bu_all, down_all, up_any, bu_any, down_any,
+    res_ref, mid_ref, cot_ref, gain_ref, bias_ref, bd_ref, up_all, bu_all, down_all, up_any, bu_any, down_any,
     out_ref, gm_ref, gml_ref, small_ref, gup_ref, gdown_ref, gfar_ref,
     n_s, nt_s, go_s, y_s, gn_s, wide_s, stage_s, up_s, bu_s, down_s, grad_s, land_s, side_s, load_sem, send_sem, recv_sem,
 ):
     step = pl.program_id(0)
     large = is_large(res_ref)
-    tiles, width = D // LANES, up_s.shape[2]
+    tiles = D // LANES
     cut, half = tiles * D, tiles * D // 2
     core, other, near = ("tensor", 1), ("tensor", 2), ("dp", 1)
 
     def slice_of(k):
-        k = k // parts
         return (bit_of(*core) + 1 - k % 2) % 2 + 2 * ((bit_of(*other) + 1 - k // 2) % 2)
 
-    def loads(k, own=False):
-        up, bu, down = (up_any, bu_any, down_any) if own else [a.at[2 - k // parts] for a in (up_all, bu_all, down_all)]
-        c = k % parts
-        lanes = pl.ds(pl.multiple_of(c * width, LANES), width)
-        return [
-            pltpu.make_async_copy(up.at[:, lanes], up_s.at[k], load_sem.at[0, k]),
-            pltpu.make_async_copy(bu.at[:, lanes], bu_s.at[k], load_sem.at[1, k]),
-            pltpu.make_async_copy(down.at[some(c * width, width)], down_s.at[k], load_sem.at[2, k]),
-        ]
+    def loads(k):
+        up, bu, down = (up_any, bu_any, down_any) if k == 3 else [a.at[2 - k] for a in (up_all, bu_all, down_all)]
+        pairs = ((up, up_s), (bu, bu_s), (down, down_s))
+        return [pltpu.make_async_copy(src, dst.at[k % 2], load_sem.at[n, k]) for n, (src, dst) in enumerate(pairs)]
 
     def to_core(k):
         return send(grad_s.at[2 * k], land_s.at[k], send_sem.at[k], recv_sem.at[k], core)
@@ -485,12 +488,11 @@
 
     @pl.when(step == 0)
     def _():
-        for k in range(parts * 4):
-            for copy in loads(k, k >= 3 * parts):
-                copy.start()
+        for copy in loads(0):
+            copy.start()
         greet((core, other, near))
 
-    @pl.when(step == 2 * parts)
+    @pl.when(step == 2)
     def _():
         to_core(0).wait()
         add_rows(grad_s.at[1], 0, land_s.at[0], 0, 2 * cut)
@@ -499,7 +501,7 @@
 
     for k in range(2):
 
-        @pl.when(step == (2 * k + 1) * parts)
+        @pl.when(step == 2 * k + 1)
         def _():
             to_core(k).start()
 
@@ -521,33 +523,33 @@
         put_rows(small_ref, 12, total(sums))
         nt_s[...] = n_s[...].T
 
-    @pl.when(step < 3 * parts)
-    def _():
-        for copy in loads(step):
-            copy.wait()
-
-    @pl.when(step >= 3 * parts)
-    def _():
-        for copy in loads(step, True):
-            copy.wait()
-
-    pre = nn(n_s[...], up_s[step]) + bu_s[step].astype(F32)[0:1, :]
+    for k in range(4):
+
+        @pl.when(step == k)
+        def _():
+            if k < 3:
+                for copy in loads(k + 1):
+                    copy.start()
+            for copy in loads(k):
+                copy.wait()
+
+    slot = step % 2
+    pre = nn(n_s[...], up_s[slot]) + bu_s[slot].astype(F32)[0:1, :]
     cdf = 0.5 * (1.0 + lax.erf(pre * 0.7071067811865476))
     act = (pre * cdf).astype(BF16)
     slope = cdf + pre * jnp.exp(pre * pre * -0.5) * 0.3989422804014327
-    ga = nt(go_s[...], down_s[step])
+    ga = nt(go_s[...], down_s[slot])
     gh = ga * slope
-    own, part = step // parts, step % parts
-    put_rows(small_ref, 24 + slice_of(step) * tiles + part * (width // LANES), total(fold8(gh)))
+    put_rows(small_ref, 24 + slice_of(step) * tiles, total(fold8(gh)))
     ghl = gh.astype(BF16)
     value = tn(act, go_s[...]).astype(BF16)
     for j in range(tiles):
-        grad_s[own, some(cut + j * D + part * width, width), :] = value[:, j * LANES : (j + 1) * LANES]
+        grad_s[step, cut + j * D : cut + (j + 1) * D, :] = value[:, j * LANES : (j + 1) * LANES]
     value = nn(nt_s[...], ghl).astype(BF16)
-    for j in range(width // LANES):
-        grad_s[own, some((part * (width // LANES) + j) * D, D), :] = value[:, j * LANES : (j + 1) * LANES]
-    y = nn(act, down_s[step])
-    gn = nt(ghl, up_s[step])
+    for j in range(tiles):
+        grad_s[step, j * D : (j + 1) * D, :] = value[:, j * LANES : (j + 1) * LANES]
+    y = nn(act, down_s[slot])
+    gn = nt(ghl, up_s[slot])
 
     @pl.when(step == 0)
     def _():
@@ -594,12 +596,12 @@
 
 
 def bwd_kernel(
-    order, res_ref, x_ref, gain_ref, bias_ref, gm_any, gml_ref, wq_ref, wk_ref, wv_ref, pw_ref, ln_ref,
+    order, first_orders, res_ref, x_ref, gain_ref, bias_ref, gm_any, gml_ref, wq_ref, wk_ref, wv_ref, pw_ref, ln_ref,
     tall_ref, cmp_ref, sel_ref, pick_ref, wp_ref, field_ref, xh_ref, q_ref, k_ref, v_ref, p_ref, o_ref, att_ref,
     gup_any, gdown_any, gfar_any,
-    gx_ref, small_ref, gwq_ref, gwk_ref, gwv_ref, gwp_ref, gup_out, gdown_out,
+    gx_ref, small_ref, first_ref, last_ref, gup_out, gdown_out,
     gpw_s, gtall_s, n_s, do_s, ds_s, dpp_s, g_s, gq_s, gin_s,
-    up_s, down_s, far_s, up_land, down_land, far_land, load_sem, own_sem, send_sem, recv_sem,
+    up_s, down_s, far_s, up_land, down_land, far_land, first_s, first_land, load_sem, own_sem, send_sem, recv_sem,
 ):
     g, h = pl.program_id(0), pl.program_id(1)
     large = is_large(res_ref)
@@ -607,7 +609,25 @@
     side = (far_s, far_land, ("tensor", 2))
     down_steps = chain(down_s, down_land, gdown_out, send_sem.at[1], recv_sem.at[1], own_sem.at[1], order, side)
 
+    share, size = first_s.shape[0] // len(first_orders), first_ref.shape[0] // len(first_orders)
+    first_steps = [
+        chain(
+            first_s.at[pl.ds(c * share, share)], first_land.at[c], None, send_sem.at[2 + c], recv_sem.at[2 + c], None, links
+        )
+        for c, links in enumerate(first_orders)
+    ]
+
+    def store(at, value):
+        value = value.astype(BF16)
+        for ref, group in ((first_s, 0), (last_ref, 1)):
+
+            @pl.when(g == group)
+            def _():
+                ref[at : at + value.shape[0], :] = value
+
     def travel(tick):
+        for steps in first_steps:
+            at_ticks(tick, FIRST_TICKS, steps)
         at_ticks(tick, UP_TICKS, up_steps)
         at_ticks(tick, DOWN_TICKS, down_steps)
 
@@ -619,7 +639,7 @@
         ]
         for copy in loads:
             copy.start()
-        greet((("tensor", 2), *order))
+        greet((("tensor", 1), ("tensor", 2), *order))
         for copy in loads:
             copy.wait()
 
@@ -655,7 +675,7 @@
         lax.fori_loop(0, SIDE, split, 0)
         gw = tn(att_ref[...], gml_ref[...])
         for j in range(D // LANES):
-            gwp_ref[j] = gw[:, j * LANES : (j + 1) * LANES].astype(BF16)
+            store(9 * D + j * WIDE, gw[:, j * LANES : (j + 1) * LANES])
 
     lane = lane_of((LENGTH, LANES))
     do = do_s[h]
@@ -748,11 +768,11 @@
             gm_load.start()
 
         gn = None
-        for p, (w, gw) in enumerate(((wq_ref, gwq_ref), (wk_ref, gwk_ref), (wv_ref, gwv_ref))):
+        for p, w in enumerate((wq_ref, wk_ref, wv_ref)):
             piece = gq_s[:, p * WIDE : (p + 1) * WIDE]
             value = tn(n_s[...], piece)
             for j in range(WIDE // LANES):
-                gw[j] = value[:, j * LANES : (j + 1) * LANES].astype(BF16)
+                store((3 * p + j) * D, value[:, j * LANES : (j + 1) * LANES])
             term = nt(piece, w[...])
             gn = term if gn is None else gn + term
 
@@ -793,15 +813,15 @@
             rel = term if rel is None else rel + term
         small_ref[104:168, :] = rel
         travel(2 * (PER + 3))
-
-
-def reduce_kernel(parts, pieces, links, *refs):
-    n = len(pieces)
-    ins, one, two, out, small = refs[:n], refs[n], refs[n + 1], refs[n + 2], refs[n + 3]
-    big, land, small_land, load_sem, send_sem, recv_sem, own_sem, ssend_sem, srecv_sem = refs[n + 4 :]
+        for c, links in enumerate(first_orders):
+            off, _ = span(share, links, len(links))
+            first_ref[c * size : (c + 1) * size, :] = first_s[some(c * share + off, size), :]
+
+
+def reduce_kernel(parts, first_orders, links, first_any, last_any, one, two, first_out, out, small, *scratch):
+    big, land, own_s, small_land, load_sem, send_sem, recv_sem, own_sem, ssend_sem, srecv_sem = scratch
     loads = [
-        pltpu.make_async_copy(ref, big.at[pl.ds(first, rows)], load_sem.at[i])
-        for i, (ref, (first, rows)) in enumerate(zip(ins, pieces))
+        pltpu.make_async_copy(src, dst, load_sem.at[k]) for k, (src, dst) in enumerate(((last_any, big), (first_any, own_s)))
     ]
     for copy in loads:
         copy.start()
@@ -810,12 +830,15 @@
     small[one.shape[0] :] = two[...]
     for copy in loads:
         copy.wait()
+    share, size = first_out.shape[0] // len(first_orders), own_s.shape[0] // len(first_orders)
     chains = []
     for i, (first, rows, order) in enumerate(parts):
         here = pl.ds(first, rows)
-        chains.append(
-            chain(big.at[here], land.at[here], out.at[here], send_sem.at[i], recv_sem.at[i], own_sem.at[i], order)
-        )
+        chains.append(chain(big.at[here], land.at[i], out.at[here], send_sem.at[i], recv_sem.at[i], own_sem.at[i], order))
+    for c, order in enumerate(first_orders):
+        i, mine = len(parts) + c, own_s.at[pl.ds(c * size, size)]
+        there = first_out.at[pl.ds(c * share, share)]
+        chains.append(chain(None, None, there, send_sem.at[i], recv_sem.at[i], own_sem.at[i], order, own=mine))
 
     def extra(s):
         return send(small, small_land.at[s], ssend_sem.at[s], srecv_sem.at[s], links[s])
@@ -831,36 +854,30 @@
             extra(k).start()
 
 
-def all_reduce(whole, one, two, sizes):
-    dp, tensor = bits("dp", sizes["dp"]), bits("tensor", sizes["tensor"])
-    links = tensor + dp
+def all_reduce(first, last, one, two, links, first_orders):
     small = sds((one.shape[0] + two.shape[0], LANES), F32)
-    pieces, at = [], 0
-    for a in whole:
-        pieces.append((at, a.shape[0]))
-        at += a.shape[0]
-    core, rest = tensor[:1], tensor[1:]
+    core, rest, dp = links[:1], links[1:2], links[2:]
     one_way, other_way = core + rest + dp, core + dp[:1] + rest + dp[1:]
     far_ways = [core + dp[1:2] + rest + dp[:1] + dp[2:], core + dp[1:2] + dp[:1] + rest + dp[2:]]
     ways = [one_way, other_way, far_ways[0], one_way, other_way, far_ways[1]]
-    count = next(n for n in (12, 6, 3) if len(links) <= halvings(at // n) + 1)
-    orders = (ways + ways)[:count]
-    share = at // len(orders)
-    parts = [(k * share, share, order) for k, order in enumerate(orders)]
-    assert at % len(orders) == 0 and all(len(order) <= halvings(rows) + 1 for _, rows, order in parts)
+    at = last.shape[0]
+    count = 6 if len(links) <= halvings(at // 6) else 3
+    share = at // count
+    parts = [(k * share, share, order) for k, order in enumerate(ways[:count])]
+    total_chains, stages = count + len(first_orders), 2 * len(links)
     dma = pltpu.SemaphoreType.DMA
-    stages = 2 * len(links)
     return pl.pallas_call(
-        functools.partial(reduce_kernel, parts, pieces, links),
-        in_specs=[pl.BlockSpec(memory_space=pl.ANY)] * len(pieces) + [pl.BlockSpec(memory_space=pltpu.VMEM)] * 2,
-        out_specs=[pl.BlockSpec(memory_space=pltpu.VMEM)] * 2,
-        out_shape=[sds((at, LANES), BF16), small],
+        functools.partial(reduce_kernel, parts, first_orders, links),
+        in_specs=[pl.BlockSpec(memory_space=pl.ANY)] * 2 + [pl.BlockSpec(memory_space=pltpu.VMEM)] * 2,
+        out_specs=[pl.BlockSpec(memory_space=pltpu.VMEM)] * 3,
+        out_shape=[sds((at, LANES), BF16), sds((at, LANES), BF16), small],
         scratch_shapes=[
             pltpu.VMEM((at, LANES), BF16),
-            pltpu.VMEM((at, LANES), BF16),
+            pltpu.VMEM((count, landing(share, len(links)), LANES), BF16),
+            pltpu.VMEM(first.shape, BF16),
             pltpu.VMEM((len(links), *small.shape), F32),
-            dma((len(pieces),)),
-            dma((len(parts), stages)), dma((len(parts), stages)), dma((len(parts),)),
+            dma((2,)),
+            dma((total_chains, stages)), dma((total_chains, stages)), dma((total_chains,)),
             dma((len(links),)), dma((len(links),)),
         ],
         compiler_params=pltpu.CompilerParams(
@@ -868,14 +885,22 @@
         ),
         name="sum_all",
         cost_estimate=pl.CostEstimate(flops=10_000_000, bytes_accessed=20_000_000, transcendentals=0),
-    )(*whole, one, two)
-
-
-def unpack_kernel(big_ref, up_ref, down_ref, small_ref, *outs):
+    )(first, last, one, two)
+
+
+def unpack_kernel(first_ref, last_ref, up_ref, down_ref, small_ref, *outs):
     squares, vectors, gb_ref, gpw_ref, gain_ref, bias_ref, rel_ref = outs[:4], outs[4:11], *outs[11:]
-    for out, ref, first, n in zip(squares, (big_ref, big_ref, up_ref, down_ref), (0, 18, 0, 0), (18, 6, 6, 6)):
-        for j in range(n):
-            out[:, j * LANES : (j + 1) * LANES] = ref[first + j].astype(F32)
+    i = pl.program_id(0)
+    for g, ref in enumerate((first_ref, last_ref)):
+        for j in range(9):
+            to = (j // 3) * D + g * WIDE + j % 3 * LANES
+            squares[0][:, to : to + LANES] = ref[j].astype(F32)
+        for m in range(3):
+            rows = pl.ds(pl.multiple_of(g * WIDE + i % 3 * LANES, LANES), LANES)
+            squares[1][rows, tile_at(2 * m + i // 3)] = ref[9 + m].astype(F32)
+    for out, ref in ((squares[2], up_ref), (squares[3], down_ref)):
+        for j in range(6):
+            out[:, j * LANES : (j + 1) * LANES] = ref[j].astype(F32)
 
     @pl.when(pl.program_id(0) == 0)
     def _():
@@ -894,7 +919,7 @@
         rel_ref[...] = small_ref[104 : 104 + REL_ROWS, :HEAD_DIM]
 
 
-def unpack(big, up, down, small):
+def unpack(first, last, up, down, small):
     def whole(*shape):
         return pl.BlockSpec(shape, lambda i: (0,) * len(shape))
 
@@ -906,13 +931,32 @@
         unpack_kernel,
         grid=(D // LANES,),
         in_specs=[
-            *[pl.BlockSpec((n, LANES, LANES), lambda i: (0, i, 0)) for n in (24, 6, 6)], whole(*small.shape),
-        ],
-        out_specs=[band(3 * D), band(D), band(D), band(D), *[whole(*shape) for shape in shapes]],
+            *[pl.BlockSpec((n, LANES, LANES), lambda i: (0, i, 0)) for n in (12, 12, 6, 6)], whole(*small.shape),
+        ],
+        out_specs=[band(3 * D), whole(D, D), band(D), band(D), *[whole(*shape) for shape in shapes]],
         out_shape=[sds((D, 3 * D), F32), *[sds((D, D), F32)] * 3, *[sds(shape, F32) for shape in shapes]],
         name="unpack",
         cost_estimate=pl.CostEstimate(flops=0, bytes_accessed=22_000_000, transcendentals=0),
-    )(big, up, down, small)
+    )(first, last, up, down, small)
+
+
+def prepare_kernel(w_ref, gain_ref, bias_ref, rel_ref, pick_ref, bu_ref, bq_in, mem_in, pw_ref, ln_ref, tall_ref, rows_ref, bq_ref, mem_ref, pad_s, rel_s):
+    pad_s[...] = jnp.zeros(pad_s.shape, F32)
+    for p in range(3):
+        pad_s[0:TAPS, 0:HEAD_DIM] = w_ref[p]
+        for j, t in enumerate(to_dense([pad_s[...]] * PER)):
+            pw_ref[p, :, j * LANES : (j + 1) * LANES] = t
+    ln_ref[...] = jnp.zeros(ln_ref.shape, F32)
+    ln_ref[0:3, 0:HEAD_DIM] = gain_ref[...]
+    ln_ref[3:6, 0:HEAD_DIM] = bias_ref[...]
+    rel_s[...] = jnp.zeros(rel_s.shape, F32)
+    rel_s[0:REL_ROWS, 0:HEAD_DIM] = rel_ref[...]
+    tall_ref[...] = tn(pick_ref[...], rel_s[...].astype(BF16)).astype(BF16)
+    rows_ref[...] = jnp.broadcast_to(line(bu_ref).astype(F32), rows_ref.shape).astype(BF16)
+    bq_ref[...] = line(bq_in)
+    for a in range(2):
+        mem = mem_in[a].astype(F32)
+        mem_ref[a] = jnp.concatenate([mem, jnp.zeros((KEYS - LENGTH - MEM, D), F32)]).astype(BF16)
 
 
 def position_tables():
@@ -961,14 +1005,17 @@
     split = lax.axis_size("tensor")
     pick, squeeze, select, marks, code = position_tables()
     assert split == 4
-    b_rows = jnp.broadcast_to(b_up, (16, b_up.shape[0]))
-    pw = jnp.pad(jnp.tile(pool_weight, (1, 1, PER)), ((0, 0), (0, 5), (0, 0)))
-    ln = jnp.pad(jnp.concatenate([pool_gain, pool_bias]), ((0, 2), (0, LANES - HEAD_DIM)))
-    tall = jnp.dot(pick, rel_table, precision=lax.Precision.HIGHEST)
-    tall = jnp.pad(tall, ((0, 0), (0, LANES - HEAD_DIM))).astype(BF16)
+    pick_rows = jnp.asarray(np.pad(pick.T, ((0, 11), (0, 0))), BF16)
     cmp = jnp.asarray(squeeze, BF16)
-    mem = jnp.pad(memory, ((0, 0), (0, KEYS - LENGTH - MEM), (0, 0)))
-    bq = b_qkv.reshape(1, -1)
+    pw, ln, tall, b_rows, bq, mem = pl.pallas_call(
+        prepare_kernel,
+        out_shape=[
+            sds((3, 32, WIDE), F32), sds((8, LANES), F32), sds((PAIRS, LANES), BF16), sds((16, b_up.shape[0]), BF16),
+            sds((1, 3 * D), F32), sds((2, KEYS - LENGTH, D), BF16),
+        ],
+        scratch_shapes=[pltpu.VMEM((32, LANES), F32), pltpu.VMEM((64, LANES), F32)],
+        name="prepare",
+    )(pool_weight, pool_gain, pool_bias, rel_table, pick_rows, b_up, b_qkv, memory)
 
     dma = pltpu.SemaphoreType.DMA
     anywhere = pl.BlockSpec(memory_space=pl.ANY)
@@ -1023,14 +1070,12 @@
         tall, cmp, jnp.asarray(select), jnp.asarray(marks), jnp.asarray(code), mem, w_proj, w_up, b_rows, w_down,
     )
 
-    hidden = w_up.shape[1]
-    piece = 384
-    parts = hidden // piece
-    tiles = hidden // LANES
-    chunks, cut = split * parts, D // LANES * D
+    assert w_up.shape[1] == D
+    tiles = D // LANES
+    cut = tiles * D
     out, gm, gml, small, gup, gdown, gfar = pl.pallas_call(
-        functools.partial(mlp_kernel, parts),
-        grid=(chunks,),
+        mlp_kernel,
+        grid=(split,),
         in_specs=[scalar, const((LENGTH, D)), const((LENGTH, D)), row, row, row, *[anywhere] * 6],
         out_specs=[
             const((LENGTH, D)), const((LENGTH, D)), const((LENGTH, D)), const((24 + split * tiles, LANES)),
@@ -1046,13 +1091,13 @@
             pltpu.VMEM((LENGTH, D), BF16),
             *[pltpu.VMEM((LENGTH, D), F32)] * 3,
             pltpu.VMEM((D // LANES, LENGTH, LANES), F32),
-            pltpu.VMEM((chunks, D, piece), BF16),
-            pltpu.VMEM((chunks, 16, piece), BF16),
-            pltpu.VMEM((chunks, piece, D), BF16),
+            pltpu.VMEM((2, D, D), BF16),
+            pltpu.VMEM((2, 16, D), BF16),
+            pltpu.VMEM((2, D, D), BF16),
             pltpu.VMEM((split, 2 * cut, LANES), BF16),
             pltpu.VMEM((2, 2 * cut, LANES), BF16),
             pltpu.VMEM((cut + cut // 2, LANES), BF16),
-            dma((3, chunks)), dma((4,)), dma((4,)),
+            dma((3, split)), dma((4,)), dma((4,)),
         ],
         compiler_params=pltpu.CompilerParams(vmem_limit_bytes=VMEM_LIMIT, collective_id=2, has_side_effects=True),
         name="mlp",
@@ -1060,8 +1105,12 @@
     )(res_ids, mid, cotangent, gain_two, bias_two, b_down, up_all, bu_all, down_all, w_up, b_rows, w_down)
 
     links = bits("dp", lax.axis_size("dp"))
-    gx, small_one, gwq, gwk, gwv, gwp, gup, gdown = pl.pallas_call(
-        functools.partial(bwd_kernel, links),
+    pieces, every = 12 * D, bits("tensor", split) + links
+    first_orders = [every, [every[0], links[0], every[1], *links[1:]]]
+    share = pieces // len(first_orders)
+    kept = len(first_orders) * (share >> min(len(every), halvings(share)))
+    gx, small_one, first, last, gup, gdown = pl.pallas_call(
+        functools.partial(bwd_kernel, links, first_orders),
         grid=(GROUPS, PER),
         in_specs=[
             scalar, const((LENGTH, D)), row, row, anywhere, const((LENGTH, D)), *w_spec,
@@ -1074,11 +1123,10 @@
         ],
         out_specs=[
             const((LENGTH, D)), const((208, LANES)),
-            *[blocked((3, D, LANES), lambda g, h: (g, 0, 0)) for _ in range(3)],
-            blocked((6, WIDE, LANES), lambda g, h: (0, g, 0)), anywhere, anywhere,
+            const((kept, LANES)), const((pieces, LANES)), anywhere, anywhere,
         ],
         out_shape=[
-            sds((LENGTH, D), F32), sds((208, LANES), F32), *[sds((6, D, LANES), BF16)] * 4,
+            sds((LENGTH, D), F32), sds((208, LANES), F32), sds((kept, LANES), BF16), sds((pieces, LANES), BF16),
             sds((cut, LANES), BF16), sds((cut, LANES), BF16),
         ],
         scratch_shapes=[
@@ -1093,20 +1141,19 @@
             pltpu.VMEM((LENGTH, 3 * WIDE), F32),
             pltpu.VMEM((cut, LANES), BF16), pltpu.VMEM((cut, LANES), BF16), pltpu.VMEM((cut // 2, LANES), BF16),
             pltpu.VMEM((cut, LANES), BF16), pltpu.VMEM((cut, LANES), BF16), pltpu.VMEM((cut // 2, LANES), BF16),
-            dma((4,)), dma((2,)), dma((2, 2 * len(links) + 1)), dma((2, 2 * len(links) + 1)),
+            pltpu.VMEM((pieces, LANES), BF16), pltpu.VMEM((len(first_orders), landing(share, len(every)), LANES), BF16),
+            dma((4,)), dma((2,)), dma((4, 2 * len(every))), dma((4, 2 * len(every))),
         ],
         compiler_params=pltpu.CompilerParams(vmem_limit_bytes=VMEM_LIMIT, collective_id=3, has_side_effects=True),
         name="attend_back",
         cost_estimate=pl.CostEstimate(flops=2 * 7_000_000_000, bytes_accessed=60_000_000, transcendentals=0),
     )(
-        res_ids, xs, gain_one, bias_one, gm, gml, w_qkv, w_qkv, w_qkv, pw, ln, tall, cmp, jnp.asarray(select), jnp.asarray(np.pad(pick.T, ((0, 11), (0, 0))), BF16), w_proj,
+        res_ids, xs, gain_one, bias_one, gm, gml, w_qkv, w_qkv, w_qkv, pw, ln, tall, cmp, jnp.asarray(select), pick_rows, w_proj,
         field, xh, qx, kx, vx, probs, outs, att, gup, gdown, gfar,
     )
 
-    flat = [a.reshape(-1, LANES) for a in (gwq, gwk, gwv, gwp)]
-    sizes = {axis: lax.axis_size(axis) for axis in ("dp", "tensor")}
-    big, small = all_reduce(flat, small_one, small, sizes)
-    outs = unpack(*[a.reshape(-1, D, LANES) for a in (big, gup, gdown)], small)
+    first, last, small = all_reduce(first, last, small_one, small, every, first_orders)
+    outs = unpack(*[a.reshape(-1, D, LANES) for a in (first, last, gup, gdown)], small)
     squares, (gain1, bias1, bp, gain2, bias2, bd, bu), (gb, gpw, pg, pb, rel) = outs[:4], outs[4:11], outs[11:]
 
     return (

time: 323 us -> 307 us (0.950)
  Pallas kernels: 309 us -> 302 us
  local copies, waits for them, and re-layouts: 9.5 us -> 3.56 us
    pallas_call x3 -> x4, Pallas kernels: 232 us -> 224 us  [the longest x1 116 us: per_device(): pl.pallas_call(functools.partial(bwd_kernel, links, first_orders), grid=(...]
where the time goes in v5:
time: 307 us; the launch traced here: 306 us
  Pallas kernels  302 us (98%)
  local copies, waits for them, and re-layouts  3.56 us (1%)
    pallas_call x1, Pallas kernels, per_device(): pl.pallas_call(functools.partial(bwd_kernel, links, first_orders), grid=(...  116 us
    pallas_call x1, Pallas kernels, per_device(): pl.pallas_call(fwd_kernel, grid=(GROUPS, PER), in_specs=[scalar, const((L...  68.6 us
    pallas_call x1, Pallas kernels, all_reduce(): pl.pallas_call(functools.partial(reduce_kernel, parts, first_orders, link...  53.4 us
    pallas_call x1, Pallas kernels, per_device(): pl.pallas_call(mlp_kernel, grid=(split,), in_specs=[scalar, const((LENGTH...  51.9 us
    pallas_call x1, Pallas kernels, unpack(): pl.pallas_call(unpack_kernel, grid=(D // LANES,), in_specs=[*[pl.BlockSpe...  9.34 us

profile of v5, /device:TPU:0, one launch (start us, length us, event | category | flops | bytes accessed | tf_op | source)
XLA Modules:
  0.0 306.5 jit_solution(5450819389542393585)
XLA Ops:
  1.3 2.3 prepare.1
  3.6 68.6 %attend.1 = (f32[800,768]{1,0:T(8,128)}, bf16[800,768]{1,0:T(8,128)(2,1)}, f32[100,8,2304]{2,1,0:T(8,128)}, f32[8,3,800,128]{3,2,1,0:T(8,128)}, bf16[8,800,128]{...) custom-call(s32[1]{0:T(128)S(6)} %copy.45.res_ref, ...), custom_call_target="tpu_custom_call" | custom-call | flops 7000000000 | bytes 60000000 | tf_op jit(solution)/shard_map/attend/pallas_call | solution.py:1036
  72.2 51.9 %mlp.1 = (bf16[800,768]{1,0:T(8,128)(2,1)}, f32[800,768]{1,0:T(8,128)}, bf16[800,768]{1,0:T(8,128)(2,1)}, f32[48,128]{1,0:T(8,128)}, bf16[4608,128]{1,0:T(8,128)...) custom-call(s32[1]{0:T(128)S(6)} %copy.45.res_ref, f32[800,768]{1,0:T(8,128)} %get-tuple-element.75.mid_ref, ...), custom_call_target="tpu_custom_call" | custom-call | flops 22599999488 | bytes 40000000 | tf_op jit(solution)/shard_map/mlp/pallas_call | solution.py:1076
  124.1 116.1 %attend_back.1 = (f32[800,768]{1,0:T(8,128)}, f32[208,128]{1,0:T(8,128)}, bf16[288,128]{1,0:T(8,128)(2,1)}, bf16[9216,128]{1,0:T(8,128)(2,1)}, bf16[4608,128]{1,0:T(8,128)(2,1)}, /*index=5*/bf16[4608,128]{1,0:T(8,128)(2,1)}) custom-call(s32[1]{0:T(128)S(6)} %copy.45.res_ref, bf16[800,768]{1,0:T(8,128)(2,1)} %get-tuple-element.80.x_ref, f32[768]{0:T(1024)} %gain_ref.7, ...), custom_call_target="tpu_custom_call" | custom-call | flops 14000000000 | bytes 60000000 | tf_op jit(solution)/shard_map/attend_back/pallas_call | solution.py:1112
  240.2 53.4 %sum_all.1 = (bf16[9216,128]{1,0:T(8,128)(2,1)}, bf16[9216,128]{1,0:T(8,128)(2,1)}, f32[256,128]{1,0:T(8,128)}) custom-call(bf16[288,128]{1,0:T(8,128)(2,1)} %get-tuple-element.95.first_any, bf16[9216,128]{1,0:T(8,128)(2,1)} %get-tuple-element.96.last_any, f32[208,128]{1,0:T(8,128)} %get-tuple-element.97.one, f32[48,128]{1,0:T(8,128)} %get-tuple-element.98.two), custom_call_target="tpu_custom_call" | custom-call | flops 10000000 | bytes 20000000 | tf_op jit(solution)/shard_map/sum_all/pallas_call | solution.py:869
  293.6 0.0 copy-start.1
  293.6 9.3 %unpack.1 = (f32[768,2304]{1,0:T(8,128)}, f32[768,768]{1,0:T(8,128)}, f32[768,768]{1,0:T(8,128)}, f32[768,768]{1,0:T(8,128)}, f32[768]{0:T(1024)}, /*index=5*/f3...) custom-call(bf16[12,768,128]{2,1,0:T(8,128)(2,1)} %bitcast.4, ...), custom_call_target="tpu_custom_call" | custom-call | bytes 22000000 | tf_op jit(solution)/shard_map/unpack/pallas_call | solution.py:930
  302.9 0.0 copy-start
  302.9 0.0 copy-done.1
  302.9 1.0 copy.46
  304.0 1.1 copy-done
  305.1 1.4 copy.47
Async XLA Ops:
  293.6 9.4 %copy-start.1 = (bf16[800,768]{1,0:T(8,128)(2,1)S(1)}, bf16[800,768]{1,0:T(8,128)(2,1)}, u32[]{:S(2)}) copy-start(bf16[800,768]{1,0:T(8,128)(2,1)} %get-tuple-element.138) | copy-start | bytes 3686404
  302.9 2.1 copy-start

commit v6 on v5

--- a/solution.py
+++ b/solution.py
@@ -35,7 +35,7 @@
 NEG = -1e30
 UP_TICKS = (0, 3, 4, 5, 6, 8, 11)
 DOWN_TICKS = (3, 5, 7, 9, 10, 11, 12, 14)
-FIRST_TICKS = (7, 8, 10, 11, 12, 14)
+FIRST_TICKS = (7, 9, 11, 12, 13, 14)
 VMEM_LIMIT = 60 * 1024 * 1024
 
 
@@ -184,11 +184,19 @@
     )
 
 
-def greet(links):
+def hail(links):
     barrier = pltpu.get_barrier_semaphore()
     for link in links:
         pl.semaphore_signal(barrier, inc=1, device_id=partner_of(*link), device_id_type=pl.DeviceIdType.MESH)
-    pl.semaphore_wait(barrier, len(links))
+
+
+def meet(links):
+    pl.semaphore_wait(pltpu.get_barrier_semaphore(), len(links))
+
+
+def greet(links):
+    hail(links)
+    meet(links)
 
 
 def some(start, rows):
@@ -204,6 +212,17 @@
         return 0
 
     lax.fori_loop(0, rows // block, add, 0)
+
+
+def add_up(dst, *sources):
+    block = 256
+
+    def add(k, _):
+        parts = [ref[some(at + k * block, block), :].astype(F32) for ref, at in sources]
+        dst[some(k * block, block), :] = sum(parts[1:], parts[0]).astype(BF16)
+        return 0
+
+    lax.fori_loop(0, dst.shape[0] // block, add, 0)
 
 
 def span(rows, order, s):
@@ -490,7 +509,15 @@
     def _():
         for copy in loads(0):
             copy.start()
-        greet((core, other, near))
+        hail((core, other, near))
+
+    for k in range(2):
+
+        @pl.when(step == 2 * k + 1)
+        def _():
+            if k == 0:
+                meet((core, other, near))
+            to_core(k).start()
 
     @pl.when(step == 2)
     def _():
@@ -498,12 +525,6 @@
         add_rows(grad_s.at[1], 0, land_s.at[0], 0, 2 * cut)
         to_side().start()
         to_near().start()
-
-    for k in range(2):
-
-        @pl.when(step == 2 * k + 1)
-        def _():
-            to_core(k).start()
 
     @pl.when(step == 0)
     def _():
@@ -584,15 +605,13 @@
         for at, v in zip((0, 6, 18), sums):
             put_rows(small_ref, at, total(v))
         to_core(1).wait()
-        add_rows(grad_s.at[3], 0, land_s.at[1], 0, 2 * cut)
         to_side().wait()
-        add_rows(grad_s.at[3], 0, side_s, 0, cut)
         to_near().wait()
         keep = cut + bit_of(*near) * half
-        add_rows(grad_s.at[1], keep, side_s, cut, half)
-        gup_ref[...] = grad_s[3, 0:cut, :]
-        gdown_ref[...] = grad_s[3, cut : 2 * cut, :]
-        gfar_ref[...] = grad_s[1, some(keep, half), :]
+        far, own = grad_s.at[1], grad_s.at[3]
+        add_up(gup_ref, (own, 0), (land_s.at[1], 0), (side_s, 0))
+        add_up(gdown_ref, (own, cut), (land_s.at[1], cut))
+        add_up(gfar_ref, (far, keep), (side_s, cut))
 
 
 def bwd_kernel(
@@ -631,19 +650,17 @@
         at_ticks(tick, UP_TICKS, up_steps)
         at_ticks(tick, DOWN_TICKS, down_steps)
 
+    loads = [
+        pltpu.make_async_copy(src, dst, load_sem.at[k])
+        for k, (src, dst) in enumerate(((gup_any, up_s), (gdown_any, down_s), (gfar_any, far_s)))
+    ]
+
     @pl.when((g == 0) & (h == 0))
     def _():
-        loads = [
-            pltpu.make_async_copy(src, dst, load_sem.at[k])
-            for k, (src, dst) in enumerate(((gup_any, up_s), (gdown_any, down_s), (gfar_any, far_s)))
-        ]
         for copy in loads:
             copy.start()
-        greet((("tensor", 1), ("tensor", 2), *order))
-        for copy in loads:
-            copy.wait()
-
-    travel((PER + 3) * g + h)
+        hail((("tensor", 1), ("tensor", 2), *order))
+
 
     @pl.when((g == 0) & (h == 0))
     def _():
@@ -660,6 +677,14 @@
         gtall_s[...] = jnp.zeros(gtall_s.shape, F32)
         small_ref[...] = jnp.zeros(small_ref.shape, F32)
         gpw_s[...] = jnp.zeros(gpw_s.shape, F32)
+
+    @pl.when((g == 0) & (h == 0))
+    def _():
+        meet((("tensor", 1), ("tensor", 2), *order))
+        for copy in loads:
+            copy.wait()
+
+    travel((PER + 3) * g + h)
 
     @pl.when(h == 0)
     def _():

time: 307 us -> 302 us (0.984)
  Pallas kernels: 302 us -> 296 us
    pallas_call x1, Pallas kernels: 116 us -> 111 us  [per_device(): pl.pallas_call(functools.partial(bwd_kernel, links, first_orders), grid=(...]
where the time goes in v6:
time: 302 us; the launch traced here: 301 us
  Pallas kernels  296 us (98%)
  local copies, waits for them, and re-layouts  3.56 us (1%)
    pallas_call x1, Pallas kernels, per_device(): pl.pallas_call(functools.partial(bwd_kernel, links, first_orders), grid=(...  111 us
    pallas_call x1, Pallas kernels, per_device(): pl.pallas_call(fwd_kernel, grid=(GROUPS, PER), in_specs=[scalar, const((L...  68.6 us
    pallas_call x1, Pallas kernels, all_reduce(): pl.pallas_call(functools.partial(reduce_kernel, parts, first_orders, link...  54.2 us
    pallas_call x1, Pallas kernels, per_device(): pl.pallas_call(mlp_kernel, grid=(split,), in_specs=[scalar, const((LENGTH...  51.1 us
    pallas_call x1, Pallas kernels, unpack(): pl.pallas_call(unpack_kernel, grid=(D // LANES,), in_specs=[*[pl.BlockSpe...  9.34 us

profile of v6, /device:TPU:0, one launch (start us, length us, event | category | flops | bytes accessed | tf_op | source)
XLA Modules:
  0.0 301.2 jit_solution(14975874524538670743)
XLA Ops:
  1.3 2.3 prepare.1
  3.6 68.6 %attend.1 = (f32[800,768]{1,0:T(8,128)}, bf16[800,768]{1,0:T(8,128)(2,1)}, f32[100,8,2304]{2,1,0:T(8,128)}, f32[8,3,800,128]{3,2,1,0:T(8,128)}, bf16[8,800,128]{...) custom-call(s32[1]{0:T(128)S(6)} %copy.45.res_ref, ...), custom_call_target="tpu_custom_call" | custom-call | flops 7000000000 | bytes 60000000 | tf_op jit(solution)/shard_map/attend/pallas_call | solution.py:1061
  72.2 51.1 %mlp.1 = (bf16[800,768]{1,0:T(8,128)(2,1)}, f32[800,768]{1,0:T(8,128)}, bf16[800,768]{1,0:T(8,128)(2,1)}, f32[48,128]{1,0:T(8,128)}, bf16[4608,128]{1,0:T(8,128)...) custom-call(s32[1]{0:T(128)S(6)} %copy.45.res_ref, f32[800,768]{1,0:T(8,128)} %get-tuple-element.75.mid_ref, ...), custom_call_target="tpu_custom_call" | custom-call | flops 22599999488 | bytes 40000000 | tf_op jit(solution)/shard_map/mlp/pallas_call | solution.py:1101
  123.3 110.7 %attend_back.1 = (f32[800,768]{1,0:T(8,128)}, f32[208,128]{1,0:T(8,128)}, bf16[288,128]{1,0:T(8,128)(2,1)}, bf16[9216,128]{1,0:T(8,128)(2,1)}, bf16[4608,128]{1,0:T(8,128)(2,1)}, /*index=5*/bf16[4608,128]{1,0:T(8,128)(2,1)}) custom-call(s32[1]{0:T(128)S(6)} %copy.45.res_ref, bf16[800,768]{1,0:T(8,128)(2,1)} %get-tuple-element.80.x_ref, f32[768]{0:T(1024)} %gain_ref.7, ...), custom_call_target="tpu_custom_call" | custom-call | flops 14000000000 | bytes 60000000 | tf_op jit(solution)/shard_map/attend_back/pallas_call | solution.py:1137
  234.1 54.2 %sum_all.1 = (bf16[9216,128]{1,0:T(8,128)(2,1)}, bf16[9216,128]{1,0:T(8,128)(2,1)}, f32[256,128]{1,0:T(8,128)}) custom-call(bf16[288,128]{1,0:T(8,128)(2,1)} %get-tuple-element.95.first_any, bf16[9216,128]{1,0:T(8,128)(2,1)} %get-tuple-element.96.last_any, f32[208,128]{1,0:T(8,128)} %get-tuple-element.97.one, f32[48,128]{1,0:T(8,128)} %get-tuple-element.98.two), custom_call_target="tpu_custom_call" | custom-call | flops 10000000 | bytes 20000000 | tf_op jit(solution)/shard_map/sum_all/pallas_call | solution.py:894
  288.2 0.0 copy-start.1
  288.2 9.3 %unpack.1 = (f32[768,2304]{1,0:T(8,128)}, f32[768,768]{1,0:T(8,128)}, f32[768,768]{1,0:T(8,128)}, f32[768,768]{1,0:T(8,128)}, f32[768]{0:T(1024)}, /*index=5*/f3...) custom-call(bf16[12,768,128]{2,1,0:T(8,128)(2,1)} %bitcast.4, ...), custom_call_target="tpu_custom_call" | custom-call | bytes 22000000 | tf_op jit(solution)/shard_map/unpack/pallas_call | solution.py:955
  297.6 0.0 copy-start
  297.6 0.0 copy-done.1
  297.6 1.0 copy.46
  298.6 1.1 copy-done
  299.7 1.4 copy.47
Async XLA Ops:
  288.2 9.4 %copy-start.1 = (bf16[800,768]{1,0:T(8,128)(2,1)S(1)}, bf16[800,768]{1,0:T(8,128)(2,1)}, u32[]{:S(2)}) copy-start(bf16[800,768]{1,0:T(8,128)(2,1)} %get-tuple-element.138) | copy-start | bytes 3686404
  297.6 2.1 copy-start
